TPU v7x, 32 devices: a whole 2x2x4 slice. The times are simulated.
32 devices in a mesh: member: 8 (over y, x, core), domain: 4 (over z).
Axes of the slice: x: 2, y: 2, z: 4, core: 2. Of those that a mesh axis runs over, the one named last changes fastest.
Arguments:
- state: float32 [8, 4, 128, 512], P('member', None, 'domain'), may hold values from -5 to 5
- perturbation: float32 [8, 4, 128, 512], P('member', None, 'domain'), may hold values from -3 to 3
- parents: int32 [8], replicated, may hold values from 0 to 7
Outputs:
- final_state: float32 [8, 4, 128, 512], P('member', None, 'domain')
- score: float32 [8], P('member')
Inputs may be any that keep to these rules, and one draw needn't show every extreme that they name: `parents`: A member may be the parent of several slots or of none.
All inputs are finite; a program needn't handle non-finite values.
Results may differ from a plain program's by a relative error of at most 0.00002.
Values sent between devices are 32-bit elements; how exact they have to be, the bound alone decides.
No kernel may reach another device: no remote copies, remote signals or barrier semaphores. Data moves between devices by JAX's collectives and lax.ppermute only.
A program may use at most 64 MiB of HBM per device.

v0:
```python
import jax
import jax.numpy as jnp
from jax import lax
from jax.sharding import PartitionSpec as P

STEPS = 3


time_step = 0.1
viscous = 0.05
coriolis = 1.0


def with_halo(cells, sides, width):
    for axis, dim in sides:
        count = lax.axis_size(axis)
        ends = count - 1
        head = lax.slice_in_dim(cells, 0, width, axis=dim)
        tail = lax.slice_in_dim(cells, cells.shape[dim] - width, cells.shape[dim], axis=dim)
        cells = jnp.concatenate(
            [
                lax.ppermute(tail, axis, [(i, (i + 1) % count) for i in range(ends)]),
                cells,
                lax.ppermute(head, axis, [((i + 1) % count, i) for i in range(ends)]),
            ],
            axis=dim,
        )
    return cells


def gradients(padded):
    middle = padded[:, 1:-1]
    east = jnp.roll(middle, -1, axis=-1)
    west = jnp.roll(middle, 1, axis=-1)
    return (middle, east, west, padded[:, 2:], padded[:, :-2])


def tendency(padded, start_row, total_rows):
    middle, east, west, north, south = gradients(padded)
    grad_x = (east - west) * 0.5
    grad_y = (north - south) * 0.5
    laplace = east + west + north + south - 4.0 * middle
    depth = 1.0 + padded[0]
    fluxes = jnp.stack([depth * padded[1], depth * padded[2]])
    flux_mid, flux_east, flux_west, flux_north, flux_south = gradients(fluxes)
    count = padded.shape[1] - 2
    global_rows = (start_row + 1 + jnp.arange(count, dtype=jnp.int32)).astype(jnp.float32)
    latitude = coriolis * (2.0 * (global_rows + 0.5) / total_rows - 1.0)
    latitude = latitude[:, None]
    height, speed_u, speed_v, tracer = (middle[0], middle[1], middle[2], middle[3])
    advect = speed_u * grad_x + speed_v * grad_y
    d_eta = (
        -((flux_east[0] - flux_west[0]) * 0.5 + (flux_north[1] - flux_south[1]) * 0.5)
        + viscous * laplace[0]
    )
    d_u = -advect[1] + latitude * speed_v - grad_x[0] + viscous * laplace[1]
    d_v = -advect[2] - latitude * speed_u - grad_y[0] + viscous * laplace[2]
    d_q = -advect[3] + viscous * laplace[3]
    return jnp.stack([d_eta, d_u, d_v, d_q])


def inside_rows(field, start_row, total_rows):
    global_rows = start_row + jnp.arange(field.shape[1], dtype=jnp.int32)
    valid = (global_rows >= 0) & (global_rows < total_rows)
    return jnp.where(valid[None, :, None], field, 0.0)


def step_deep(field, first_row, total_rows):
    padded = with_halo(field, (("domain", 1),), 3)
    first = padded[:, 1:-1] + time_step * tendency(padded, first_row - 3, total_rows)
    first = inside_rows(first, first_row - 2, total_rows)
    second = 0.75 * padded[:, 2:-2] + 0.25 * (
        first[:, 1:-1] + time_step * tendency(first, first_row - 2, total_rows)
    )
    second = inside_rows(second, first_row - 1, total_rows)
    return 1.0 / 3.0 * padded[:, 3:-3] + 2.0 / 3.0 * (
        second[:, 1:-1] + time_step * tendency(second, first_row - 1, total_rows)
    )


def run_steps(field, first_row, total_rows):
    for count in range(STEPS):
        field = step_deep(field, first_row, total_rows)
    return field


def on_device(state, perturbation, parents):
    rows = state.shape[2]
    width = state.shape[3]
    total_rows = rows * lax.axis_size("domain")
    first_row = lax.axis_index("domain") * rows
    before = run_steps(state[0], first_row, total_rows)
    global_rows = (first_row + jnp.arange(rows, dtype=jnp.int32)).astype(jnp.float32)
    weight = 1.0 + 2.0 * global_rows / (total_rows - 1)
    local_score = jnp.sum(weight[:, None] * before[3] * before[3])
    score = lax.psum(local_score, "domain") / (total_rows * width)
    parent = lax.dynamic_index_in_dim(parents, lax.axis_index("member"), 0, keepdims=False)
    piece = lax.all_gather(before[None], "member", axis=0, tiled=True)
    count = piece.shape[0]
    inside = (parent >= 0) & (parent < count)
    chosen = lax.dynamic_index_in_dim(piece, jnp.clip(parent, 0, count - 1), 0, keepdims=False)
    cloned = jnp.where(inside, chosen, jnp.zeros_like(before))
    after = run_steps(cloned + perturbation[0], first_row, total_rows)
    return (after[None], jnp.reshape(score, (1,)))


def solution(mesh):
    placed = (P("member", None, "domain", None), P("member", None, "domain", None), P())
    return jax.shard_map(
        on_device,
        mesh=mesh,
        in_specs=placed,
        out_specs=(P("member", None, "domain", None), P("member")),
        check_vma=False,
    )
```

profile of v0, /device:TPU:0, one launch (start us, length us, event | category | flops | bytes accessed | tf_op | source)
XLA Modules:
  0.0 129.2 jit_solution(8384120893960685727)
XLA Ops:
  7.2 0.9 fusion.403
  8.1 1.3 %collective-permute-start.1 = (f32[4,3,512]{2,1,0:T(4,128)S(1)}, f32[4,3,512]{2,1,0:T(4,128)S(1)}, u32[]{:S(2)}, u32[]{:S(2)}) collective-permute-start(f32[4,3,512]{2,1,0:T(4,128)S(1)} %get-tuple-element.301), channel_id=1, source_target_pairs={{1,0},{2,1},{3,2},{5,4},{6,5},{7,6},{9,8},{10,9},{11,10},{13,12},{... | collective-permute-start | bytes 73736 | tf_op jit(solution)/shard_map/ppermute | solution.py:24
  9.4 5.6 %collective-permute-start = (f32[4,3,512]{2,1,0:T(4,128)S(1)}, f32[4,3,512]{2,1,0:T(4,128)S(1)}, u32[]{:S(2)}, u32[]{:S(2)}) collective-permute-start(f32[4,3,512]{2,1,0:T(4,128)S(1)} %get-tuple-element.300), channel_id=1, source_target_pairs={{0,1},{1,2},{2,3},{4,5},{5,6},{6,7},{8,9},{9,10},{10,11},{12,13},{... | collective-permute-start | bytes 73736 | tf_op jit(solution)/shard_map/ppermute | solution.py:22
  15.1 1.5 %collective-permute-done = f32[4,3,512]{2,1,0:T(4,128)S(1)} collective-permute-done((f32[4,3,512]{2,1,0:T(4,128)S(1)}, f32[4,3,512]{2,1,0:T(4,128)S(1)}, u32[]{:S(2)}, u32[]{:S(2)}) %collective-permute-start) | collective-permute-done | bytes 24608 | tf_op jit(solution)/shard_map/ppermute | solution.py:22
  16.5 1.0 pad_maximum_fusion
  17.6 0.2 fusion.396
  18.1 0.3 multiply_add_fusion.11
  18.4 0.1 fusion.227
  18.6 0.2 fusion.394
  19.1 0.3 multiply_add_fusion.10
  19.4 0.1 fusion.215
  20.2 0.2 multiply_add_fusion.17
  20.6 0.6 copy-done
  21.3 1.3 %collective-permute-start.3 = (f32[4,3,512]{2,1,0:T(4,128)S(1)}, f32[4,3,512]{2,1,0:T(4,128)S(1)}, u32[]{:S(2)}, u32[]{:S(2)}) collective-permute-start(f32[4,3,512]{2,1,0:T(4,128)S(1)} %get-tuple-element.298), channel_id=1, source_target_pairs={{1,0},{2,1},{3,2},{5,4},{6,5},{7,6},{9,8},{10,9},{11,10},{13,12},{... | collective-permute-start | bytes 73736 | tf_op jit(solution)/shard_map/ppermute | solution.py:24
  22.6 4.9 %collective-permute-start.2 = (f32[4,3,512]{2,1,0:T(4,128)S(1)}, f32[4,3,512]{2,1,0:T(4,128)S(1)}, u32[]{:S(2)}, u32[]{:S(2)}) collective-permute-start(f32[4,3,512]{2,1,0:T(4,128)S(1)} %get-tuple-element.297), channel_id=1, source_target_pairs={{0,1},{1,2},{2,3},{4,5},{5,6},{6,7},{8,9},{9,10},{10,11},{12,13},{... | collective-permute-start | bytes 73736 | tf_op jit(solution)/shard_map/ppermute | solution.py:22
  27.4 1.6 %collective-permute-done.2 = f32[4,3,512]{2,1,0:T(4,128)S(1)} collective-permute-done((f32[4,3,512]{2,1,0:T(4,128)S(1)}, f32[4,3,512]{2,1,0:T(4,128)S(1)}, u32[]{:S(2)}, u32[]{:S(2)}) %collective-permute-start.2) | collective-permute-done | bytes 24608 | tf_op jit(solution)/shard_map/ppermute | solution.py:22
  29.1 0.2 fusion.390
  29.6 0.3 multiply_add_fusion.9
  29.9 0.1 fusion.203
  30.1 0.2 fusion.388
  30.6 0.3 multiply_add_fusion.8
  30.9 0.1 fusion.191
  31.7 0.2 multiply_add_fusion.16
  32.2 1.3 %collective-permute-start.5 = (f32[4,3,512]{2,1,0:T(4,128)S(1)}, f32[4,3,512]{2,1,0:T(4,128)S(1)}, u32[]{:S(2)}, u32[]{:S(2)}) collective-permute-start(f32[4,3,512]{2,1,0:T(4,128)S(1)} %get-tuple-element.295), channel_id=1, source_target_pairs={{1,0},{2,1},{3,2},{5,4},{6,5},{7,6},{9,8},{10,9},{11,10},{13,12},{... | collective-permute-start | bytes 73736 | tf_op jit(solution)/shard_map/ppermute | solution.py:24
  33.5 4.9 %collective-permute-start.4 = (f32[4,3,512]{2,1,0:T(4,128)S(1)}, f32[4,3,512]{2,1,0:T(4,128)S(1)}, u32[]{:S(2)}, u32[]{:S(2)}) collective-permute-start(f32[4,3,512]{2,1,0:T(4,128)S(1)} %get-tuple-element.294), channel_id=1, source_target_pairs={{0,1},{1,2},{2,3},{4,5},{5,6},{6,7},{8,9},{9,10},{10,11},{12,13},{... | collective-permute-start | bytes 73736 | tf_op jit(solution)/shard_map/ppermute | solution.py:22
  38.4 1.6 %collective-permute-done.4 = f32[4,3,512]{2,1,0:T(4,128)S(1)} collective-permute-done((f32[4,3,512]{2,1,0:T(4,128)S(1)}, f32[4,3,512]{2,1,0:T(4,128)S(1)}, u32[]{:S(2)}, u32[]{:S(2)}) %collective-permute-start.4) | collective-permute-done | bytes 24608 | tf_op jit(solution)/shard_map/ppermute | solution.py:22
  40.0 0.2 fusion.384
  40.5 0.3 multiply_add_fusion.7
  40.8 0.1 fusion.179
  41.1 0.2 fusion.382
  41.6 0.3 multiply_add_fusion.6
  42.6 0.2 multiply_add_fusion.15
  43.0 0.8 fusion.44
  43.8 0.6 dynamic_slice.8
  46.4 28.8 %all-gather.3.cloned.1.call-done = f32[32,32,512]{2,1,0:T(8,128)} async-done(((f32[4,32,512]{2,1,0:T(8,128)}), f32[32,32,512]{2,1,0:T(8,128)}) %all-gather.3.cloned.1.call-update) | async-done | bytes 2097168 | tf_op jit(solution)/shard_map/all_gather | solution.py:98
  75.2 1.0 add_bitcast_fusion
  76.2 1.3 %collective-permute-start.7 = (f32[4,3,512]{2,1,0:T(4,128)S(1)}, f32[4,3,512]{2,1,0:T(4,128)S(1)}, u32[]{:S(2)}, u32[]{:S(2)}) collective-permute-start(f32[4,3,512]{2,1,0:T(4,128)S(1)} %get-tuple-element.292), channel_id=1, source_target_pairs={{1,0},{2,1},{3,2},{5,4},{6,5},{7,6},{9,8},{10,9},{11,10},{13,12},{... | collective-permute-start | bytes 73736 | tf_op jit(solution)/shard_map/ppermute | solution.py:24
  77.5 4.5 %collective-permute-start.6 = (f32[4,3,512]{2,1,0:T(4,128)S(1)}, f32[4,3,512]{2,1,0:T(4,128)S(1)}, u32[]{:S(2)}, u32[]{:S(2)}) collective-permute-start(f32[4,3,512]{2,1,0:T(4,128)S(1)} %get-tuple-element.291), channel_id=1, source_target_pairs={{0,1},{1,2},{2,3},{4,5},{5,6},{6,7},{8,9},{9,10},{10,11},{12,13},{... | collective-permute-start | bytes 73736 | tf_op jit(solution)/shard_map/ppermute | solution.py:22
  82.1 1.6 %collective-permute-done.6 = f32[4,3,512]{2,1,0:T(4,128)S(1)} collective-permute-done((f32[4,3,512]{2,1,0:T(4,128)S(1)}, f32[4,3,512]{2,1,0:T(4,128)S(1)}, u32[]{:S(2)}, u32[]{:S(2)}) %collective-permute-start.6) | collective-permute-done | bytes 24608 | tf_op jit(solution)/shard_map/ppermute | solution.py:22
  83.7 0.2 fusion.378
  84.2 0.3 multiply_add_fusion.5
  84.8 0.2 fusion.376
  85.3 0.3 multiply_add_fusion.4
  86.3 0.2 multiply_add_fusion.14
  86.8 1.3 %collective-permute-start.9 = (f32[4,3,512]{2,1,0:T(4,128)S(1)}, f32[4,3,512]{2,1,0:T(4,128)S(1)}, u32[]{:S(2)}, u32[]{:S(2)}) collective-permute-start(f32[4,3,512]{2,1,0:T(4,128)S(1)} %get-tuple-element.289), channel_id=1, source_target_pairs={{1,0},{2,1},{3,2},{5,4},{6,5},{7,6},{9,8},{10,9},{11,10},{13,12},{... | collective-permute-start | bytes 73736 | tf_op jit(solution)/shard_map/ppermute | solution.py:24
  88.1 5.0 %collective-permute-start.8 = (f32[4,3,512]{2,1,0:T(4,128)S(1)}, f32[4,3,512]{2,1,0:T(4,128)S(1)}, u32[]{:S(2)}, u32[]{:S(2)}) collective-permute-start(f32[4,3,512]{2,1,0:T(4,128)S(1)} %get-tuple-element.288), channel_id=1, source_target_pairs={{0,1},{1,2},{2,3},{4,5},{5,6},{6,7},{8,9},{9,10},{10,11},{12,13},{... | collective-permute-start | bytes 73736 | tf_op jit(solution)/shard_map/ppermute | solution.py:22
  93.2 1.4 %collective-permute-done.8 = f32[4,3,512]{2,1,0:T(4,128)S(1)} collective-permute-done((f32[4,3,512]{2,1,0:T(4,128)S(1)}, f32[4,3,512]{2,1,0:T(4,128)S(1)}, u32[]{:S(2)}, u32[]{:S(2)}) %collective-permute-start.8) | collective-permute-done | bytes 24608 | tf_op jit(solution)/shard_map/ppermute | solution.py:22
  94.6 0.2 fusion.372
  95.1 0.3 multiply_add_fusion.3
  95.7 0.2 fusion.370
  96.2 0.3 multiply_add_fusion.2
  97.3 0.2 multiply_add_fusion.13
  97.7 1.3 %collective-permute-start.11 = (f32[4,3,512]{2,1,0:T(4,128)S(1)}, f32[4,3,512]{2,1,0:T(4,128)S(1)}, u32[]{:S(2)}, u32[]{:S(2)}) collective-permute-start(f32[4,3,512]{2,1,0:T(4,128)S(1)} %get-tuple-element.286), channel_id=1, source_target_pairs={{1,0},{2,1},{3,2},{5,4},{6,5},{7,6},{9,8},{10,9},{11,10},{13,12},{... | collective-permute-start | bytes 73736 | tf_op jit(solution)/shard_map/ppermute | solution.py:24
  99.0 4.9 %collective-permute-start.10 = (f32[4,3,512]{2,1,0:T(4,128)S(1)}, f32[4,3,512]{2,1,0:T(4,128)S(1)}, u32[]{:S(2)}, u32[]{:S(2)}) collective-permute-start(f32[4,3,512]{2,1,0:T(4,128)S(1)} %get-tuple-element.285), channel_id=1, source_target_pairs={{0,1},{1,2},{2,3},{4,5},{5,6},{6,7},{8,9},{9,10},{10,11},{12,13},{... | collective-permute-start | bytes 73736 | tf_op jit(solution)/shard_map/ppermute | solution.py:22
  103.9 1.5 %fusion.235 = f32[]{:T(128)} fusion(f32[4,32,512]{2,1,0:T(8,128)} %fusion.44, f32[32]{0:T(128)S(1)} %multiply_add_fusion.18), kind=kLoop, calls=%fused_computation.699 | loop fusion | flops 49151 | bytes 65668 | tf_op jit(solution)/shard_map/reduce_sum | solution.py:95
  105.4 11.2 %psum.7 = f32[]{:T(128)} all-reduce(f32[]{:T(128)} %fusion.235), channel_id=1, replica_groups=mesh['member'=8,'domain'=4] {'domain'}, use_global_device_ids=true, to_apply=%region_1.2 | all-reduce | flops 1 | bytes 8 | tf_op jit(solution)/shard_map/psum | solution.py:96
  117.4 0.2 fusion.366
  117.9 0.3 multiply_add_fusion.1
  118.2 0.1 fusion.107
  118.5 0.2 fusion.364
  119.0 0.3 multiply_add_fusion
  119.3 0.1 fusion.95
  120.1 0.2 multiply_add_fusion.12
  120.4 0.8 fusion.54
  (153 shorter events, 10.1 us)
Async XLA Ops:
  7.2 68.0 %all-gather.3.cloned.1.call-start = ((), (), s32[]{:S(2)}) async-start(), calls=%async_computation | async-start | bytes 2359296 | tf_op jit(solution)/shard_map/all_gather | solution.py:98
  8.1 6.9 %collective-permute-start.1 = (f32[4,3,512]{2,1,0:T(4,128)S(1)}, f32[4,3,512]{2,1,0:T(4,128)S(1)}, u32[]{:S(2)}, u32[]{:S(2)}) collective-permute-start(f32[4,3,512]{2,1,0:T(4,128)S(1)} %get-tuple-element.301), channel_id=1, source_target_pairs={{1,0},{2,1},{3,2},{5,4},{6,5},{7,6},{9,8},{10,9},{11,10},{13,12},{... | collective-permute-start | bytes 73736 | tf_op jit(solution)/shard_map/ppermute | solution.py:24
  9.4 7.1 %collective-permute-start = (f32[4,3,512]{2,1,0:T(4,128)S(1)}, f32[4,3,512]{2,1,0:T(4,128)S(1)}, u32[]{:S(2)}, u32[]{:S(2)}) collective-permute-start(f32[4,3,512]{2,1,0:T(4,128)S(1)} %get-tuple-element.300), channel_id=1, source_target_pairs={{0,1},{1,2},{2,3},{4,5},{5,6},{6,7},{8,9},{9,10},{10,11},{12,13},{... | collective-permute-start | bytes 73736 | tf_op jit(solution)/shard_map/ppermute | solution.py:22
  20.2 1.0 copy-start
  21.3 6.2 %collective-permute-start.3 = (f32[4,3,512]{2,1,0:T(4,128)S(1)}, f32[4,3,512]{2,1,0:T(4,128)S(1)}, u32[]{:S(2)}, u32[]{:S(2)}) collective-permute-start(f32[4,3,512]{2,1,0:T(4,128)S(1)} %get-tuple-element.298), channel_id=1, source_target_pairs={{1,0},{2,1},{3,2},{5,4},{6,5},{7,6},{9,8},{10,9},{11,10},{13,12},{... | collective-permute-start | bytes 73736 | tf_op jit(solution)/shard_map/ppermute | solution.py:24
  22.6 6.4 %collective-permute-start.2 = (f32[4,3,512]{2,1,0:T(4,128)S(1)}, f32[4,3,512]{2,1,0:T(4,128)S(1)}, u32[]{:S(2)}, u32[]{:S(2)}) collective-permute-start(f32[4,3,512]{2,1,0:T(4,128)S(1)} %get-tuple-element.297), channel_id=1, source_target_pairs={{0,1},{1,2},{2,3},{4,5},{5,6},{6,7},{8,9},{9,10},{10,11},{12,13},{... | collective-permute-start | bytes 73736 | tf_op jit(solution)/shard_map/ppermute | solution.py:22
  32.2 6.2 %collective-permute-start.5 = (f32[4,3,512]{2,1,0:T(4,128)S(1)}, f32[4,3,512]{2,1,0:T(4,128)S(1)}, u32[]{:S(2)}, u32[]{:S(2)}) collective-permute-start(f32[4,3,512]{2,1,0:T(4,128)S(1)} %get-tuple-element.295), channel_id=1, source_target_pairs={{1,0},{2,1},{3,2},{5,4},{6,5},{7,6},{9,8},{10,9},{11,10},{13,12},{... | collective-permute-start | bytes 73736 | tf_op jit(solution)/shard_map/ppermute | solution.py:24
  33.5 6.4 %collective-permute-start.4 = (f32[4,3,512]{2,1,0:T(4,128)S(1)}, f32[4,3,512]{2,1,0:T(4,128)S(1)}, u32[]{:S(2)}, u32[]{:S(2)}) collective-permute-start(f32[4,3,512]{2,1,0:T(4,128)S(1)} %get-tuple-element.294), channel_id=1, source_target_pairs={{0,1},{1,2},{2,3},{4,5},{5,6},{6,7},{8,9},{9,10},{10,11},{12,13},{... | collective-permute-start | bytes 73736 | tf_op jit(solution)/shard_map/ppermute | solution.py:22
  42.6 1.2 copy-start.2
  42.6 32.6 %copy-start.1 = (f32[1,4,32,512]{3,2,1,0:T(8,128)S(1)}, f32[1,4,32,512]{3,2,1,0:T(8,128)}, u32[]{:S(2)}) copy-start(f32[1,4,32,512]{3,2,1,0:T(8,128)} %param.4) | copy-start | bytes 786436
  76.2 5.9 %collective-permute-start.7 = (f32[4,3,512]{2,1,0:T(4,128)S(1)}, f32[4,3,512]{2,1,0:T(4,128)S(1)}, u32[]{:S(2)}, u32[]{:S(2)}) collective-permute-start(f32[4,3,512]{2,1,0:T(4,128)S(1)} %get-tuple-element.292), channel_id=1, source_target_pairs={{1,0},{2,1},{3,2},{5,4},{6,5},{7,6},{9,8},{10,9},{11,10},{13,12},{... | collective-permute-start | bytes 73736 | tf_op jit(solution)/shard_map/ppermute | solution.py:24
  77.5 6.1 %collective-permute-start.6 = (f32[4,3,512]{2,1,0:T(4,128)S(1)}, f32[4,3,512]{2,1,0:T(4,128)S(1)}, u32[]{:S(2)}, u32[]{:S(2)}) collective-permute-start(f32[4,3,512]{2,1,0:T(4,128)S(1)} %get-tuple-element.291), channel_id=1, source_target_pairs={{0,1},{1,2},{2,3},{4,5},{5,6},{6,7},{8,9},{9,10},{10,11},{12,13},{... | collective-permute-start | bytes 73736 | tf_op jit(solution)/shard_map/ppermute | solution.py:22
  86.8 6.4 %collective-permute-start.9 = (f32[4,3,512]{2,1,0:T(4,128)S(1)}, f32[4,3,512]{2,1,0:T(4,128)S(1)}, u32[]{:S(2)}, u32[]{:S(2)}) collective-permute-start(f32[4,3,512]{2,1,0:T(4,128)S(1)} %get-tuple-element.289), channel_id=1, source_target_pairs={{1,0},{2,1},{3,2},{5,4},{6,5},{7,6},{9,8},{10,9},{11,10},{13,12},{... | collective-permute-start | bytes 73736 | tf_op jit(solution)/shard_map/ppermute | solution.py:24
  88.1 6.4 %collective-permute-start.8 = (f32[4,3,512]{2,1,0:T(4,128)S(1)}, f32[4,3,512]{2,1,0:T(4,128)S(1)}, u32[]{:S(2)}, u32[]{:S(2)}) collective-permute-start(f32[4,3,512]{2,1,0:T(4,128)S(1)} %get-tuple-element.288), channel_id=1, source_target_pairs={{0,1},{1,2},{2,3},{4,5},{5,6},{6,7},{8,9},{9,10},{10,11},{12,13},{... | collective-permute-start | bytes 73736 | tf_op jit(solution)/shard_map/ppermute | solution.py:22
  97.7 19.6 %collective-permute-start.11 = (f32[4,3,512]{2,1,0:T(4,128)S(1)}, f32[4,3,512]{2,1,0:T(4,128)S(1)}, u32[]{:S(2)}, u32[]{:S(2)}) collective-permute-start(f32[4,3,512]{2,1,0:T(4,128)S(1)} %get-tuple-element.286), channel_id=1, source_target_pairs={{1,0},{2,1},{3,2},{5,4},{6,5},{7,6},{9,8},{10,9},{11,10},{13,12},{... | collective-permute-start | bytes 73736 | tf_op jit(solution)/shard_map/ppermute | solution.py:24
  99.0 18.3 %collective-permute-start.10 = (f32[4,3,512]{2,1,0:T(4,128)S(1)}, f32[4,3,512]{2,1,0:T(4,128)S(1)}, u32[]{:S(2)}, u32[]{:S(2)}) collective-permute-start(f32[4,3,512]{2,1,0:T(4,128)S(1)} %get-tuple-element.285), channel_id=1, source_target_pairs={{0,1},{1,2},{2,3},{4,5},{5,6},{6,7},{8,9},{9,10},{10,11},{12,13},{... | collective-permute-start | bytes 73736 | tf_op jit(solution)/shard_map/ppermute | solution.py:22
Sparse Core Ops, SparseCore 0:
  44.0 31.1 all-gather.2
where the time goes:
time: 130 us; the launch traced here: 129 us
  starting transfers between devices  37.5 us (29%)
  waiting for transfers between devices  36.4 us (28%)
  between operations  19 us (15%)
  other arithmetic  18.5 us (14%)
  blocking collectives  11.2 us (9%)
  local copies, waits for them, and re-layouts  6.58 us (5%)
    ppermute x6, starting transfers between devices, with_halo(): lax.ppermute(tail, axis, [(i, (i + 1) % count) for i in range(ends)])  29.7 us
    all_gather x1, waiting for transfers between devices, on_device(): piece = lax.all_gather(before[None], 'member', axis=0, tiled=True)  28.8 us
    psum x1, blocking collectives, on_device(): score = lax.psum(local_score, 'domain') / (total_rows * width)  11.2 us
    ppermute x6, starting transfers between devices, with_halo(): lax.ppermute(head, axis, [((i + 1) % count, i) for i in range(ends)])  7.75 us
    ppermute x6, waiting for transfers between devices, with_halo(): lax.ppermute(tail, axis, [(i, (i + 1) % count) for i in range(ends)])  7.57 us
    add x18, other arithmetic, tendency(): advect = speed_u * grad_x + speed_v * grad_y  4.8 us
    slice x36, local copies, waits for them, and re-layouts, gradients(): east = jnp.roll(middle, -1, axis=-1)  4.43 us
    another operation x36, other arithmetic, tendency(): fluxes = jnp.stack([depth * padded[1], depth * padded[2]])  3.2 us
  transfers between devices with their start and end apart: 13, of which 6 were waited for; matrix products, arithmetic and copies ran while one was open for 2% of the time, Pallas kernels for 0%

commit v1 on v0

v1 whole, which is shorter than its diff:
```python
import functools

import jax
import jax.numpy as jnp
from jax import lax
from jax.experimental import pallas as pl
from jax.experimental.pallas import tpu as pltpu
from jax.sharding import PartitionSpec as P

STEPS = 3
REACH = 3 * STEPS

time_step = 0.1
viscous = 0.05
coriolis = 1.0

LANES = 128
SUB = 8
VMEM = pl.BlockSpec(memory_space=pltpu.VMEM)
SMEM = pl.BlockSpec(memory_space=pltpu.SMEM)


def stage(src, base, dst, first, count, keep, gain, global_row, total_rows):
    chunks = src.shape[1]
    lane = lax.broadcasted_iota(jnp.int32, (SUB, LANES), 1)
    sub = lax.broadcasted_iota(jnp.int32, (SUB, LANES), 0)
    at_last = lane == LANES - 1
    at_first = lane == 0
    step = gain * time_step
    for row in range(first, first + count, SUB):

        def load(field, chunk, offset):
            return src[field, chunk, pl.ds(row + offset, SUB), :]

        cells = [[load(f, j, 0) for j in range(chunks)] for f in range(4)]
        to_west = [[pltpu.roll(c, LANES - 1, 1) for c in line] for line in cells]
        to_east = [[pltpu.roll(c, 1, 1) for c in line] for line in cells]
        rows = (sub + (row + global_row)).astype(jnp.float32)
        turn = ((rows + 0.5) * (2.0 * coriolis / total_rows) - coriolis) * step
        for j in range(chunks):
            c = [cells[f][j] for f in range(4)]
            n = [load(f, j, 1) for f in range(4)]
            s = [load(f, j, -1) for f in range(4)]
            e = [jnp.where(at_last, to_west[f][(j + 1) % chunks], to_west[f][j]) for f in range(4)]
            w = [jnp.where(at_first, to_east[f][(j - 1) % chunks], to_east[f][j]) for f in range(4)]
            dx = [e[f] - w[f] for f in range(4)]
            dy = [n[f] - s[f] for f in range(4)]
            near = [(e[f] + w[f]) + (n[f] + s[f]) for f in range(4)]
            u = c[1] * (-0.5 * step)
            v = c[2] * (-0.5 * step)
            out = [
                near[f] * (step * viscous) + c[f] * (gain - 4.0 * step * viscous)
                for f in range(4)
            ]
            flux = ((1.0 + e[0]) * e[1] - (1.0 + w[0]) * w[1]) + (
                (1.0 + n[0]) * n[2] - (1.0 + s[0]) * s[2]
            )
            out[0] = out[0] + flux * (-0.5 * step)
            out[1] = out[1] + (u * dx[1] + v * dy[1]) + (turn * c[2] - dx[0] * (0.5 * step))
            out[2] = out[2] + (u * dx[2] + v * dy[2]) - (turn * c[1] + dy[0] * (0.5 * step))
            out[3] = out[3] + (u * dx[3] + v * dy[3])
            for f in range(4):
                if keep:
                    out[f] = out[f] + keep * base[f, j, pl.ds(row, SUB), :]
                dst[f, j, pl.ds(row, SUB), :] = out[f]


def advance(bufs, origin, rows, reach, domain, domains, total_rows):
    state, one, two = bufs
    global_row = domain * rows - origin
    thirds = ((state, one, 0.0, 1.0), (one, two, 0.75, 0.25), (two, state, 1.0 / 3.0, 2.0 / 3.0))
    for _ in range(STEPS):
        for src, dst, keep, gain in thirds:
            reach -= 1
            first, count = origin - reach, rows + 2 * reach
            stage(src, state, dst, first, count, keep, gain, global_row, total_rows)
            if reach > 0:
                blank = jnp.zeros(dst.shape[:2] + (1, LANES), jnp.float32)

                @pl.when(domain == 0)
                def _():
                    dst[:, :, pl.ds(origin - 1, 1), :] = blank

                @pl.when(domain == domains - 1)
                def _():
                    dst[:, :, pl.ds(origin + rows, 1), :] = blank


def put(buf, field, row, count, block, row_from, add=False):
    for j in range(buf.shape[1]):
        piece = block[pl.ds(row_from, count), pl.ds(j * LANES, LANES)]
        if add:
            piece = piece + buf[field, j, pl.ds(row, count), :]
        buf[field, j, pl.ds(row, count), :] = piece


class Sizes:
    def __init__(self, rows):
        self.rows = rows
        self.half = rows // 2
        self.extra = max(0, 2 * REACH - self.half)
        self.half_rows = 4 * (self.half + self.extra)
        self.body = REACH // SUB * SUB
        self.tail = REACH - self.body
        self.edge_rows = 8 * REACH

    def half_at(self, field):
        return field * self.half

    def extra_at(self, field):
        return 4 * self.half + field * self.extra

    def edge_at(self, which, field):
        return (which * 4 + field) * self.body

    def tail_at(self, which, field):
        return 8 * self.body + (which * 4 + field) * self.tail


def pack_kernel(sizes, state, pert, mine, other, edge_one, edge_two):
    rows, half, extra, body, tail = sizes.rows, sizes.half, sizes.extra, sizes.body, sizes.tail
    core = lax.rem(lax.axis_index("member"), 2)
    parity = lax.rem(lax.axis_index("domain"), 2)

    def south_half(out):
        for f in range(4):
            out[pl.ds(sizes.half_at(f), half), :] = state[f, pl.ds(0, half), :]
            out[pl.ds(sizes.extra_at(f), extra), :] = state[f, pl.ds(half, extra), :]

    def north_half(out):
        for f in range(4):
            out[pl.ds(sizes.half_at(f), half), :] = state[f, pl.ds(rows - half, half), :]
            out[pl.ds(sizes.extra_at(f), extra), :] = state[f, pl.ds(rows - half - extra, extra), :]

    def south_edge(out):
        for k, a in enumerate((state, pert)):
            for f in range(4):
                out[pl.ds(sizes.edge_at(k, f), body), :] = a[f, pl.ds(0, body), :]
                out[pl.ds(sizes.tail_at(k, f), tail), :] = a[f, pl.ds(body, tail), :]

    def north_edge(out):
        for k, a in enumerate((state, pert)):
            for f in range(4):
                out[pl.ds(sizes.edge_at(k, f), body), :] = a[f, pl.ds(rows - body, body), :]
                out[pl.ds(sizes.tail_at(k, f), tail), :] = a[f, pl.ds(rows - REACH, tail), :]

    @pl.when(core == 0)
    def _():
        south_half(mine)
        north_half(other)

    @pl.when(core == 1)
    def _():
        north_half(mine)
        south_half(other)

    @pl.when(parity == 0)
    def _():
        north_edge(edge_one)
        south_edge(edge_two)

    @pl.when(parity == 1)
    def _():
        south_edge(edge_one)
        north_edge(edge_two)


class Place:
    def __init__(self, chips_a, chips_b):
        self.sizes = (chips_a, chips_b)
        member = lax.axis_index("member")
        self.core = lax.rem(member, 2)
        chip = member // 2
        self.a, self.b = chip // chips_b, lax.rem(chip, chips_b)

    def child(self, hop, core):
        chips_a, chips_b = self.sizes
        a = jnp.where(self.core == 0, lax.rem(self.a + hop, chips_a), self.a)
        b = jnp.where(self.core == 0, self.b, lax.rem(self.b + hop, chips_b))
        return (a * chips_b + b) * 2 + core

    def first_hop(self, parent):
        chips_a, chips_b = self.sizes
        chip = parent // 2
        a, b = chip // chips_b, lax.rem(chip, chips_b)
        return jnp.where(
            self.core == 0,
            lax.rem(self.b - b + chips_b, chips_b),
            lax.rem(self.a - a + chips_a, chips_a),
        )

    def second_hop(self, parent):
        chips_a, chips_b = self.sizes
        chip = parent // 2
        a, b = chip // chips_b, lax.rem(chip, chips_b)
        return jnp.where(
            self.core == 0,
            lax.rem(self.a - a + chips_a, chips_a),
            lax.rem(self.b - b + chips_b, chips_b),
        )


def parent_of(parents, member):
    return jnp.clip(parents[member], 0, parents.shape[0] - 1)


def pick_kernel(chips, hops, parents, *refs):
    place = Place(*chips)
    held, outs = refs[: 2 * hops], refs[2 * hops :]
    at = 0
    for hop in range(hops):
        for own in (True, False):
            core = place.core if own else 1 - place.core
            parent = parent_of(parents, place.child(hop, core))
            index = 2 * place.first_hop(parent) + jnp.where(
                lax.rem(parent, 2) == place.core, 0, 1
            )
            out = outs[at]
            at += 1
            for k in range(2 * hops):

                @pl.when(index == k)
                def _():
                    out[...] = held[k][...]


def settle_kernel(chips, own, parents, *refs):
    place = Place(*chips)
    sources, out = refs[:-1], refs[-1]
    core = place.core if own else 1 - place.core
    parent = parent_of(parents, place.child(0, core))
    index = place.second_hop(parent)
    for k, source in enumerate(sources):

        @pl.when(index == k)
        def _():
            out[...] = source[...]


def put_edges(sizes, which, buf, origin, edge_one, edge_two, add=False):
    rows, body, tail = sizes.rows, sizes.body, sizes.tail
    parity = lax.rem(lax.axis_index("domain"), 2)

    def south(edge):
        for f in range(4):
            put(buf, f, origin - body, body, edge, sizes.edge_at(which, f), add)
            put(buf, f, origin - REACH, tail, edge, sizes.tail_at(which, f), add)

    def north(edge):
        for f in range(4):
            put(buf, f, origin + rows, body, edge, sizes.edge_at(which, f), add)
            put(buf, f, origin + rows + body, tail, edge, sizes.tail_at(which, f), add)

    @pl.when(parity == 0)
    def _():
        north(edge_one)
        south(edge_two)

    @pl.when(parity == 1)
    def _():
        south(edge_one)
        north(edge_two)


def score_kernel(sizes, domains, state, edge_one, edge_two, out, *bufs):
    rows = sizes.rows
    origin = 16
    total_rows = rows * domains
    domain = lax.axis_index("domain")
    for f in range(4):
        put(bufs[0], f, origin, rows, state.at[f], 0)
    put_edges(sizes, 0, bufs[0], origin, edge_one, edge_two)
    advance(bufs, origin, rows, REACH, domain, domains, total_rows)
    sub = lax.broadcasted_iota(jnp.int32, (SUB, LANES), 0)
    total = jnp.zeros((SUB, LANES), jnp.float32)
    for row in range(0, rows, SUB):
        line = jnp.zeros((SUB, LANES), jnp.float32)
        for j in range(bufs[0].shape[1]):
            q = bufs[0][3, j, pl.ds(origin + row, SUB), :]
            line = line + q * q
        place = (sub + (row + domain * rows)).astype(jnp.float32)
        total = total + (1.0 + 2.0 * place / (total_rows - 1)) * line
    out[...] = total


def final_kernel(
    sizes, domains, own_half, far_half, near_halo, far_halo, pert, edge_one, edge_two, out, *bufs
):
    rows, half, extra = sizes.rows, sizes.half, sizes.extra
    origin = 24
    total_rows = rows * domains
    domain = lax.axis_index("domain")
    core = lax.rem(lax.axis_index("member"), 2)
    start = bufs[0]

    def fill(south, north, south_halo, north_halo):
        for f in range(4):
            at, more = sizes.half_at(f), sizes.extra_at(f)
            put(start, f, origin - half, half, south_halo, at)
            put(start, f, origin - half - extra, extra, south_halo, more)
            put(start, f, origin, half, south, at)
            put(start, f, origin + half, half, north, at)
            put(start, f, origin + rows, half, north_halo, at)
            put(start, f, origin + rows + half, extra, north_halo, more)

    @pl.when(core == 0)
    def _():
        fill(own_half, far_half, near_halo, far_halo)

    @pl.when(core == 1)
    def _():
        fill(far_half, own_half, far_halo, near_halo)

    advance(bufs, origin, rows, 2 * REACH, domain, domains, total_rows)
    for f in range(4):
        put(start, f, origin, rows, pert.at[f], 0, add=True)
    put_edges(sizes, 1, start, origin, edge_one, edge_two, add=True)
    advance(bufs, origin, rows, REACH, domain, domains, total_rows)
    for f in range(4):
        for j in range(start.shape[1]):
            out[f, :, pl.ds(j * LANES, LANES)] = start[f, j, pl.ds(origin, rows), :]


def chip_grid(chips):
    b = 1
    while chips % (2 * b) == 0 and (2 * b) * (2 * b) <= chips:
        b *= 2
    return chips // b, b


def on_device(state, perturbation, parents, members, domains):
    state, perturbation = state[0], perturbation[0]
    rows, width = state.shape[1:]
    sizes = Sizes(rows)
    chunks = width // LANES
    chips = chip_grid(members // 2)
    chips_a, chips_b = chips
    hops = max(chips)
    params = pltpu.CompilerParams(vmem_limit_bytes=40 * 2**20)
    half_shape = jax.ShapeDtypeStruct((sizes.half_rows, width), jnp.float32)
    edge_shape = jax.ShapeDtypeStruct((sizes.edge_rows, width), jnp.float32)

    def member(a, b, core):
        return ((a % chips_a) * chips_b + b % chips_b) * 2 + core

    everywhere = [(a, b) for a in range(chips_a) for b in range(chips_b)]
    sibling = [(i, i ^ 1) for i in range(members)]

    def same_core(first, k):
        pairs = []
        for a, b in everywhere:
            if k < (chips_b if first else chips_a):
                pairs.append((member(a, b, 0), member(a, b + k, 0) if first else member(a + k, b, 0)))
            if k < (chips_a if first else chips_b):
                pairs.append((member(a, b, 1), member(a + k, b, 1) if first else member(a, b + k, 1)))
        return pairs

    def other_core(k):
        pairs = []
        for a, b in everywhere:
            if k < chips_a:
                pairs.append((member(a, b, 0), member(a + k, b, 1)))
            if k < chips_b:
                pairs.append((member(a, b, 1), member(a, b + k, 0)))
        return pairs

    def flat(m, z):
        return m * domains + z

    south_north = []
    for chip in range(members // 2):
        for z in range(1, domains):
            south_north.append((flat(2 * chip, z), flat(2 * chip + 1, z - 1)))
            south_north.append((flat(2 * chip + 1, z - 1), flat(2 * chip, z)))
    both = ("member", "domain")
    pair_one = [(z, z ^ 1) for z in range(domains) if z ^ 1 < domains]
    pair_two = [(z, ((z + 1) ^ 1) - 1) for z in range(domains) if 0 <= ((z + 1) ^ 1) - 1 < domains]

    mine, other, edge_one, edge_two = pl.pallas_call(
        functools.partial(pack_kernel, sizes),
        out_shape=(half_shape, half_shape, edge_shape, edge_shape),
        in_specs=[VMEM, VMEM],
        out_specs=(VMEM,) * 4,
        compiler_params=params,
    )(state, perturbation)

    held = [mine, None]
    for k in range(1, hops):
        held.append(lax.ppermute(mine, "member", same_core(True, k)))
        held.append(lax.ppermute(other, "member", other_core(k)))
    held[1] = lax.ppermute(other, "member", sibling)
    edge_one = lax.ppermute(edge_one, "domain", pair_one)
    edge_two = lax.ppermute(edge_two, "domain", pair_two)

    picked = pl.pallas_call(
        functools.partial(pick_kernel, chips, hops),
        out_shape=(half_shape,) * (2 * hops),
        in_specs=[SMEM] + [VMEM] * (2 * hops),
        out_specs=(VMEM,) * (2 * hops),
        compiler_params=params,
    )(parents, *held)

    def settle(own):
        which = 0 if own else 1
        sources = [picked[which]]
        for k in range(1, hops):
            sources.append(lax.ppermute(picked[2 * k + which], "member", same_core(False, k)))
        return pl.pallas_call(
            functools.partial(settle_kernel, chips, own),
            out_shape=half_shape,
            in_specs=[SMEM] + [VMEM] * hops,
            out_specs=VMEM,
            compiler_params=params,
        )(parents, *sources)

    own_half = settle(True)
    sibling_halo = lax.ppermute(own_half, both, south_north)
    sibling_half = settle(False)
    near_halo = lax.ppermute(sibling_half, both, south_north)
    far_half = lax.ppermute(sibling_half, "member", sibling)
    far_halo = lax.ppermute(sibling_halo, "member", sibling)

    score = pl.pallas_call(
        functools.partial(score_kernel, sizes, domains),
        out_shape=jax.ShapeDtypeStruct((SUB, LANES), jnp.float32),
        in_specs=[VMEM] * 3,
        out_specs=VMEM,
        scratch_shapes=[pltpu.VMEM((4, chunks, rows + 32, LANES), jnp.float32)] * 3,
        compiler_params=params,
    )(state, edge_one, edge_two)
    if domains & (domains - 1) == 0:
        bit = 1
        while bit < domains:
            score = score + lax.ppermute(score, "domain", [(z, z ^ bit) for z in range(domains)])
            bit *= 2
    else:
        score = lax.psum(score, "domain")
    score = jnp.sum(score) / (rows * domains * width)

    after = pl.pallas_call(
        functools.partial(final_kernel, sizes, domains),
        out_shape=jax.ShapeDtypeStruct((4, rows, width), jnp.float32),
        in_specs=[VMEM] * 7,
        out_specs=VMEM,
        scratch_shapes=[pltpu.VMEM((4, chunks, rows + 48, LANES), jnp.float32)] * 3,
        compiler_params=params,
    )(own_half, far_half, near_halo, far_halo, perturbation, edge_one, edge_two)
    return after[None], jnp.reshape(score, (1,))


def solution(mesh):
    placed = (P("member", None, "domain", None), P("member", None, "domain", None), P())
    return jax.shard_map(
        functools.partial(
            on_device, members=mesh.shape["member"], domains=mesh.shape["domain"]
        ),
        mesh=mesh,
        in_specs=placed,
        out_specs=(P("member", None, "domain", None), P("member")),
        check_vma=False,
    )
```

time: 130 us -> 50.3 us (0.39)
  waiting for transfers between devices: 36.4 us -> 11.8 us
  other arithmetic: 18.5 us -> 0.6 us
  starting transfers between devices: 37.5 us -> 20.8 us
  between operations: 19 us -> 2.57 us
  Pallas kernels: 0 us -> 12.4 us
  blocking collectives: 11.2 us -> 0 us
  local copies, waits for them, and re-layouts: 6.58 us -> 1.91 us
    all_gather x1 -> x0, waiting for transfers between devices: 28.8 us -> none  [on_device(): piece = lax.all_gather(before[None], 'member', axis=0, tiled=True)]
    ppermute x12 -> x13, starting transfers between devices: 37.4 us -> 20.8 us  [the longest x1 4.44 us: on_device(): far_halo = lax.ppermute(sibling_halo, 'member', sibling)]
    pallas_call x0 -> x6, Pallas kernels: none -> 12.4 us  [the longest x1 7.26 us: on_device(): pl.pallas_call(functools.partial(final_kernel, sizes, domains), out_shape...]
    psum x1 -> x0, blocking collectives: 11.2 us -> none  [on_device(): score = lax.psum(local_score, 'domain') / (total_rows * width)]
    add x43 -> x1, other arithmetic: 9.53 us -> 0.01 us  [on_device(): score + lax.ppermute(score, 'domain', [(z, z ^ bit) for z in range(domain...]
    slice x42 -> x0, local copies, waits for them, and re-layouts: 5.4 us -> none  [the longest x36 4.43 us: gradients(): east = jnp.roll(middle, -1, axis=-1)]
    ppermute x12 -> x13, waiting for transfers between devices: 7.59 us -> 11.8 us  [the longest x2 4.18 us: on_device(): lax.ppermute(score, 'domain', [(z, z ^ bit) for z in range(domains)])]
    another operation x36 -> x0, other arithmetic: 3.2 us -> none  [tendency(): fluxes = jnp.stack([depth * padded[1], depth * padded[2]])]
  transfers between devices with their start and end apart: 13 -> 13, of which waited for: 6 -> 5; matrix products, arithmetic and copies ran while one was open for 2% -> 1% of each run, Pallas kernels for 0% -> 9%
where the time goes in v1:
time: 50.3 us; the launch traced here: 50.1 us
  starting transfers between devices  20.8 us (41%)
  Pallas kernels  12.4 us (25%)
  waiting for transfers between devices  11.8 us (23%)
  between operations  2.57 us (5%)
  local copies, waits for them, and re-layouts  1.91 us (4%)
  other arithmetic  0.6 us (1%)
    pallas_call x1, Pallas kernels, on_device(): pl.pallas_call(functools.partial(final_kernel, sizes, domains), out_shape...  7.26 us
    ppermute x1, starting transfers between devices, on_device(): far_halo = lax.ppermute(sibling_halo, 'member', sibling)  4.44 us
    ppermute x2, waiting for transfers between devices, on_device(): lax.ppermute(score, 'domain', [(z, z ^ bit) for z in range(domains)])  4.18 us
    ppermute x2, starting transfers between devices, on_device(): lax.ppermute(score, 'domain', [(z, z ^ bit) for z in range(domains)])  4 us
    ppermute x1, waiting for transfers between devices, on_device(): held.append(lax.ppermute(mine, 'member', same_core(True, k)))  3.63 us
    ppermute x1, starting transfers between devices, on_device(): edge_one = lax.ppermute(edge_one, 'domain', pair_one)  3.39 us
    pallas_call x1, Pallas kernels, on_device(): pl.pallas_call(functools.partial(score_kernel, sizes, domains), out_shape...  3.1 us
    ppermute x2, waiting for transfers between devices, settle(): lax.ppermute(picked[2 * k + which], 'member', same_core(False, k))  3.05 us
  transfers between devices with their start and end apart: 13, of which 5 were waited for; matrix products, arithmetic and copies ran while one was open for 1% of the time, Pallas kernels for 9%

profile of v1, /device:TPU:0, one launch (start us, length us, event | category | flops | bytes accessed | tf_op | source)
XLA Modules:
  0.0 50.1 jit_solution(7240215874990977568)
XLA Ops:
  0.6 0.0 copy-start
  0.6 0.9 %copy-done = f32[1,4,32,512]{3,2,1,0:T(8,128)S(1)} copy-done((f32[1,4,32,512]{3,2,1,0:T(8,128)S(1)}, f32[1,4,32,512]{3,2,1,0:T(8,128)}, u32[]{:S(2)}) %copy-start) | copy-done | bytes 262168
  1.6 0.0 copy-start.2
  1.6 0.9 %copy-done.2 = f32[1,4,32,512]{3,2,1,0:T(8,128)S(1)} copy-done((f32[1,4,32,512]{3,2,1,0:T(8,128)S(1)}, f32[1,4,32,512]{3,2,1,0:T(8,128)}, u32[]{:S(2)}) %copy-start.2) | copy-done | bytes 262168
  2.5 0.1 shard_map.50
  2.6 0.0 copy-start.4
  2.6 0.5 %collective-permute-start = (f32[72,512]{1,0:T(8,128)S(1)}, f32[72,512]{1,0:T(8,128)S(1)}, u32[]{:S(2)}, u32[]{:S(2)}) collective-permute-start(f32[72,512]{1,0:T(8,128)S(1)} %get-tuple-element.11), channel_id=1, source_target_pairs={{0,4},{4,0},{8,12},{12,8},{16,20},{20,16},{24,28},{28,24},{1,5},{5... | collective-permute-start | bytes 442376 | tf_op jit(solution)/shard_map/ppermute | solution.py:391
  3.1 2.6 %collective-permute-start.1 = (f32[72,512]{1,0:T(8,128)S(1)}, f32[72,512]{1,0:T(8,128)S(1)}, u32[]{:S(2)}, u32[]{:S(2)}) collective-permute-start(f32[72,512]{1,0:T(8,128)S(1)} %get-tuple-element.10.refs_0_), channel_id=1, source_target_pairs={{0,8},{4,20},{8,0},{12,28},{16,24},{20,4},{24,16},{28,12},{1,9},{5... | collective-permute-start | bytes 442376 | tf_op jit(solution)/shard_map/ppermute | solution.py:389
  5.7 0.1 collective-permute-start.2
  5.8 0.0 collective-permute-done.refs_1_
  5.8 3.6 %collective-permute-done.1.refs_2_ = f32[72,512]{1,0:T(8,128)S(1)} collective-permute-done((f32[72,512]{1,0:T(8,128)S(1)}, f32[72,512]{1,0:T(8,128)S(1)}, u32[]{:S(2)}, u32[]{:S(2)}) %collective-permute-start.1) | collective-permute-done | bytes 147488 | tf_op jit(solution)/shard_map/ppermute | solution.py:389
  9.4 1.0 %collective-permute-done.2.refs_3_ = f32[72,512]{1,0:T(8,128)S(1)} collective-permute-done((f32[72,512]{1,0:T(8,128)S(1)}, f32[72,512]{1,0:T(8,128)S(1)}, u32[]{:S(2)}, u32[]{:S(2)}) %collective-permute-start.2) | collective-permute-done | bytes 147488 | tf_op jit(solution)/shard_map/ppermute | solution.py:390
  10.4 0.0 copy-done.4
  10.4 0.8 %shard_map.51 = (f32[72,512]{1,0:T(8,128)S(1)}, f32[72,512]{1,0:T(8,128)S(1)}, f32[72,512]{1,0:T(8,128)S(1)}, f32[72,512]{1,0:T(8,128)S(1)}) custom-call(s32[8]{0:T(128)S(1)} %copy-done.4, f32[72,512]{1,0:T(8,128)S(1)} %get-tuple-element.10.refs_0_, f32[72,512]{1,0:T(8,128)S(1)} %collective-permute-done.refs_1_, ...), custom_call_target="tpu_custom_call" | custom-call | tf_op jit(solution)/shard_map/pallas_call | solution.py:395
  11.2 2.1 %collective-permute-start.3 = (f32[72,512]{1,0:T(8,128)S(1)}, f32[72,512]{1,0:T(8,128)S(1)}, u32[]{:S(2)}, u32[]{:S(2)}) collective-permute-start(f32[72,512]{1,0:T(8,128)S(1)} %get-tuple-element.13), channel_id=1, source_target_pairs={{0,16},{4,12},{8,24},{12,4},{16,0},{20,28},{24,8},{28,20},{1,17},{... | collective-permute-start | bytes 442376 | tf_op jit(solution)/shard_map/ppermute | solution.py:407
  13.3 0.1 collective-permute-start.4
  13.4 3.0 %collective-permute-done.3.refs_1_ = f32[72,512]{1,0:T(8,128)S(1)} collective-permute-done((f32[72,512]{1,0:T(8,128)S(1)}, f32[72,512]{1,0:T(8,128)S(1)}, u32[]{:S(2)}, u32[]{:S(2)}) %collective-permute-start.3) | collective-permute-done | bytes 147488 | tf_op jit(solution)/shard_map/ppermute | solution.py:407
  16.4 0.6 %shard_map.52.own_half = f32[72,512]{1,0:T(8,128)S(1)} custom-call(s32[8]{0:T(128)S(1)} %copy-done.4, f32[72,512]{1,0:T(8,128)S(1)} %get-tuple-element.12.refs_0_, f32[72,512]{1,0:T(8,128)S(1)} %collective-permute-done.3.refs_1_), custom_call_target="tpu_custom_call" | custom-call | tf_op jit(solution)/shard_map/pallas_call | solution.py:408
  17.0 0.0 copy-start.1
  17.0 0.8 %collective-permute-start.7 = (f32[72,512]{1,0:T(8,128)S(1)}, f32[72,512]{1,0:T(8,128)S(1)}, u32[]{:S(2)}, u32[]{:S(2)}) collective-permute-start(f32[72,512]{1,0:T(8,128)S(1)} %shard_map.52.own_half), channel_id=1, source_target_pairs={{1,4},{4,1},{2,5},{5,2},{3,6},{6,3},{9,12},{12,9},{10,13},{13,10},... | collective-permute-start | bytes 442376 | tf_op jit(solution)/shard_map/ppermute | solution.py:417
  17.8 3.4 %collective-permute-start.9 = (f32[72,512]{1,0:T(8,128)S(1)}, f32[72,512]{1,0:T(8,128)S(1)}, u32[]{:S(2)}, u32[]{:S(2)}) collective-permute-start(f32[72,512]{1,0:T(8,128)S(1)} %get-tuple-element.16), channel_id=1, source_target_pairs={{0,1},{1,0},{2,3},{3,2},{4,5},{5,4},{6,7},{7,6},{8,9},{9,8},{10,11... | collective-permute-start | bytes 442376 | tf_op jit(solution)/shard_map/ppermute | solution.py:392
  21.2 0.7 %collective-permute-start.10 = (f32[72,512]{1,0:T(8,128)S(1)}, f32[72,512]{1,0:T(8,128)S(1)}, u32[]{:S(2)}, u32[]{:S(2)}) collective-permute-start(f32[72,512]{1,0:T(8,128)S(1)} %get-tuple-element.17), channel_id=1, source_target_pairs={{1,2},{2,1},{5,6},{6,5},{9,10},{10,9},{13,14},{14,13},{17,18},{18,... | collective-permute-start | bytes 442376 | tf_op jit(solution)/shard_map/ppermute | solution.py:393
  21.9 0.0 collective-permute-done.4.refs_1_
  21.9 0.6 %shard_map.53 = f32[72,512]{1,0:T(8,128)S(1)} custom-call(s32[8]{0:T(128)S(1)} %copy-done.4, f32[72,512]{1,0:T(8,128)S(1)} %get-tuple-element.14.refs_0_, f32[72,512]{1,0:T(8,128)S(1)} %collective-permute-done.4.refs_1_), custom_call_target="tpu_custom_call" | custom-call | tf_op jit(solution)/shard_map/pallas_call | solution.py:408
  22.5 0.0 copy-start.3
  22.5 1.5 %collective-permute-start.5 = (f32[72,512]{1,0:T(8,128)S(1)}, f32[72,512]{1,0:T(8,128)S(1)}, u32[]{:S(2)}, u32[]{:S(2)}) collective-permute-start(f32[72,512]{1,0:T(8,128)S(1)} %shard_map.53), channel_id=1, source_target_pairs={{0,4},{4,0},{8,12},{12,8},{16,20},{20,16},{24,28},{28,24},{1,5},{5... | collective-permute-start | bytes 442376 | tf_op jit(solution)/shard_map/ppermute | solution.py:420
  24.0 0.7 %collective-permute-start.6 = (f32[72,512]{1,0:T(8,128)S(1)}, f32[72,512]{1,0:T(8,128)S(1)}, u32[]{:S(2)}, u32[]{:S(2)}) collective-permute-start(f32[72,512]{1,0:T(8,128)S(1)} %shard_map.53), channel_id=1, source_target_pairs={{1,4},{4,1},{2,5},{5,2},{3,6},{6,3},{9,12},{12,9},{10,13},{13,10},... | collective-permute-start | bytes 442376 | tf_op jit(solution)/shard_map/ppermute | solution.py:419
  24.7 0.0 collective-permute-done.7
  24.7 4.4 %collective-permute-start.8 = (f32[72,512]{1,0:T(8,128)S(1)}, f32[72,512]{1,0:T(8,128)S(1)}, u32[]{:S(2)}, u32[]{:S(2)}) collective-permute-start(f32[72,512]{1,0:T(8,128)S(1)} %collective-permute-done.7), channel_id=1, source_target_pairs={{0,4},{4,0},{8,12},{12,8},{16,20},{20,16},{24,28},{28,24},{1,5},{5... | collective-permute-start | bytes 442376 | tf_op jit(solution)/shard_map/ppermute | solution.py:421
  29.1 0.0 collective-permute-done.9.edge_one
  29.1 0.0 collective-permute-done.10.edge_two
  29.1 0.0 copy-done.1
  29.1 3.1 %shard_map.55 = f32[8,128]{1,0:T(8,128)S(1)} custom-call(f32[4,32,512]{2,1,0:T(8,128)S(1)} %bitcast.5, f32[72,512]{1,0:T(8,128)S(1)} %collective-permute-done.9.edge_one, f32[72,512]{1,0:T(8,128)S(1)} %collective-permute-done.10.edge_two), custom_call_target="tpu_custom_call" | custom-call | tf_op jit(solution)/shard_map/pallas_call | solution.py:423
  32.2 1.6 %collective-permute-start.11 = (f32[8,128]{1,0:T(8,128)S(1)}, f32[8,128]{1,0:T(8,128)S(1)}, u32[]{:S(2)}, u32[]{:S(2)}) collective-permute-start(f32[8,128]{1,0:T(8,128)S(1)} %shard_map.55), channel_id=1, source_target_pairs={{0,1},{1,0},{2,3},{3,2},{4,5},{5,4},{6,7},{7,6},{8,9},{9,8},{10,11... | collective-permute-start | bytes 12296 | tf_op jit(solution)/shard_map/ppermute | solution.py:434
  33.8 2.1 %collective-permute-done.11 = f32[8,128]{1,0:T(8,128)S(1)} collective-permute-done((f32[8,128]{1,0:T(8,128)S(1)}, f32[8,128]{1,0:T(8,128)S(1)}, u32[]{:S(2)}, u32[]{:S(2)}) %collective-permute-start.11) | collective-permute-done | bytes 4128 | tf_op jit(solution)/shard_map/ppermute | solution.py:434
  35.9 2.4 %collective-permute-start.12 = (f32[8,128]{1,0:T(8,128)S(1)}, f32[8,128]{1,0:T(8,128)S(1)}, u32[]{:S(2)}, u32[]{:S(2)}) collective-permute-start(f32[8,128]{1,0:T(8,128)S(1)} %add.6), channel_id=1, source_target_pairs={{0,2},{1,3},{2,0},{3,1},{4,6},{5,7},{6,4},{7,5},{8,10},{9,11},{10,... | collective-permute-start | bytes 12296 | tf_op jit(solution)/shard_map/ppermute | solution.py:434
  38.3 2.1 %collective-permute-done.12 = f32[8,128]{1,0:T(8,128)S(1)} collective-permute-done((f32[8,128]{1,0:T(8,128)S(1)}, f32[8,128]{1,0:T(8,128)S(1)}, u32[]{:S(2)}, u32[]{:S(2)}) %collective-permute-start.12) | collective-permute-done | bytes 4128 | tf_op jit(solution)/shard_map/ppermute | solution.py:434
  40.4 0.6 %add_reduce_fusion = f32[]{:T(128)} fusion(f32[8,128]{1,0:T(8,128)S(1)} %add.6, f32[8,128]{1,0:T(8,128)S(1)} %collective-permute-done.12), kind=kLoop, calls=%fused_computation | loop fusion | flops 2047 | bytes 8196 | tf_op jit(solution)/shard_map/reduce_sum | solution.py:438
  41.7 0.0 collective-permute-done.5.far_half
  41.7 0.0 collective-permute-done.6.near_halo
  41.7 0.0 collective-permute-done.8.far_halo
  41.7 0.0 copy-done.3
  41.7 7.3 %shard_map.54 = f32[4,32,512]{2,1,0:T(8,128)} custom-call(f32[72,512]{1,0:T(8,128)S(1)} %shard_map.52.own_half, f32[72,512]{1,0:T(8,128)S(1)} %collective-permute-done.5.far_half, f32[72,512]{1,0:T(8,128)S(1)} %collective-permute-done.6.near_halo, f32[72,512]{1,0:T(8,128)S(1)} %collective-permute-done.8.far_halo, f32[4,32,512]{2,1,0:T(8,128)S(1)} %bitcast.7, ...), custom_call_target="tpu_custom_call" | custom-call | tf_op jit(solution)/shard_map/pallas_call | solution.py:440
  (1 shorter events, 0.0 us)
Async XLA Ops:
  0.6 1.0 %copy-start = (f32[1,4,32,512]{3,2,1,0:T(8,128)S(1)}, f32[1,4,32,512]{3,2,1,0:T(8,128)}, u32[]{:S(2)}) copy-start(f32[1,4,32,512]{3,2,1,0:T(8,128)} %param.3) | copy-start | bytes 786436
  1.6 0.9 %copy-start.2 = (f32[1,4,32,512]{3,2,1,0:T(8,128)S(1)}, f32[1,4,32,512]{3,2,1,0:T(8,128)}, u32[]{:S(2)}) copy-start(f32[1,4,32,512]{3,2,1,0:T(8,128)} %param.4) | copy-start | bytes 786436
  2.6 7.8 %copy-start.4 = (s32[8]{0:T(128)S(1)}, s32[8]{0:T(128)}, u32[]{:S(2)}) copy-start(s32[8]{0:T(128)} %parents.5) | copy-start | bytes 100
  2.6 3.2 %collective-permute-start = (f32[72,512]{1,0:T(8,128)S(1)}, f32[72,512]{1,0:T(8,128)S(1)}, u32[]{:S(2)}, u32[]{:S(2)}) collective-permute-start(f32[72,512]{1,0:T(8,128)S(1)} %get-tuple-element.11), channel_id=1, source_target_pairs={{0,4},{4,0},{8,12},{12,8},{16,20},{20,16},{24,28},{28,24},{1,5},{5... | collective-permute-start | bytes 442376 | tf_op jit(solution)/shard_map/ppermute | solution.py:391
  3.1 6.3 %collective-permute-start.1 = (f32[72,512]{1,0:T(8,128)S(1)}, f32[72,512]{1,0:T(8,128)S(1)}, u32[]{:S(2)}, u32[]{:S(2)}) collective-permute-start(f32[72,512]{1,0:T(8,128)S(1)} %get-tuple-element.10.refs_0_), channel_id=1, source_target_pairs={{0,8},{4,20},{8,0},{12,28},{16,24},{20,4},{24,16},{28,12},{1,9},{5... | collective-permute-start | bytes 442376 | tf_op jit(solution)/shard_map/ppermute | solution.py:389
  5.7 4.7 %collective-permute-start.2 = (f32[72,512]{1,0:T(8,128)S(1)}, f32[72,512]{1,0:T(8,128)S(1)}, u32[]{:S(2)}, u32[]{:S(2)}) collective-permute-start(f32[72,512]{1,0:T(8,128)S(1)} %get-tuple-element.11), channel_id=1, source_target_pairs={{0,20},{4,8},{8,28},{12,0},{16,4},{20,24},{24,12},{28,16},{1,21},{... | collective-permute-start | bytes 442376 | tf_op jit(solution)/shard_map/ppermute | solution.py:390
  11.2 5.2 %collective-permute-start.3 = (f32[72,512]{1,0:T(8,128)S(1)}, f32[72,512]{1,0:T(8,128)S(1)}, u32[]{:S(2)}, u32[]{:S(2)}) collective-permute-start(f32[72,512]{1,0:T(8,128)S(1)} %get-tuple-element.13), channel_id=1, source_target_pairs={{0,16},{4,12},{8,24},{12,4},{16,0},{20,28},{24,8},{28,20},{1,17},{... | collective-permute-start | bytes 442376 | tf_op jit(solution)/shard_map/ppermute | solution.py:407
  13.3 8.6 %collective-permute-start.4 = (f32[72,512]{1,0:T(8,128)S(1)}, f32[72,512]{1,0:T(8,128)S(1)}, u32[]{:S(2)}, u32[]{:S(2)}) collective-permute-start(f32[72,512]{1,0:T(8,128)S(1)} %get-tuple-element.15), channel_id=1, source_target_pairs={{0,16},{4,12},{8,24},{12,4},{16,0},{20,28},{24,8},{28,20},{1,17},{... | collective-permute-start | bytes 442376 | tf_op jit(solution)/shard_map/ppermute | solution.py:407
  17.0 12.1 %copy-start.1 = (f32[1,4,32,512]{3,2,1,0:T(8,128)S(1)}, f32[1,4,32,512]{3,2,1,0:T(8,128)}, u32[]{:S(2)}) copy-start(f32[1,4,32,512]{3,2,1,0:T(8,128)} %param.3) | copy-start | bytes 786436
  17.0 7.6 %collective-permute-start.7 = (f32[72,512]{1,0:T(8,128)S(1)}, f32[72,512]{1,0:T(8,128)S(1)}, u32[]{:S(2)}, u32[]{:S(2)}) collective-permute-start(f32[72,512]{1,0:T(8,128)S(1)} %shard_map.52.own_half), channel_id=1, source_target_pairs={{1,4},{4,1},{2,5},{5,2},{3,6},{6,3},{9,12},{12,9},{10,13},{13,10},... | collective-permute-start | bytes 442376 | tf_op jit(solution)/shard_map/ppermute | solution.py:417
  17.8 11.3 %collective-permute-start.9 = (f32[72,512]{1,0:T(8,128)S(1)}, f32[72,512]{1,0:T(8,128)S(1)}, u32[]{:S(2)}, u32[]{:S(2)}) collective-permute-start(f32[72,512]{1,0:T(8,128)S(1)} %get-tuple-element.16), channel_id=1, source_target_pairs={{0,1},{1,0},{2,3},{3,2},{4,5},{5,4},{6,7},{7,6},{8,9},{9,8},{10,11... | collective-permute-start | bytes 442376 | tf_op jit(solution)/shard_map/ppermute | solution.py:392
  21.2 7.9 %collective-permute-start.10 = (f32[72,512]{1,0:T(8,128)S(1)}, f32[72,512]{1,0:T(8,128)S(1)}, u32[]{:S(2)}, u32[]{:S(2)}) collective-permute-start(f32[72,512]{1,0:T(8,128)S(1)} %get-tuple-element.17), channel_id=1, source_target_pairs={{1,2},{2,1},{5,6},{6,5},{9,10},{10,9},{13,14},{14,13},{17,18},{18,... | collective-permute-start | bytes 442376 | tf_op jit(solution)/shard_map/ppermute | solution.py:393
  22.5 19.2 %copy-start.3 = (f32[1,4,32,512]{3,2,1,0:T(8,128)S(1)}, f32[1,4,32,512]{3,2,1,0:T(8,128)}, u32[]{:S(2)}) copy-start(f32[1,4,32,512]{3,2,1,0:T(8,128)} %param.4) | copy-start | bytes 786436
  22.5 19.1 %collective-permute-start.5 = (f32[72,512]{1,0:T(8,128)S(1)}, f32[72,512]{1,0:T(8,128)S(1)}, u32[]{:S(2)}, u32[]{:S(2)}) collective-permute-start(f32[72,512]{1,0:T(8,128)S(1)} %shard_map.53), channel_id=1, source_target_pairs={{0,4},{4,0},{8,12},{12,8},{16,20},{20,16},{24,28},{28,24},{1,5},{5... | collective-permute-start | bytes 442376 | tf_op jit(solution)/shard_map/ppermute | solution.py:420
  24.0 17.7 %collective-permute-start.6 = (f32[72,512]{1,0:T(8,128)S(1)}, f32[72,512]{1,0:T(8,128)S(1)}, u32[]{:S(2)}, u32[]{:S(2)}) collective-permute-start(f32[72,512]{1,0:T(8,128)S(1)} %shard_map.53), channel_id=1, source_target_pairs={{1,4},{4,1},{2,5},{5,2},{3,6},{6,3},{9,12},{12,9},{10,13},{13,10},... | collective-permute-start | bytes 442376 | tf_op jit(solution)/shard_map/ppermute | solution.py:419
  24.7 17.0 %collective-permute-start.8 = (f32[72,512]{1,0:T(8,128)S(1)}, f32[72,512]{1,0:T(8,128)S(1)}, u32[]{:S(2)}, u32[]{:S(2)}) collective-permute-start(f32[72,512]{1,0:T(8,128)S(1)} %collective-permute-done.7), channel_id=1, source_target_pairs={{0,4},{4,0},{8,12},{12,8},{16,20},{20,16},{24,28},{28,24},{1,5},{5... | collective-permute-start | bytes 442376 | tf_op jit(solution)/shard_map/ppermute | solution.py:421
  32.2 3.7 %collective-permute-start.11 = (f32[8,128]{1,0:T(8,128)S(1)}, f32[8,128]{1,0:T(8,128)S(1)}, u32[]{:S(2)}, u32[]{:S(2)}) collective-permute-start(f32[8,128]{1,0:T(8,128)S(1)} %shard_map.55), channel_id=1, source_target_pairs={{0,1},{1,0},{2,3},{3,2},{4,5},{5,4},{6,7},{7,6},{8,9},{9,8},{10,11... | collective-permute-start | bytes 12296 | tf_op jit(solution)/shard_map/ppermute | solution.py:434
  35.9 4.5 %collective-permute-start.12 = (f32[8,128]{1,0:T(8,128)S(1)}, f32[8,128]{1,0:T(8,128)S(1)}, u32[]{:S(2)}, u32[]{:S(2)}) collective-permute-start(f32[8,128]{1,0:T(8,128)S(1)} %add.6), channel_id=1, source_target_pairs={{0,2},{1,3},{2,0},{3,1},{4,6},{5,7},{6,4},{7,5},{8,10},{9,11},{10,... | collective-permute-start | bytes 12296 | tf_op jit(solution)/shard_map/ppermute | solution.py:434

commit v2 on v1

v2 whole, which is shorter than its diff:
```python
import functools

import jax
import jax.numpy as jnp
from jax import lax
from jax.experimental import pallas as pl
from jax.experimental.pallas import tpu as pltpu
from jax.sharding import PartitionSpec as P

STEPS = 3
REACH = 3 * STEPS

time_step = 0.1
viscous = 0.05
coriolis = 1.0

LANES = 128
SUB = 8
VMEM = pl.BlockSpec(memory_space=pltpu.VMEM)
SMEM = pl.BlockSpec(memory_space=pltpu.SMEM)


def stage(src, base, dst, first, count, keep, gain, global_row, total_rows):
    chunks = src.shape[1]
    lane = lax.broadcasted_iota(jnp.int32, (SUB, LANES), 1)
    sub = lax.broadcasted_iota(jnp.int32, (SUB, LANES), 0)
    at_last = lane == LANES - 1
    at_first = lane == 0
    step = gain * time_step
    for row in range(first, first + count, SUB):

        def load(field, chunk, offset):
            return src[field, chunk, pl.ds(row + offset, SUB), :]

        cells = [[load(f, j, 0) for j in range(chunks)] for f in range(4)]
        to_west = [[pltpu.roll(c, LANES - 1, 1) for c in line] for line in cells]
        to_east = [[pltpu.roll(c, 1, 1) for c in line] for line in cells]
        rows = (sub + (row + global_row)).astype(jnp.float32)
        turn = ((rows + 0.5) * (2.0 * coriolis / total_rows) - coriolis) * step
        for j in range(chunks):
            c = [cells[f][j] for f in range(4)]
            n = [load(f, j, 1) for f in range(4)]
            s = [load(f, j, -1) for f in range(4)]
            e = [jnp.where(at_last, to_west[f][(j + 1) % chunks], to_west[f][j]) for f in range(4)]
            w = [jnp.where(at_first, to_east[f][(j - 1) % chunks], to_east[f][j]) for f in range(4)]
            dx = [e[f] - w[f] for f in range(4)]
            dy = [n[f] - s[f] for f in range(4)]
            near = [(e[f] + w[f]) + (n[f] + s[f]) for f in range(4)]
            u = c[1] * (-0.5 * step)
            v = c[2] * (-0.5 * step)
            out = [
                near[f] * (step * viscous) + c[f] * (gain - 4.0 * step * viscous)
                for f in range(4)
            ]
            flux = ((1.0 + e[0]) * e[1] - (1.0 + w[0]) * w[1]) + (
                (1.0 + n[0]) * n[2] - (1.0 + s[0]) * s[2]
            )
            out[0] = out[0] + flux * (-0.5 * step)
            out[1] = out[1] + (u * dx[1] + v * dy[1]) + (turn * c[2] - dx[0] * (0.5 * step))
            out[2] = out[2] + (u * dx[2] + v * dy[2]) - (turn * c[1] + dy[0] * (0.5 * step))
            out[3] = out[3] + (u * dx[3] + v * dy[3])
            for f in range(4):
                if keep:
                    out[f] = out[f] + keep * base[f, j, pl.ds(row, SUB), :]
                dst[f, j, pl.ds(row, SUB), :] = out[f]


def advance(bufs, origin, rows, reach, domain, domains, total_rows):
    state, one, two = bufs
    global_row = domain * rows - origin
    thirds = ((state, one, 0.0, 1.0), (one, two, 0.75, 0.25), (two, state, 1.0 / 3.0, 2.0 / 3.0))
    for _ in range(STEPS):
        for src, dst, keep, gain in thirds:
            reach -= 1
            first, count = origin - reach, rows + 2 * reach
            stage(src, state, dst, first, count, keep, gain, global_row, total_rows)
            if reach > 0:
                blank = jnp.zeros(dst.shape[:2] + (1, LANES), jnp.float32)

                @pl.when(domain == 0)
                def _():
                    dst[:, :, pl.ds(origin - 1, 1), :] = blank

                @pl.when(domain == domains - 1)
                def _():
                    dst[:, :, pl.ds(origin + rows, 1), :] = blank


def put(buf, field, row, count, block, row_from, add=False):
    for j in range(buf.shape[1]):
        piece = block[pl.ds(row_from, count), pl.ds(j * LANES, LANES)]
        if add:
            piece = piece + buf[field, j, pl.ds(row, count), :]
        buf[field, j, pl.ds(row, count), :] = piece


class Sizes:
    def __init__(self, rows):
        self.rows = rows
        self.half = rows // 2
        self.half_rows = 4 * self.half
        self.body = REACH // SUB * SUB
        self.tail = REACH - self.body
        self.edge_rows = -(-4 * REACH // SUB) * SUB

    def half_at(self, field):
        return field * self.half

    def edge_at(self, field):
        return field * self.body

    def tail_at(self, field):
        return 4 * self.body + field * self.tail


def south_edge(sizes, load, out):
    for f in range(4):
        out[pl.ds(sizes.edge_at(f), sizes.body), :] = load(f, 0, sizes.body)
        out[pl.ds(sizes.tail_at(f), sizes.tail), :] = load(f, sizes.body, sizes.tail)


def north_edge(sizes, load, out, rows):
    for f in range(4):
        out[pl.ds(sizes.edge_at(f), sizes.body), :] = load(f, rows - sizes.body, sizes.body)
        out[pl.ds(sizes.tail_at(f), sizes.tail), :] = load(f, rows - REACH, sizes.tail)


def edges_kernel(sizes, state, edge_one, edge_two):
    parity = lax.rem(lax.axis_index("domain"), 2)

    def load(f, row, count):
        return state[f, pl.ds(row, count), :]

    @pl.when(parity == 0)
    def _():
        north_edge(sizes, load, edge_one, sizes.rows)
        south_edge(sizes, load, edge_two)

    @pl.when(parity == 1)
    def _():
        south_edge(sizes, load, edge_one)
        north_edge(sizes, load, edge_two, sizes.rows)


class Place:
    def __init__(self, chips_a, chips_b):
        self.sizes = (chips_a, chips_b)
        member = lax.axis_index("member")
        self.core = lax.rem(member, 2)
        chip = member // 2
        self.a, self.b = chip // chips_b, lax.rem(chip, chips_b)

    def child(self, hop, core):
        chips_a, chips_b = self.sizes
        a = jnp.where(self.core == 0, lax.rem(self.a + hop, chips_a), self.a)
        b = jnp.where(self.core == 0, self.b, lax.rem(self.b + hop, chips_b))
        return (a * chips_b + b) * 2 + core

    def first_hop(self, parent):
        chips_a, chips_b = self.sizes
        chip = parent // 2
        a, b = chip // chips_b, lax.rem(chip, chips_b)
        return jnp.where(
            self.core == 0,
            lax.rem(self.b - b + chips_b, chips_b),
            lax.rem(self.a - a + chips_a, chips_a),
        )

    def second_hop(self, parent):
        chips_a, chips_b = self.sizes
        chip = parent // 2
        a, b = chip // chips_b, lax.rem(chip, chips_b)
        return jnp.where(
            self.core == 0,
            lax.rem(self.a - a + chips_a, chips_a),
            lax.rem(self.b - b + chips_b, chips_b),
        )


def parent_of(parents, member):
    return jnp.clip(parents[member], 0, parents.shape[0] - 1)


def routes_kernel(chips, hops, parents, out):
    place = Place(*chips)
    tile = 0
    for hop in range(hops):
        for own in (True, False):
            core = place.core if own else 1 - place.core
            parent = parent_of(parents, place.child(hop, core))
            same = jnp.where(lax.rem(parent, 2) == place.core, 0, 1)
            index = 2 * place.first_hop(parent) + same
            out[pl.ds(tile * SUB, SUB), :] = jnp.full((SUB, LANES), index, jnp.int32)
            tile += 1
    for own in (True, False):
        core = place.core if own else 1 - place.core
        index = place.second_hop(parent_of(parents, place.child(0, core)))
        out[pl.ds(tile * SUB, SUB), :] = jnp.full((SUB, LANES), index, jnp.int32)
        tile += 1


def choose(routes, tile, sources, out):
    index = routes[pl.ds(tile * SUB, SUB), :]
    takes = [index == k for k in range(1, len(sources))]
    for row in range(0, out.shape[0], SUB):
        for lane in range(0, out.shape[1], LANES):
            where = (pl.ds(row, SUB), pl.ds(lane, LANES))
            value = sources[0][where]
            for take, source in zip(takes, sources[1:]):
                value = jnp.where(take, source[where], value)
            out[where] = value


def pick_kernel(hops, routes, *refs):
    held, outs = refs[: 2 * hops], refs[-2 * hops :]
    for tile, out in enumerate(outs):
        choose(routes, tile, held, out)


def settle_kernel(sizes, hops, routes, pert, sibling_pert, *refs):
    own_half, sibling_half, own_edge, sibling_edge = refs[-4:]
    core = lax.rem(lax.axis_index("member"), 2)
    for own, out, added in ((0, own_half, pert), (1, sibling_half, sibling_pert)):
        choose(routes, 2 * hops + own, refs[own * hops : (own + 1) * hops], out)
        for f in range(4):
            first = pl.multiple_of(core * sizes.half, SUB)
            at = pl.ds(sizes.half_at(f), sizes.half)
            out[at, :] = out[at, :] + added[f, pl.ds(first, sizes.half), :]
    for half, edge in ((own_half, own_edge), (sibling_half, sibling_edge)):

        def load(f, row, count):
            return half[pl.ds(sizes.half_at(f) + row, count), :]

        @pl.when(core == 0)
        def _():
            south_edge(sizes, load, edge)

        @pl.when(core == 1)
        def _():
            north_edge(sizes, load, edge, sizes.half)


ORIGIN = 16


def put_south(sizes, buf, edge):
    for f in range(4):
        put(buf, f, ORIGIN - sizes.body, sizes.body, edge, sizes.edge_at(f))
        put(buf, f, ORIGIN - REACH, sizes.tail, edge, sizes.tail_at(f))


def put_north(sizes, buf, edge):
    for f in range(4):
        put(buf, f, ORIGIN + sizes.rows, sizes.body, edge, sizes.edge_at(f))
        put(buf, f, ORIGIN + sizes.rows + sizes.body, sizes.tail, edge, sizes.tail_at(f))


def before_kernel(sizes, domains, state, edge_one, edge_two, mine, other, score, *bufs):
    rows, half = sizes.rows, sizes.half
    total_rows = rows * domains
    domain = lax.axis_index("domain")
    parity = lax.rem(domain, 2)
    core = lax.rem(lax.axis_index("member"), 2)
    start = bufs[0]
    chunks = start.shape[1]
    for f in range(4):
        put(start, f, ORIGIN, rows, state.at[f], 0)

    @pl.when(parity == 0)
    def _():
        put_north(sizes, start, edge_one)
        put_south(sizes, start, edge_two)

    @pl.when(parity == 1)
    def _():
        put_south(sizes, start, edge_one)
        put_north(sizes, start, edge_two)

    advance(bufs, ORIGIN, rows, REACH, domain, domains, total_rows)
    for f in range(4):
        for j in range(chunks):
            at = (pl.ds(sizes.half_at(f), half), pl.ds(j * LANES, LANES))
            first = pl.multiple_of(ORIGIN + core * half, SUB)
            mine[at] = start[f, j, pl.ds(first, half), :]
            first = pl.multiple_of(ORIGIN + (1 - core) * half, SUB)
            other[at] = start[f, j, pl.ds(first, half), :]
    sub = lax.broadcasted_iota(jnp.int32, (SUB, LANES), 0)
    total = jnp.zeros((SUB, LANES), jnp.float32)
    for row in range(0, rows, SUB):
        line = jnp.zeros((SUB, LANES), jnp.float32)
        for j in range(chunks):
            q = start[3, j, pl.ds(ORIGIN + row, SUB), :]
            line = line + q * q
        place = (sub + (row + domain * rows)).astype(jnp.float32)
        total = total + (1.0 + 2.0 * place / (total_rows - 1)) * line
    score[...] = total


def after_kernel(
    sizes, domains, own_half, far_half, near_halo, far_halo, score_one, score_two, out, score, *bufs
):
    rows, half = sizes.rows, sizes.half
    total_rows = rows * domains
    domain = lax.axis_index("domain")
    core = lax.rem(lax.axis_index("member"), 2)
    start = bufs[0]
    chunks = start.shape[1]
    score[0, 0] = jnp.sum(score_one[...] + score_two[...]) / (total_rows * out.shape[2])
    for f in range(4):
        at = sizes.half_at(f)
        put(start, f, pl.multiple_of(ORIGIN + core * half, SUB), half, own_half, at)
        put(start, f, pl.multiple_of(ORIGIN + (1 - core) * half, SUB), half, far_half, at)

    @pl.when(core == 0)
    def _():
        put_south(sizes, start, near_halo)
        put_north(sizes, start, far_halo)

    @pl.when(core == 1)
    def _():
        put_south(sizes, start, far_halo)
        put_north(sizes, start, near_halo)

    advance(bufs, ORIGIN, rows, REACH, domain, domains, total_rows)
    for f in range(4):
        for j in range(chunks):
            out[f, :, pl.ds(j * LANES, LANES)] = start[f, j, pl.ds(ORIGIN, rows), :]


def chip_grid(chips):
    b = 1
    while chips % (2 * b) == 0 and (2 * b) * (2 * b) <= chips:
        b *= 2
    return chips // b, b


def on_device(state, perturbation, parents, members, domains):
    state, perturbation = state[0], perturbation[0]
    rows, width = state.shape[1:]
    sizes = Sizes(rows)
    chunks = width // LANES
    chips = chip_grid(members // 2)
    chips_a, chips_b = chips
    hops = max(chips)
    params = pltpu.CompilerParams(vmem_limit_bytes=40 * 2**20)
    half_shape = jax.ShapeDtypeStruct((sizes.half_rows, width), jnp.float32)
    score_shape = jax.ShapeDtypeStruct((SUB, LANES), jnp.float32)
    edge_shape = jax.ShapeDtypeStruct((sizes.edge_rows, width), jnp.float32)

    def member(a, b, core):
        return ((a % chips_a) * chips_b + b % chips_b) * 2 + core

    everywhere = [(a, b) for a in range(chips_a) for b in range(chips_b)]
    sibling = [(i, i ^ 1) for i in range(members)]

    def same_core(first, k):
        pairs = []
        for a, b in everywhere:
            if k < (chips_b if first else chips_a):
                pairs.append((member(a, b, 0), member(a, b + k, 0) if first else member(a + k, b, 0)))
            if k < (chips_a if first else chips_b):
                pairs.append((member(a, b, 1), member(a + k, b, 1) if first else member(a, b + k, 1)))
        return pairs

    def other_core(k):
        pairs = []
        for a, b in everywhere:
            if k < chips_a:
                pairs.append((member(a, b, 0), member(a + k, b, 1)))
            if k < chips_b:
                pairs.append((member(a, b, 1), member(a, b + k, 0)))
        return pairs

    def flat(m, z):
        return m * domains + z

    to_other, to_same = [], []
    for chip in range(members // 2):
        for z in range(1, domains):
            for target, way in ((1, to_other), (0, to_same)):
                way.append((flat(2 * chip, z), flat(2 * chip + target, z - 1)))
            for target, way in ((0, to_other), (1, to_same)):
                way.append((flat(2 * chip + 1, z - 1), flat(2 * chip + target, z)))
    both = ("member", "domain")
    pair_one = [(z, z ^ 1) for z in range(domains) if z ^ 1 < domains]
    pair_two = [(z, ((z + 1) ^ 1) - 1) for z in range(domains) if 0 <= ((z + 1) ^ 1) - 1 < domains]

    def call(kernel, out_shape, in_specs, out_specs, scratch=()):
        return pl.pallas_call(
            kernel,
            out_shape=out_shape,
            in_specs=in_specs,
            out_specs=out_specs,
            scratch_shapes=scratch,
            compiler_params=params,
        )

    bufs = [pltpu.VMEM((4, chunks, rows + 32, LANES), jnp.float32)] * 3
    edge_one, edge_two = call(
        functools.partial(edges_kernel, sizes), (edge_shape,) * 2, [VMEM], (VMEM,) * 2
    )(state)
    edge_one = lax.ppermute(edge_one, "domain", pair_one)
    edge_two = lax.ppermute(edge_two, "domain", pair_two)
    sibling_pert = lax.ppermute(perturbation, "member", sibling)
    routes = call(
        functools.partial(routes_kernel, chips, hops),
        jax.ShapeDtypeStruct(((2 * hops + 2) * SUB, LANES), jnp.int32),
        [SMEM],
        VMEM,
    )(parents)

    mine, other, score = call(
        functools.partial(before_kernel, sizes, domains),
        (half_shape, half_shape, score_shape),
        [VMEM] * 3,
        (VMEM,) * 3,
        bufs,
    )(state, edge_one, edge_two)

    held = [mine, lax.ppermute(other, "member", sibling)]
    for k in range(1, hops):
        held.append(lax.ppermute(mine, "member", same_core(True, k)))
        held.append(lax.ppermute(other, "member", other_core(k)))

    scores = [score, jnp.zeros_like(score)]
    if domains & (domains - 1) == 0:
        bit = 1
        while bit < domains:
            score = scores[0] if bit == 1 else scores[0] + scores[1]
            pairs = [(z, z ^ bit) for z in range(domains)]
            scores = [score, lax.ppermute(score, "domain", pairs)]
            bit *= 2
    else:
        scores[0] = lax.psum(score, "domain")

    picked = call(
        functools.partial(pick_kernel, hops),
        (half_shape,) * (2 * hops),
        [VMEM] * (2 * hops + 2),
        (VMEM,) * (2 * hops),
    )(routes, *held, scores[0])

    own, other = [picked[0]], [picked[1]]
    for k in range(1, hops):
        own.append(lax.ppermute(picked[2 * k], "member", same_core(False, k)))
        other.append(lax.ppermute(picked[2 * k + 1], "member", same_core(False, k)))
    own_half, sibling_half, own_edge, sibling_edge = call(
        functools.partial(settle_kernel, sizes, hops),
        (half_shape, half_shape, edge_shape, edge_shape),
        [VMEM] * (2 * hops + 4),
        (VMEM,) * 4,
    )(routes, perturbation, sibling_pert, *own, *other, scores[1])
    near_halo = lax.ppermute(sibling_edge, both, to_other)
    far_halo = lax.ppermute(own_edge, both, to_same)
    far_half = lax.ppermute(sibling_half, "member", sibling)

    after, score = call(
        functools.partial(after_kernel, sizes, domains),
        (
            jax.ShapeDtypeStruct((4, rows, width), jnp.float32),
            jax.ShapeDtypeStruct((1, 1), jnp.float32),
        ),
        [VMEM] * 6,
        (VMEM, SMEM),
        bufs,
    )(own_half, far_half, near_halo, far_halo, *scores)
    return after[None], jnp.reshape(score, (1,))


def solution(mesh):
    placed = (P("member", None, "domain", None), P("member", None, "domain", None), P())
    return jax.shard_map(
        functools.partial(
            on_device, members=mesh.shape["member"], domains=mesh.shape["domain"]
        ),
        mesh=mesh,
        in_specs=placed,
        out_specs=(P("member", None, "domain", None), P("member")),
        check_vma=False,
    )
```

time: 50.3 us -> 39.5 us (0.79)
  Pallas kernels: 12.4 us -> 7.88 us
  between operations: 2.57 us -> 0.74 us
  starting transfers between devices: 20.8 us -> 19.1 us
  waiting for transfers between devices: 11.8 us -> 10.7 us
  local copies, waits for them, and re-layouts: 1.91 us -> 0.95 us
  other arithmetic: 0.6 us -> 0.01 us
    pallas_call x6, Pallas kernels: 12.4 us -> 7.88 us  [the longest x1 3.86 us: on_device(): call(functools.partial(after_kernel, sizes, domains), (jax.ShapeDtypeStru...]
    ppermute x1, waiting for transfers between devices: 3.63 us -> 0.01 us  [on_device(): held.append(lax.ppermute(mine, 'member', same_core(True, k)))]
    ppermute x1, waiting for transfers between devices: 0.01 us -> 1.78 us  [on_device(): edge_one = lax.ppermute(edge_one, 'domain', pair_one)]
    ppermute x8, waiting for transfers between devices: 7.23 us -> 8.88 us  [the longest x1 6.37 us: on_device(): far_halo = lax.ppermute(own_edge, both, to_same)]
    ppermute x1, starting transfers between devices: 1.46 us -> 0.07 us  [on_device(): far_half = lax.ppermute(sibling_half, 'member', sibling)]
    ppermute x1, waiting for transfers between devices: 0.97 us -> 0.01 us  [on_device(): held.append(lax.ppermute(other, 'member', other_core(k)))]
    unnamed x10 -> x6, local copies, waits for them, and re-layouts: 1.91 us -> 0.95 us
    ppermute x8, starting transfers between devices: 12.6 us -> 13.3 us  [the longest x2 8.73 us: on_device(): scores = [score, lax.ppermute(score, 'domain', pairs)]]
  transfers between devices with their start and end apart: 13 -> 13, of which waited for: 5 -> 4; matrix products, arithmetic and copies ran while one was open for 1% -> 0% of each run, Pallas kernels for 9% -> 2%
where the time goes in v2:
time: 39.5 us; the launch traced here: 39.3 us
  starting transfers between devices  19.1 us (48%)
  waiting for transfers between devices  10.7 us (27%)
  Pallas kernels  7.88 us (20%)
  local copies, waits for them, and re-layouts  0.95 us (2%)
  between operations  0.74 us (2%)
    ppermute x2, starting transfers between devices, on_device(): scores = [score, lax.ppermute(score, 'domain', pairs)]  8.73 us
    ppermute x1, waiting for transfers between devices, on_device(): far_halo = lax.ppermute(own_edge, both, to_same)  6.37 us
    pallas_call x1, Pallas kernels, on_device(): call(functools.partial(after_kernel, sizes, domains), (jax.ShapeDtypeStru...  3.86 us
    pallas_call x1, Pallas kernels, on_device(): call(functools.partial(before_kernel, sizes, domains), (half_shape, half_...  3.13 us
    ppermute x1, starting transfers between devices, on_device(): edge_one = lax.ppermute(edge_one, 'domain', pair_one)  3.08 us
    ppermute x2, waiting for transfers between devices, on_device(): scores = [score, lax.ppermute(score, 'domain', pairs)]  2.5 us
    ppermute x1, starting transfers between devices, on_device(): held.append(lax.ppermute(mine, 'member', same_core(True, k)))  1.98 us
    ppermute x1, waiting for transfers between devices, on_device(): edge_one = lax.ppermute(edge_one, 'domain', pair_one)  1.78 us
  transfers between devices with their start and end apart: 13, of which 4 were waited for; matrix products, arithmetic and copies ran while one was open for 0% of the time, Pallas kernels for 2%

profile of v2, /device:TPU:0, one launch (start us, length us, event | category | flops | bytes accessed | tf_op | source)
XLA Modules:
  0.0 39.3 jit_solution(8927924543108511359)
XLA Ops:
  0.6 0.0 copy-start
  0.6 0.9 %copy-done = f32[1,4,32,512]{3,2,1,0:T(8,128)S(1)} copy-done((f32[1,4,32,512]{3,2,1,0:T(8,128)S(1)}, f32[1,4,32,512]{3,2,1,0:T(8,128)}, u32[]{:S(2)}) %copy-start) | copy-done | bytes 262168
  1.6 0.0 copy-start.1
  1.6 3.1 %collective-permute-start.1 = (f32[40,512]{1,0:T(8,128)S(1)}, f32[40,512]{1,0:T(8,128)S(1)}, u32[]{:S(2)}, u32[]{:S(2)}) collective-permute-start(f32[40,512]{1,0:T(8,128)S(1)} %get-tuple-element.17), channel_id=1, source_target_pairs={{0,1},{1,0},{2,3},{3,2},{4,5},{5,4},{6,7},{7,6},{8,9},{9,8},{10,11... | collective-permute-start | bytes 245768 | tf_op jit(solution)/shard_map/ppermute | solution.py:402
  4.7 0.7 %collective-permute-start.2 = (f32[40,512]{1,0:T(8,128)S(1)}, f32[40,512]{1,0:T(8,128)S(1)}, u32[]{:S(2)}, u32[]{:S(2)}) collective-permute-start(f32[40,512]{1,0:T(8,128)S(1)} %get-tuple-element.18), channel_id=1, source_target_pairs={{1,2},{2,1},{5,6},{6,5},{9,10},{10,9},{13,14},{14,13},{17,18},{18,... | collective-permute-start | bytes 245768 | tf_op jit(solution)/shard_map/ppermute | solution.py:403
  5.4 1.8 %collective-permute-done.1.edge_one = f32[40,512]{1,0:T(8,128)S(1)} collective-permute-done((f32[40,512]{1,0:T(8,128)S(1)}, f32[40,512]{1,0:T(8,128)S(1)}, u32[]{:S(2)}, u32[]{:S(2)}) %collective-permute-start.1) | collective-permute-done | bytes 81952 | tf_op jit(solution)/shard_map/ppermute | solution.py:402
  7.1 0.0 collective-permute-done.2.edge_two
  7.1 3.1 %shard_map.52 = (f32[64,512]{1,0:T(8,128)S(1)}, f32[64,512]{1,0:T(8,128)S(1)}, f32[8,128]{1,0:T(8,128)S(1)}) custom-call(f32[4,32,512]{2,1,0:T(8,128)S(1)} %bitcast.5, f32[40,512]{1,0:T(8,128)S(1)} %collective-permute-done.1.edge_one, f32[40,512]{1,0:T(8,128)S(1)} %collective-permute-done.2.edge_two), custom_call_target="tpu_custom_call" | custom-call | tf_op jit(solution)/shard_map/pallas_call | solution.py:412
  10.3 2.0 %collective-permute-start.4 = (f32[64,512]{1,0:T(8,128)S(1)}, f32[64,512]{1,0:T(8,128)S(1)}, u32[]{:S(2)}, u32[]{:S(2)}) collective-permute-start(f32[64,512]{1,0:T(8,128)S(1)} %get-tuple-element.19.refs_0_), channel_id=1, source_target_pairs={{0,8},{4,20},{8,0},{12,28},{16,24},{20,4},{24,16},{28,12},{1,9},{5... | collective-permute-start | bytes 393224 | tf_op jit(solution)/shard_map/ppermute | solution.py:422
  12.3 0.0 collective-permute-start.5
  12.3 0.2 collective-permute-start.3
  12.5 0.0 copy-done.1
  12.5 0.0 copy-start.2
  12.5 0.3 collective-permute-start
  12.8 4.7 %collective-permute-start.6 = (f32[8,128]{1,0:T(8,128)S(1)}, f32[8,128]{1,0:T(8,128)S(1)}, u32[]{:S(2)}, u32[]{:S(2)}) collective-permute-start(f32[8,128]{1,0:T(8,128)S(1)} %get-tuple-element.21), channel_id=1, source_target_pairs={{0,1},{1,0},{2,3},{3,2},{4,5},{5,4},{6,7},{7,6},{8,9},{9,8},{10,11... | collective-permute-start | bytes 12296 | tf_op jit(solution)/shard_map/ppermute | solution.py:431
  17.5 0.0 copy-done.2
  17.5 0.7 %shard_map.50.routes = s32[48,128]{1,0:T(8,128)S(1)} custom-call(s32[8]{0:T(128)S(1)} %copy-done.2), custom_call_target="tpu_custom_call" | custom-call | tf_op jit(solution)/shard_map/pallas_call | solution.py:405
  18.2 0.9 %collective-permute-done.6 = f32[8,128]{1,0:T(8,128)S(1)} collective-permute-done((f32[8,128]{1,0:T(8,128)S(1)}, f32[8,128]{1,0:T(8,128)S(1)}, u32[]{:S(2)}, u32[]{:S(2)}) %collective-permute-start.6) | collective-permute-done | bytes 4128 | tf_op jit(solution)/shard_map/ppermute | solution.py:431
  19.1 0.0 collective-permute-done.4.refs_2_
  19.1 0.0 collective-permute-done.5.refs_3_
  19.1 0.0 collective-permute-done.3.refs_1_
  19.1 0.1 shard_map.53
  19.2 1.6 %collective-permute-start.7 = (f32[64,512]{1,0:T(8,128)S(1)}, f32[64,512]{1,0:T(8,128)S(1)}, u32[]{:S(2)}, u32[]{:S(2)}) collective-permute-start(f32[64,512]{1,0:T(8,128)S(1)} %get-tuple-element.23), channel_id=1, source_target_pairs={{0,16},{4,12},{8,24},{12,4},{16,0},{20,28},{24,8},{28,20},{1,17},{... | collective-permute-start | bytes 393224 | tf_op jit(solution)/shard_map/ppermute | solution.py:445
  20.8 0.5 %collective-permute-start.8 = (f32[64,512]{1,0:T(8,128)S(1)}, f32[64,512]{1,0:T(8,128)S(1)}, u32[]{:S(2)}, u32[]{:S(2)}) collective-permute-start(f32[64,512]{1,0:T(8,128)S(1)} %get-tuple-element.25), channel_id=1, source_target_pairs={{0,16},{4,12},{8,24},{12,4},{16,0},{20,28},{24,8},{28,20},{1,17},{... | collective-permute-start | bytes 393224 | tf_op jit(solution)/shard_map/ppermute | solution.py:446
  21.3 4.0 %collective-permute-start.9 = (f32[8,128]{1,0:T(8,128)S(1)}, f32[8,128]{1,0:T(8,128)S(1)}, u32[]{:S(2)}, u32[]{:S(2)}) collective-permute-start(f32[8,128]{1,0:T(8,128)S(1)} %add.3.refs_4_.score_one), channel_id=1, source_target_pairs={{0,2},{1,3},{2,0},{3,1},{4,6},{5,7},{6,4},{7,5},{8,10},{9,11},{10,... | collective-permute-start | bytes 12296 | tf_op jit(solution)/shard_map/ppermute | solution.py:431
  25.3 1.6 %collective-permute-done.9.refs_4_.score_two = f32[8,128]{1,0:T(8,128)S(1)} collective-permute-done((f32[8,128]{1,0:T(8,128)S(1)}, f32[8,128]{1,0:T(8,128)S(1)}, u32[]{:S(2)}, u32[]{:S(2)}) %collective-permute-start.9) | collective-permute-done | bytes 4128 | tf_op jit(solution)/shard_map/ppermute | solution.py:431
  26.9 0.0 collective-permute-done.sibling_pert
  26.9 0.0 collective-permute-done.7.refs_1_
  26.9 0.0 collective-permute-done.8.refs_3_
  26.9 0.1 shard_map.54
  27.0 0.1 collective-permute-start.10
  27.1 0.7 %collective-permute-start.11 = (f32[40,512]{1,0:T(8,128)S(1)}, f32[40,512]{1,0:T(8,128)S(1)}, u32[]{:S(2)}, u32[]{:S(2)}) collective-permute-start(f32[40,512]{1,0:T(8,128)S(1)} %get-tuple-element.28), channel_id=1, source_target_pairs={{1,4},{4,1},{2,5},{5,2},{3,6},{6,3},{9,12},{12,9},{10,13},{13,10},... | collective-permute-start | bytes 245768 | tf_op jit(solution)/shard_map/ppermute | solution.py:453
  27.8 1.3 %collective-permute-start.12 = (f32[40,512]{1,0:T(8,128)S(1)}, f32[40,512]{1,0:T(8,128)S(1)}, u32[]{:S(2)}, u32[]{:S(2)}) collective-permute-start(f32[40,512]{1,0:T(8,128)S(1)} %get-tuple-element.29), channel_id=1, source_target_pairs={{1,0},{4,5},{2,1},{5,6},{3,2},{6,7},{9,8},{12,13},{10,9},{13,14},{... | collective-permute-start | bytes 245768 | tf_op jit(solution)/shard_map/ppermute | solution.py:454
  29.1 0.0 collective-permute-done.11.near_halo
  29.1 6.4 %collective-permute-done.12.far_halo = f32[40,512]{1,0:T(8,128)S(1)} collective-permute-done((f32[40,512]{1,0:T(8,128)S(1)}, f32[40,512]{1,0:T(8,128)S(1)}, u32[]{:S(2)}, u32[]{:S(2)}) %collective-permute-start.12) | collective-permute-done | bytes 81952 | tf_op jit(solution)/shard_map/ppermute | solution.py:454
  35.5 0.0 collective-permute-done.10.far_half
  35.5 3.9 %shard_map.55 = (f32[4,32,512]{2,1,0:T(8,128)}, f32[1,1]{1,0:T(1,128)}) custom-call(f32[64,512]{1,0:T(8,128)S(1)} %get-tuple-element.26.own_half, f32[64,512]{1,0:T(8,128)S(1)} %collective-permute-done.10.far_half, f32[40,512]{1,0:T(8,128)S(1)} %collective-permute-done.11.near_halo, f32[40,512]{1,0:T(8,128)S(1)} %collective-permute-done.12.far_halo, ...), custom_call_target="tpu_custom_call" | custom-call | tf_op jit(solution)/shard_map/pallas_call | solution.py:457
  (2 shorter events, 0.0 us)
Async XLA Ops:
  0.6 1.0 %copy-start = (f32[1,4,32,512]{3,2,1,0:T(8,128)S(1)}, f32[1,4,32,512]{3,2,1,0:T(8,128)}, u32[]{:S(2)}) copy-start(f32[1,4,32,512]{3,2,1,0:T(8,128)} %param.3) | copy-start | bytes 786436
  1.6 10.9 %copy-start.1 = (f32[1,4,32,512]{3,2,1,0:T(8,128)S(1)}, f32[1,4,32,512]{3,2,1,0:T(8,128)}, u32[]{:S(2)}) copy-start(f32[1,4,32,512]{3,2,1,0:T(8,128)} %param.4) | copy-start | bytes 786436
  1.6 5.5 %collective-permute-start.1 = (f32[40,512]{1,0:T(8,128)S(1)}, f32[40,512]{1,0:T(8,128)S(1)}, u32[]{:S(2)}, u32[]{:S(2)}) collective-permute-start(f32[40,512]{1,0:T(8,128)S(1)} %get-tuple-element.17), channel_id=1, source_target_pairs={{0,1},{1,0},{2,3},{3,2},{4,5},{5,4},{6,7},{7,6},{8,9},{9,8},{10,11... | collective-permute-start | bytes 245768 | tf_op jit(solution)/shard_map/ppermute | solution.py:402
  4.7 2.4 %collective-permute-start.2 = (f32[40,512]{1,0:T(8,128)S(1)}, f32[40,512]{1,0:T(8,128)S(1)}, u32[]{:S(2)}, u32[]{:S(2)}) collective-permute-start(f32[40,512]{1,0:T(8,128)S(1)} %get-tuple-element.18), channel_id=1, source_target_pairs={{1,2},{2,1},{5,6},{6,5},{9,10},{10,9},{13,14},{14,13},{17,18},{18,... | collective-permute-start | bytes 245768 | tf_op jit(solution)/shard_map/ppermute | solution.py:403
  10.3 8.8 %collective-permute-start.4 = (f32[64,512]{1,0:T(8,128)S(1)}, f32[64,512]{1,0:T(8,128)S(1)}, u32[]{:S(2)}, u32[]{:S(2)}) collective-permute-start(f32[64,512]{1,0:T(8,128)S(1)} %get-tuple-element.19.refs_0_), channel_id=1, source_target_pairs={{0,8},{4,20},{8,0},{12,28},{16,24},{20,4},{24,16},{28,12},{1,9},{5... | collective-permute-start | bytes 393224 | tf_op jit(solution)/shard_map/ppermute | solution.py:422
  12.3 6.8 %collective-permute-start.5 = (f32[64,512]{1,0:T(8,128)S(1)}, f32[64,512]{1,0:T(8,128)S(1)}, u32[]{:S(2)}, u32[]{:S(2)}) collective-permute-start(f32[64,512]{1,0:T(8,128)S(1)} %get-tuple-element.20), channel_id=1, source_target_pairs={{0,20},{4,8},{8,28},{12,0},{16,4},{20,24},{24,12},{28,16},{1,21},{... | collective-permute-start | bytes 393224 | tf_op jit(solution)/shard_map/ppermute | solution.py:423
  12.3 6.8 %collective-permute-start.3 = (f32[64,512]{1,0:T(8,128)S(1)}, f32[64,512]{1,0:T(8,128)S(1)}, u32[]{:S(2)}, u32[]{:S(2)}) collective-permute-start(f32[64,512]{1,0:T(8,128)S(1)} %get-tuple-element.20), channel_id=1, source_target_pairs={{0,4},{4,0},{8,12},{12,8},{16,20},{20,16},{24,28},{28,24},{1,5},{5... | collective-permute-start | bytes 393224 | tf_op jit(solution)/shard_map/ppermute | solution.py:420
  12.5 5.0 %copy-start.2 = (s32[8]{0:T(128)S(1)}, s32[8]{0:T(128)}, u32[]{:S(2)}) copy-start(s32[8]{0:T(128)} %parents.1) | copy-start | bytes 100
  12.5 14.4 %collective-permute-start = (f32[4,32,512]{2,1,0:T(8,128)S(1)}, f32[4,32,512]{2,1,0:T(8,128)S(1)}, u32[]{:S(2)}, u32[]{:S(2)}) collective-permute-start(f32[4,32,512]{2,1,0:T(8,128)S(1)} %bitcast.6), channel_id=1, source_target_pairs={{0,4},{4,0},{8,12},{12,8},{16,20},{20,16},{24,28},{28,24},{1,5},{5... | collective-permute-start | bytes 786440 | tf_op jit(solution)/shard_map/ppermute | solution.py:404
  12.8 6.3 %collective-permute-start.6 = (f32[8,128]{1,0:T(8,128)S(1)}, f32[8,128]{1,0:T(8,128)S(1)}, u32[]{:S(2)}, u32[]{:S(2)}) collective-permute-start(f32[8,128]{1,0:T(8,128)S(1)} %get-tuple-element.21), channel_id=1, source_target_pairs={{0,1},{1,0},{2,3},{3,2},{4,5},{5,4},{6,7},{7,6},{8,9},{9,8},{10,11... | collective-permute-start | bytes 12296 | tf_op jit(solution)/shard_map/ppermute | solution.py:431
  19.2 7.7 %collective-permute-start.7 = (f32[64,512]{1,0:T(8,128)S(1)}, f32[64,512]{1,0:T(8,128)S(1)}, u32[]{:S(2)}, u32[]{:S(2)}) collective-permute-start(f32[64,512]{1,0:T(8,128)S(1)} %get-tuple-element.23), channel_id=1, source_target_pairs={{0,16},{4,12},{8,24},{12,4},{16,0},{20,28},{24,8},{28,20},{1,17},{... | collective-permute-start | bytes 393224 | tf_op jit(solution)/shard_map/ppermute | solution.py:445
  20.8 6.1 %collective-permute-start.8 = (f32[64,512]{1,0:T(8,128)S(1)}, f32[64,512]{1,0:T(8,128)S(1)}, u32[]{:S(2)}, u32[]{:S(2)}) collective-permute-start(f32[64,512]{1,0:T(8,128)S(1)} %get-tuple-element.25), channel_id=1, source_target_pairs={{0,16},{4,12},{8,24},{12,4},{16,0},{20,28},{24,8},{28,20},{1,17},{... | collective-permute-start | bytes 393224 | tf_op jit(solution)/shard_map/ppermute | solution.py:446
  21.3 5.6 %collective-permute-start.9 = (f32[8,128]{1,0:T(8,128)S(1)}, f32[8,128]{1,0:T(8,128)S(1)}, u32[]{:S(2)}, u32[]{:S(2)}) collective-permute-start(f32[8,128]{1,0:T(8,128)S(1)} %add.3.refs_4_.score_one), channel_id=1, source_target_pairs={{0,2},{1,3},{2,0},{3,1},{4,6},{5,7},{6,4},{7,5},{8,10},{9,11},{10,... | collective-permute-start | bytes 12296 | tf_op jit(solution)/shard_map/ppermute | solution.py:431
  27.0 8.4 %collective-permute-start.10 = (f32[64,512]{1,0:T(8,128)S(1)}, f32[64,512]{1,0:T(8,128)S(1)}, u32[]{:S(2)}, u32[]{:S(2)}) collective-permute-start(f32[64,512]{1,0:T(8,128)S(1)} %get-tuple-element.27), channel_id=1, source_target_pairs={{0,4},{4,0},{8,12},{12,8},{16,20},{20,16},{24,28},{28,24},{1,5},{5... | collective-permute-start | bytes 393224 | tf_op jit(solution)/shard_map/ppermute | solution.py:455
  27.1 2.0 %collective-permute-start.11 = (f32[40,512]{1,0:T(8,128)S(1)}, f32[40,512]{1,0:T(8,128)S(1)}, u32[]{:S(2)}, u32[]{:S(2)}) collective-permute-start(f32[40,512]{1,0:T(8,128)S(1)} %get-tuple-element.28), channel_id=1, source_target_pairs={{1,4},{4,1},{2,5},{5,2},{3,6},{6,3},{9,12},{12,9},{10,13},{13,10},... | collective-permute-start | bytes 245768 | tf_op jit(solution)/shard_map/ppermute | solution.py:453
  27.8 7.7 %collective-permute-start.12 = (f32[40,512]{1,0:T(8,128)S(1)}, f32[40,512]{1,0:T(8,128)S(1)}, u32[]{:S(2)}, u32[]{:S(2)}) collective-permute-start(f32[40,512]{1,0:T(8,128)S(1)} %get-tuple-element.29), channel_id=1, source_target_pairs={{1,0},{4,5},{2,1},{5,6},{3,2},{6,7},{9,8},{12,13},{10,9},{13,14},{... | collective-permute-start | bytes 245768 | tf_op jit(solution)/shard_map/ppermute | solution.py:454

commit v3 on v2

--- a/solution.py
+++ b/solution.py
@@ -68,6 +68,18 @@
 def advance(bufs, origin, rows, reach, domain, domains, total_rows):
     state, one, two = bufs
     global_row = domain * rows - origin
+    blank = jnp.zeros(state.shape[:2] + (1, LANES), jnp.float32)
+
+    def blank_outside(buf):
+        @pl.when(domain == 0)
+        def _():
+            buf[:, :, pl.ds(origin - 1, 1), :] = blank
+
+        @pl.when(domain == domains - 1)
+        def _():
+            buf[:, :, pl.ds(origin + rows, 1), :] = blank
+
+    blank_outside(state)
     thirds = ((state, one, 0.0, 1.0), (one, two, 0.75, 0.25), (two, state, 1.0 / 3.0, 2.0 / 3.0))
     for _ in range(STEPS):
         for src, dst, keep, gain in thirds:
@@ -75,15 +87,7 @@
             first, count = origin - reach, rows + 2 * reach
             stage(src, state, dst, first, count, keep, gain, global_row, total_rows)
             if reach > 0:
-                blank = jnp.zeros(dst.shape[:2] + (1, LANES), jnp.float32)
-
-                @pl.when(domain == 0)
-                def _():
-                    dst[:, :, pl.ds(origin - 1, 1), :] = blank
-
-                @pl.when(domain == domains - 1)
-                def _():
-                    dst[:, :, pl.ds(origin + rows, 1), :] = blank
+                blank_outside(dst)
 
 
 def put(buf, field, row, count, block, row_from, add=False):
@@ -374,16 +378,31 @@
     def flat(m, z):
         return m * domains + z
 
+    levels = range(domains)
+    near = members // 2 % 2 == 0
+
+    def matched(partner):
+        return [
+            (flat(m, z), flat(m, partner(z)) if 0 <= partner(z) < domains else flat(m ^ 1, z))
+            for m in range(members)
+            for z in levels
+        ]
+
+    pair_one = matched(lambda z: z ^ 1)
+    pair_two = matched(lambda z: ((z + 1) ^ 1) - 1)
     to_other, to_same = [], []
-    for chip in range(members // 2):
-        for z in range(1, domains):
-            for target, way in ((1, to_other), (0, to_same)):
-                way.append((flat(2 * chip, z), flat(2 * chip + target, z - 1)))
-            for target, way in ((0, to_other), (1, to_same)):
-                way.append((flat(2 * chip + 1, z - 1), flat(2 * chip + target, z)))
+    for m in range(members):
+        core = m % 2
+        for z in levels:
+            level = z + 1 if core else z - 1
+            if 0 <= level < domains:
+                to_other.append((flat(m, z), flat(m ^ 1, level)))
+                to_same.append((flat(m, z), flat(m, level)))
+            else:
+                if near:
+                    to_other.append((flat(m, z), flat(m ^ 2, z)))
+                to_same.append((flat(m, z), flat(m ^ 1, z)))
     both = ("member", "domain")
-    pair_one = [(z, z ^ 1) for z in range(domains) if z ^ 1 < domains]
-    pair_two = [(z, ((z + 1) ^ 1) - 1) for z in range(domains) if 0 <= ((z + 1) ^ 1) - 1 < domains]
 
     def call(kernel, out_shape, in_specs, out_specs, scratch=()):
         return pl.pallas_call(
@@ -399,8 +418,8 @@
     edge_one, edge_two = call(
         functools.partial(edges_kernel, sizes), (edge_shape,) * 2, [VMEM], (VMEM,) * 2
     )(state)
-    edge_one = lax.ppermute(edge_one, "domain", pair_one)
-    edge_two = lax.ppermute(edge_two, "domain", pair_two)
+    edge_one = lax.ppermute(edge_one, both, pair_one)
+    edge_two = lax.ppermute(edge_two, both, pair_two)
     sibling_pert = lax.ppermute(perturbation, "member", sibling)
     routes = call(
         functools.partial(routes_kernel, chips, hops),

time: 39.5 us -> 35.2 us (0.89)
  starting transfers between devices: 19.1 us -> 16.2 us
  waiting for transfers between devices: 10.7 us -> 9.28 us
    ppermute x1, waiting for transfers between devices: 6.37 us -> 1.46 us  [on_device(): far_halo = lax.ppermute(own_edge, both, to_same)]
    ppermute x1, waiting for transfers between devices: 0.01 us -> 2.87 us  [on_device(): near_halo = lax.ppermute(sibling_edge, both, to_other)]
    ppermute x2, starting transfers between devices: 8.73 us -> 6.84 us  [on_device(): scores = [score, lax.ppermute(score, 'domain', pairs)]]
    ppermute x1, starting transfers between devices: 1.29 us -> 0.12 us  [on_device(): far_halo = lax.ppermute(own_edge, both, to_same)]
    ppermute x1, starting transfers between devices: 0.67 us -> 1.52 us  [on_device(): near_halo = lax.ppermute(sibling_edge, both, to_other)]
    ppermute x2, waiting for transfers between devices: 1.78 us -> 2.44 us  [the longest x1 2.44 us: on_device(): edge_one = lax.ppermute(edge_one, both, pair_one)]
    ppermute x2, starting transfers between devices: 3.74 us -> 3.09 us  [the longest x1 3.08 us: on_device(): edge_one = lax.ppermute(edge_one, both, pair_one)]
  transfers between devices with their start and end apart: 13 -> 13, of which waited for: 4 -> 5; matrix products, arithmetic and copies ran while one was open for 0% -> 0% of each run, Pallas kernels for 2% -> 2%
where the time goes in v3:
time: 35.2 us; the launch traced here: 35.1 us
  starting transfers between devices  16.2 us (46%)
  waiting for transfers between devices  9.28 us (26%)
  Pallas kernels  7.9 us (22%)
  local copies, waits for them, and re-layouts  0.95 us (3%)
  between operations  0.71 us (2%)
    ppermute x2, starting transfers between devices, on_device(): scores = [score, lax.ppermute(score, 'domain', pairs)]  6.84 us
    pallas_call x1, Pallas kernels, on_device(): call(functools.partial(after_kernel, sizes, domains), (jax.ShapeDtypeStru...  3.88 us
    pallas_call x1, Pallas kernels, on_device(): call(functools.partial(before_kernel, sizes, domains), (half_shape, half_...  3.14 us
    ppermute x1, starting transfers between devices, on_device(): edge_one = lax.ppermute(edge_one, both, pair_one)  3.08 us
    ppermute x1, waiting for transfers between devices, on_device(): near_halo = lax.ppermute(sibling_edge, both, to_other)  2.87 us
    ppermute x2, waiting for transfers between devices, on_device(): scores = [score, lax.ppermute(score, 'domain', pairs)]  2.5 us
    ppermute x1, waiting for transfers between devices, on_device(): edge_one = lax.ppermute(edge_one, both, pair_one)  2.44 us
    ppermute x1, starting transfers between devices, on_device(): held.append(lax.ppermute(mine, 'member', same_core(True, k)))  1.98 us
  transfers between devices with their start and end apart: 13, of which 5 were waited for; matrix products, arithmetic and copies ran while one was open for 0% of the time, Pallas kernels for 2%

profile of v3, /device:TPU:0, one launch (start us, length us, event | category | flops | bytes accessed | tf_op | source)
XLA Modules:
  0.0 35.1 jit_solution(6572676071206060827)
XLA Ops:
  0.6 0.0 copy-start
  0.6 0.9 %copy-done = f32[1,4,32,512]{3,2,1,0:T(8,128)S(1)} copy-done((f32[1,4,32,512]{3,2,1,0:T(8,128)S(1)}, f32[1,4,32,512]{3,2,1,0:T(8,128)}, u32[]{:S(2)}) %copy-start) | copy-done | bytes 262168
  1.6 0.0 copy-start.1
  1.6 3.1 %collective-permute-start.1 = (f32[40,512]{1,0:T(8,128)S(1)}, f32[40,512]{1,0:T(8,128)S(1)}, u32[]{:S(2)}, u32[]{:S(2)}) collective-permute-start(f32[40,512]{1,0:T(8,128)S(1)} %get-tuple-element.17), channel_id=1, source_target_pairs={{0,1},{1,0},{2,3},{3,2},{4,5},{5,4},{6,7},{7,6},{8,9},{9,8},{10,11... | collective-permute-start | bytes 245768 | tf_op jit(solution)/shard_map/ppermute | solution.py:421
  4.7 0.0 collective-permute-start.2
  4.7 2.4 %collective-permute-done.1.edge_one = f32[40,512]{1,0:T(8,128)S(1)} collective-permute-done((f32[40,512]{1,0:T(8,128)S(1)}, f32[40,512]{1,0:T(8,128)S(1)}, u32[]{:S(2)}, u32[]{:S(2)}) %collective-permute-start.1) | collective-permute-done | bytes 81952 | tf_op jit(solution)/shard_map/ppermute | solution.py:421
  7.1 0.0 collective-permute-done.2.edge_two
  7.1 3.1 %shard_map.52 = (f32[64,512]{1,0:T(8,128)S(1)}, f32[64,512]{1,0:T(8,128)S(1)}, f32[8,128]{1,0:T(8,128)S(1)}) custom-call(f32[4,32,512]{2,1,0:T(8,128)S(1)} %bitcast.5, f32[40,512]{1,0:T(8,128)S(1)} %collective-permute-done.1.edge_one, f32[40,512]{1,0:T(8,128)S(1)} %collective-permute-done.2.edge_two), custom_call_target="tpu_custom_call" | custom-call | tf_op jit(solution)/shard_map/pallas_call | solution.py:431
  10.3 2.0 %collective-permute-start.4 = (f32[64,512]{1,0:T(8,128)S(1)}, f32[64,512]{1,0:T(8,128)S(1)}, u32[]{:S(2)}, u32[]{:S(2)}) collective-permute-start(f32[64,512]{1,0:T(8,128)S(1)} %get-tuple-element.19.refs_0_), channel_id=1, source_target_pairs={{0,8},{4,20},{8,0},{12,28},{16,24},{20,4},{24,16},{28,12},{1,9},{5... | collective-permute-start | bytes 393224 | tf_op jit(solution)/shard_map/ppermute | solution.py:441
  12.3 0.0 collective-permute-start.5
  12.3 0.2 collective-permute-start.3
  12.5 0.0 copy-done.1
  12.5 0.0 copy-start.2
  12.5 0.3 collective-permute-start
  12.8 2.8 %collective-permute-start.6 = (f32[8,128]{1,0:T(8,128)S(1)}, f32[8,128]{1,0:T(8,128)S(1)}, u32[]{:S(2)}, u32[]{:S(2)}) collective-permute-start(f32[8,128]{1,0:T(8,128)S(1)} %get-tuple-element.21), channel_id=1, source_target_pairs={{0,1},{1,0},{2,3},{3,2},{4,5},{5,4},{6,7},{7,6},{8,9},{9,8},{10,11... | collective-permute-start | bytes 12296 | tf_op jit(solution)/shard_map/ppermute | solution.py:450
  15.6 0.0 copy-done.2
  15.6 0.7 %shard_map.50.routes = s32[48,128]{1,0:T(8,128)S(1)} custom-call(s32[8]{0:T(128)S(1)} %copy-done.2), custom_call_target="tpu_custom_call" | custom-call | tf_op jit(solution)/shard_map/pallas_call | solution.py:424
  16.3 0.9 %collective-permute-done.6 = f32[8,128]{1,0:T(8,128)S(1)} collective-permute-done((f32[8,128]{1,0:T(8,128)S(1)}, f32[8,128]{1,0:T(8,128)S(1)}, u32[]{:S(2)}, u32[]{:S(2)}) %collective-permute-start.6) | collective-permute-done | bytes 4128 | tf_op jit(solution)/shard_map/ppermute | solution.py:450
  17.2 0.0 collective-permute-done.4.refs_2_
  17.2 0.0 collective-permute-done.5.refs_3_
  17.2 0.0 collective-permute-done.3.refs_1_
  17.2 0.1 shard_map.53
  17.4 1.6 %collective-permute-start.7 = (f32[64,512]{1,0:T(8,128)S(1)}, f32[64,512]{1,0:T(8,128)S(1)}, u32[]{:S(2)}, u32[]{:S(2)}) collective-permute-start(f32[64,512]{1,0:T(8,128)S(1)} %get-tuple-element.23), channel_id=1, source_target_pairs={{0,16},{4,12},{8,24},{12,4},{16,0},{20,28},{24,8},{28,20},{1,17},{... | collective-permute-start | bytes 393224 | tf_op jit(solution)/shard_map/ppermute | solution.py:464
  18.9 0.5 %collective-permute-start.8 = (f32[64,512]{1,0:T(8,128)S(1)}, f32[64,512]{1,0:T(8,128)S(1)}, u32[]{:S(2)}, u32[]{:S(2)}) collective-permute-start(f32[64,512]{1,0:T(8,128)S(1)} %get-tuple-element.25), channel_id=1, source_target_pairs={{0,16},{4,12},{8,24},{12,4},{16,0},{20,28},{24,8},{28,20},{1,17},{... | collective-permute-start | bytes 393224 | tf_op jit(solution)/shard_map/ppermute | solution.py:465
  19.5 4.0 %collective-permute-start.9 = (f32[8,128]{1,0:T(8,128)S(1)}, f32[8,128]{1,0:T(8,128)S(1)}, u32[]{:S(2)}, u32[]{:S(2)}) collective-permute-start(f32[8,128]{1,0:T(8,128)S(1)} %add.3.refs_4_.score_one), channel_id=1, source_target_pairs={{0,2},{1,3},{2,0},{3,1},{4,6},{5,7},{6,4},{7,5},{8,10},{9,11},{10,... | collective-permute-start | bytes 12296 | tf_op jit(solution)/shard_map/ppermute | solution.py:450
  23.5 1.6 %collective-permute-done.9.refs_4_.score_two = f32[8,128]{1,0:T(8,128)S(1)} collective-permute-done((f32[8,128]{1,0:T(8,128)S(1)}, f32[8,128]{1,0:T(8,128)S(1)}, u32[]{:S(2)}, u32[]{:S(2)}) %collective-permute-start.9) | collective-permute-done | bytes 4128 | tf_op jit(solution)/shard_map/ppermute | solution.py:450
  25.1 0.0 collective-permute-done.sibling_pert
  25.1 0.0 collective-permute-done.7.refs_1_
  25.1 0.0 collective-permute-done.8.refs_3_
  25.1 0.1 shard_map.54
  25.2 0.1 collective-permute-start.10
  25.2 1.5 %collective-permute-start.11 = (f32[40,512]{1,0:T(8,128)S(1)}, f32[40,512]{1,0:T(8,128)S(1)}, u32[]{:S(2)}, u32[]{:S(2)}) collective-permute-start(f32[40,512]{1,0:T(8,128)S(1)} %get-tuple-element.28), channel_id=1, source_target_pairs={{0,8},{1,4},{2,5},{3,6},{4,1},{5,2},{6,3},{7,15},{8,0},{9,12},{10,... | collective-permute-start | bytes 245768 | tf_op jit(solution)/shard_map/ppermute | solution.py:472
  26.8 0.1 collective-permute-start.12
  26.9 2.9 %collective-permute-done.11.near_halo = f32[40,512]{1,0:T(8,128)S(1)} collective-permute-done((f32[40,512]{1,0:T(8,128)S(1)}, f32[40,512]{1,0:T(8,128)S(1)}, u32[]{:S(2)}, u32[]{:S(2)}) %collective-permute-start.11) | collective-permute-done | bytes 81952 | tf_op jit(solution)/shard_map/ppermute | solution.py:472
  29.7 1.5 %collective-permute-done.12.far_halo = f32[40,512]{1,0:T(8,128)S(1)} collective-permute-done((f32[40,512]{1,0:T(8,128)S(1)}, f32[40,512]{1,0:T(8,128)S(1)}, u32[]{:S(2)}, u32[]{:S(2)}) %collective-permute-start.12) | collective-permute-done | bytes 81952 | tf_op jit(solution)/shard_map/ppermute | solution.py:473
  31.2 0.0 collective-permute-done.10.far_half
  31.2 3.9 %shard_map.55 = (f32[4,32,512]{2,1,0:T(8,128)}, f32[1,1]{1,0:T(1,128)}) custom-call(f32[64,512]{1,0:T(8,128)S(1)} %get-tuple-element.26.own_half, f32[64,512]{1,0:T(8,128)S(1)} %collective-permute-done.10.far_half, f32[40,512]{1,0:T(8,128)S(1)} %collective-permute-done.11.near_halo, f32[40,512]{1,0:T(8,128)S(1)} %collective-permute-done.12.far_halo, ...), custom_call_target="tpu_custom_call" | custom-call | tf_op jit(solution)/shard_map/pallas_call | solution.py:476
  (2 shorter events, 0.0 us)
Async XLA Ops:
  0.6 1.0 %copy-start = (f32[1,4,32,512]{3,2,1,0:T(8,128)S(1)}, f32[1,4,32,512]{3,2,1,0:T(8,128)}, u32[]{:S(2)}) copy-start(f32[1,4,32,512]{3,2,1,0:T(8,128)} %param.3) | copy-start | bytes 786436
  1.6 10.9 %copy-start.1 = (f32[1,4,32,512]{3,2,1,0:T(8,128)S(1)}, f32[1,4,32,512]{3,2,1,0:T(8,128)}, u32[]{:S(2)}) copy-start(f32[1,4,32,512]{3,2,1,0:T(8,128)} %param.4) | copy-start | bytes 786436
  1.6 5.5 %collective-permute-start.1 = (f32[40,512]{1,0:T(8,128)S(1)}, f32[40,512]{1,0:T(8,128)S(1)}, u32[]{:S(2)}, u32[]{:S(2)}) collective-permute-start(f32[40,512]{1,0:T(8,128)S(1)} %get-tuple-element.17), channel_id=1, source_target_pairs={{0,1},{1,0},{2,3},{3,2},{4,5},{5,4},{6,7},{7,6},{8,9},{9,8},{10,11... | collective-permute-start | bytes 245768 | tf_op jit(solution)/shard_map/ppermute | solution.py:421
  4.7 2.4 %collective-permute-start.2 = (f32[40,512]{1,0:T(8,128)S(1)}, f32[40,512]{1,0:T(8,128)S(1)}, u32[]{:S(2)}, u32[]{:S(2)}) collective-permute-start(f32[40,512]{1,0:T(8,128)S(1)} %get-tuple-element.18), channel_id=1, source_target_pairs={{0,4},{1,2},{2,1},{3,7},{4,0},{5,6},{6,5},{7,3},{8,12},{9,10},{10,... | collective-permute-start | bytes 245768 | tf_op jit(solution)/shard_map/ppermute | solution.py:422
  10.3 6.9 %collective-permute-start.4 = (f32[64,512]{1,0:T(8,128)S(1)}, f32[64,512]{1,0:T(8,128)S(1)}, u32[]{:S(2)}, u32[]{:S(2)}) collective-permute-start(f32[64,512]{1,0:T(8,128)S(1)} %get-tuple-element.19.refs_0_), channel_id=1, source_target_pairs={{0,8},{4,20},{8,0},{12,28},{16,24},{20,4},{24,16},{28,12},{1,9},{5... | collective-permute-start | bytes 393224 | tf_op jit(solution)/shard_map/ppermute | solution.py:441
  12.3 4.9 %collective-permute-start.5 = (f32[64,512]{1,0:T(8,128)S(1)}, f32[64,512]{1,0:T(8,128)S(1)}, u32[]{:S(2)}, u32[]{:S(2)}) collective-permute-start(f32[64,512]{1,0:T(8,128)S(1)} %get-tuple-element.20), channel_id=1, source_target_pairs={{0,20},{4,8},{8,28},{12,0},{16,4},{20,24},{24,12},{28,16},{1,21},{... | collective-permute-start | bytes 393224 | tf_op jit(solution)/shard_map/ppermute | solution.py:442
  12.3 4.9 %collective-permute-start.3 = (f32[64,512]{1,0:T(8,128)S(1)}, f32[64,512]{1,0:T(8,128)S(1)}, u32[]{:S(2)}, u32[]{:S(2)}) collective-permute-start(f32[64,512]{1,0:T(8,128)S(1)} %get-tuple-element.20), channel_id=1, source_target_pairs={{0,4},{4,0},{8,12},{12,8},{16,20},{20,16},{24,28},{28,24},{1,5},{5... | collective-permute-start | bytes 393224 | tf_op jit(solution)/shard_map/ppermute | solution.py:439
  12.5 3.1 %copy-start.2 = (s32[8]{0:T(128)S(1)}, s32[8]{0:T(128)}, u32[]{:S(2)}) copy-start(s32[8]{0:T(128)} %parents.1) | copy-start | bytes 100
  12.5 12.5 %collective-permute-start = (f32[4,32,512]{2,1,0:T(8,128)S(1)}, f32[4,32,512]{2,1,0:T(8,128)S(1)}, u32[]{:S(2)}, u32[]{:S(2)}) collective-permute-start(f32[4,32,512]{2,1,0:T(8,128)S(1)} %bitcast.6), channel_id=1, source_target_pairs={{0,4},{4,0},{8,12},{12,8},{16,20},{20,16},{24,28},{28,24},{1,5},{5... | collective-permute-start | bytes 786440 | tf_op jit(solution)/shard_map/ppermute | solution.py:423
  12.8 4.4 %collective-permute-start.6 = (f32[8,128]{1,0:T(8,128)S(1)}, f32[8,128]{1,0:T(8,128)S(1)}, u32[]{:S(2)}, u32[]{:S(2)}) collective-permute-start(f32[8,128]{1,0:T(8,128)S(1)} %get-tuple-element.21), channel_id=1, source_target_pairs={{0,1},{1,0},{2,3},{3,2},{4,5},{5,4},{6,7},{7,6},{8,9},{9,8},{10,11... | collective-permute-start | bytes 12296 | tf_op jit(solution)/shard_map/ppermute | solution.py:450
  17.4 7.7 %collective-permute-start.7 = (f32[64,512]{1,0:T(8,128)S(1)}, f32[64,512]{1,0:T(8,128)S(1)}, u32[]{:S(2)}, u32[]{:S(2)}) collective-permute-start(f32[64,512]{1,0:T(8,128)S(1)} %get-tuple-element.23), channel_id=1, source_target_pairs={{0,16},{4,12},{8,24},{12,4},{16,0},{20,28},{24,8},{28,20},{1,17},{... | collective-permute-start | bytes 393224 | tf_op jit(solution)/shard_map/ppermute | solution.py:464
  18.9 6.1 %collective-permute-start.8 = (f32[64,512]{1,0:T(8,128)S(1)}, f32[64,512]{1,0:T(8,128)S(1)}, u32[]{:S(2)}, u32[]{:S(2)}) collective-permute-start(f32[64,512]{1,0:T(8,128)S(1)} %get-tuple-element.25), channel_id=1, source_target_pairs={{0,16},{4,12},{8,24},{12,4},{16,0},{20,28},{24,8},{28,20},{1,17},{... | collective-permute-start | bytes 393224 | tf_op jit(solution)/shard_map/ppermute | solution.py:465
  19.5 5.6 %collective-permute-start.9 = (f32[8,128]{1,0:T(8,128)S(1)}, f32[8,128]{1,0:T(8,128)S(1)}, u32[]{:S(2)}, u32[]{:S(2)}) collective-permute-start(f32[8,128]{1,0:T(8,128)S(1)} %add.3.refs_4_.score_one), channel_id=1, source_target_pairs={{0,2},{1,3},{2,0},{3,1},{4,6},{5,7},{6,4},{7,5},{8,10},{9,11},{10,... | collective-permute-start | bytes 12296 | tf_op jit(solution)/shard_map/ppermute | solution.py:450
  25.2 6.0 %collective-permute-start.10 = (f32[64,512]{1,0:T(8,128)S(1)}, f32[64,512]{1,0:T(8,128)S(1)}, u32[]{:S(2)}, u32[]{:S(2)}) collective-permute-start(f32[64,512]{1,0:T(8,128)S(1)} %get-tuple-element.27), channel_id=1, source_target_pairs={{0,4},{4,0},{8,12},{12,8},{16,20},{20,16},{24,28},{28,24},{1,5},{5... | collective-permute-start | bytes 393224 | tf_op jit(solution)/shard_map/ppermute | solution.py:474
  25.2 4.5 %collective-permute-start.11 = (f32[40,512]{1,0:T(8,128)S(1)}, f32[40,512]{1,0:T(8,128)S(1)}, u32[]{:S(2)}, u32[]{:S(2)}) collective-permute-start(f32[40,512]{1,0:T(8,128)S(1)} %get-tuple-element.28), channel_id=1, source_target_pairs={{0,8},{1,4},{2,5},{3,6},{4,1},{5,2},{6,3},{7,15},{8,0},{9,12},{10,... | collective-permute-start | bytes 245768 | tf_op jit(solution)/shard_map/ppermute | solution.py:472
  26.8 4.4 %collective-permute-start.12 = (f32[40,512]{1,0:T(8,128)S(1)}, f32[40,512]{1,0:T(8,128)S(1)}, u32[]{:S(2)}, u32[]{:S(2)}) collective-permute-start(f32[40,512]{1,0:T(8,128)S(1)} %get-tuple-element.29), channel_id=1, source_target_pairs={{0,4},{1,0},{2,1},{3,2},{4,5},{5,6},{6,7},{7,3},{8,12},{9,8},{10,9... | collective-permute-start | bytes 245768 | tf_op jit(solution)/shard_map/ppermute | solution.py:473

commit v4 on v1

--- a/solution.py
+++ b/solution.py
@@ -20,13 +20,21 @@
 SMEM = pl.BlockSpec(memory_space=pltpu.SMEM)
 
 
-def stage(src, base, dst, first, count, keep, gain, global_row, total_rows):
+def stage(src, base, dst, first, count, keep, gain, scales, turn, walls, fields):
+    scale, scale_out = scales
     chunks = src.shape[1]
     lane = lax.broadcasted_iota(jnp.int32, (SUB, LANES), 1)
     sub = lax.broadcasted_iota(jnp.int32, (SUB, LANES), 0)
     at_last = lane == LANES - 1
     at_first = lane == 0
     step = gain * time_step
+    linear = scale_out / scale
+    quadratic = -0.5 * step * linear / scale
+    diffuse = step * viscous * linear
+    middle = (gain - 4.0 * step * viscous) * linear
+    slope = 0.5 * step * linear
+    keep = keep * scale_out
+    turn_first, turn_slope = turn
     for row in range(first, first + count, SUB):
 
         def load(field, chunk, offset):
@@ -35,55 +43,66 @@
         cells = [[load(f, j, 0) for j in range(chunks)] for f in range(4)]
         to_west = [[pltpu.roll(c, LANES - 1, 1) for c in line] for line in cells]
         to_east = [[pltpu.roll(c, 1, 1) for c in line] for line in cells]
-        rows = (sub + (row + global_row)).astype(jnp.float32)
-        turn = ((rows + 0.5) * (2.0 * coriolis / total_rows) - coriolis) * step
+        spin = (turn_first + row * turn_slope) * (step * linear)
+        outside = [(sub == at - row) & flag for at, flag in walls if row <= at < row + SUB]
         for j in range(chunks):
             c = [cells[f][j] for f in range(4)]
             n = [load(f, j, 1) for f in range(4)]
             s = [load(f, j, -1) for f in range(4)]
             e = [jnp.where(at_last, to_west[f][(j + 1) % chunks], to_west[f][j]) for f in range(4)]
             w = [jnp.where(at_first, to_east[f][(j - 1) % chunks], to_east[f][j]) for f in range(4)]
-            dx = [e[f] - w[f] for f in range(4)]
-            dy = [n[f] - s[f] for f in range(4)]
-            near = [(e[f] + w[f]) + (n[f] + s[f]) for f in range(4)]
-            u = c[1] * (-0.5 * step)
-            v = c[2] * (-0.5 * step)
-            out = [
-                near[f] * (step * viscous) + c[f] * (gain - 4.0 * step * viscous)
-                for f in range(4)
-            ]
-            flux = ((1.0 + e[0]) * e[1] - (1.0 + w[0]) * w[1]) + (
-                (1.0 + n[0]) * n[2] - (1.0 + s[0]) * s[2]
-            )
-            out[0] = out[0] + flux * (-0.5 * step)
-            out[1] = out[1] + (u * dx[1] + v * dy[1]) + (turn * c[2] - dx[0] * (0.5 * step))
-            out[2] = out[2] + (u * dx[2] + v * dy[2]) - (turn * c[1] + dy[0] * (0.5 * step))
-            out[3] = out[3] + (u * dx[3] + v * dy[3])
-            for f in range(4):
+            u = c[1] * quadratic
+            v = c[2] * quadratic
+            by_e, by_w, by_n, by_s = diffuse + u, diffuse - u, diffuse + v, diffuse - v
+            for f in fields:
+                if f == 0:
+                    near = (e[0] + w[0]) + (n[0] + s[0])
+                    flux = ((scale + e[0]) * e[1] - (scale + w[0]) * w[1]) + (
+                        (scale + n[0]) * n[2] - (scale + s[0]) * s[2]
+                    )
+                    out = near * diffuse + flux * quadratic
+                else:
+                    out = (e[f] * by_e + w[f] * by_w) + (n[f] * by_n + s[f] * by_s)
+                if f == 1:
+                    out = out + (spin * c[2] - (e[0] - w[0]) * slope)
+                if f == 2:
+                    out = out - (spin * c[1] + (n[0] - s[0]) * slope)
+                out = out + (c[f] if abs(middle - 1.0) < 1e-12 else c[f] * middle)
                 if keep:
-                    out[f] = out[f] + keep * base[f, j, pl.ds(row, SUB), :]
-                dst[f, j, pl.ds(row, SUB), :] = out[f]
-
-
-def advance(bufs, origin, rows, reach, domain, domains, total_rows):
+                    kept = base[f, j, pl.ds(row, SUB), :]
+                    out = out + (kept if abs(keep - 1.0) < 1e-12 else kept * keep)
+                for hide in outside:
+                    out = jnp.where(hide, 0.0, out)
+                dst[f, j, pl.ds(row, SUB), :] = out
+
+
+def advance(bufs, origin, rows, reach, domain, domains, total_rows, last_fields=(0, 1, 2, 3)):
     state, one, two = bufs
-    global_row = domain * rows - origin
-    thirds = ((state, one, 0.0, 1.0), (one, two, 0.75, 0.25), (two, state, 1.0 / 3.0, 2.0 / 3.0))
-    for _ in range(STEPS):
-        for src, dst, keep, gain in thirds:
-            reach -= 1
-            first, count = origin - reach, rows + 2 * reach
-            stage(src, state, dst, first, count, keep, gain, global_row, total_rows)
-            if reach > 0:
-                blank = jnp.zeros(dst.shape[:2] + (1, LANES), jnp.float32)
-
-                @pl.when(domain == 0)
-                def _():
-                    dst[:, :, pl.ds(origin - 1, 1), :] = blank
-
-                @pl.when(domain == domains - 1)
-                def _():
-                    dst[:, :, pl.ds(origin + rows, 1), :] = blank
+    sub = lax.broadcasted_iota(jnp.int32, (SUB, LANES), 0)
+    slope = 2.0 * coriolis / total_rows
+    turn_first = ((sub + (domain * rows - origin)).astype(jnp.float32) + 0.5) * slope - coriolis
+    walls = [
+        (origin - 1, jnp.full((SUB, LANES), domain, jnp.int32) == 0),
+        (origin + rows, jnp.full((SUB, LANES), domain, jnp.int32) == domains - 1),
+    ]
+    for at, flag in walls:
+        for f in range(4):
+            for j in range(state.shape[1]):
+                line = state[f, j, pl.ds(at, 1), :]
+                state[f, j, pl.ds(at, 1), :] = jnp.where(flag[:1], 0.0, line)
+    scale_one = 1.0 / (1.0 - 4.0 * time_step * viscous)
+    scale_two = 1.0 / 0.75
+    thirds = (
+        (state, one, 0.0, 1.0, (1.0, scale_one)),
+        (one, two, 0.75, 0.25, (scale_one, scale_two)),
+        (two, state, 1.0 / 3.0, 2.0 / 3.0, (scale_two, 1.0)),
+    )
+    for number in range(3 * STEPS):
+        src, dst, keep, gain, scales = thirds[number % 3]
+        reach -= 1
+        first, count = origin - reach, rows + 2 * reach
+        fields = range(4) if number < 3 * STEPS - 1 else last_fields
+        stage(src, state, dst, first, count, keep, gain, scales, (turn_first, slope), walls, fields)
 
 
 def put(buf, field, row, count, block, row_from, add=False):
@@ -117,10 +136,9 @@
         return 8 * self.body + (which * 4 + field) * self.tail
 
 
-def pack_kernel(sizes, state, pert, mine, other, edge_one, edge_two):
-    rows, half, extra, body, tail = sizes.rows, sizes.half, sizes.extra, sizes.body, sizes.tail
+def pack_kernel(sizes, state, mine, other):
+    rows, half, extra = sizes.rows, sizes.half, sizes.extra
     core = lax.rem(lax.axis_index("member"), 2)
-    parity = lax.rem(lax.axis_index("domain"), 2)
 
     def south_half(out):
         for f in range(4):
@@ -131,6 +149,21 @@
         for f in range(4):
             out[pl.ds(sizes.half_at(f), half), :] = state[f, pl.ds(rows - half, half), :]
             out[pl.ds(sizes.extra_at(f), extra), :] = state[f, pl.ds(rows - half - extra, extra), :]
+
+    @pl.when(core == 0)
+    def _():
+        south_half(mine)
+        north_half(other)
+
+    @pl.when(core == 1)
+    def _():
+        north_half(mine)
+        south_half(other)
+
+
+def edges_kernel(sizes, state, pert, _, edge_one, edge_two):
+    rows, body, tail = sizes.rows, sizes.body, sizes.tail
+    parity = lax.rem(lax.axis_index("domain"), 2)
 
     def south_edge(out):
         for k, a in enumerate((state, pert)):
@@ -143,16 +176,6 @@
             for f in range(4):
                 out[pl.ds(sizes.edge_at(k, f), body), :] = a[f, pl.ds(rows - body, body), :]
                 out[pl.ds(sizes.tail_at(k, f), tail), :] = a[f, pl.ds(rows - REACH, tail), :]
-
-    @pl.when(core == 0)
-    def _():
-        south_half(mine)
-        north_half(other)
-
-    @pl.when(core == 1)
-    def _():
-        north_half(mine)
-        south_half(other)
 
     @pl.when(parity == 0)
     def _():
@@ -204,37 +227,46 @@
     return jnp.clip(parents[member], 0, parents.shape[0] - 1)
 
 
-def pick_kernel(chips, hops, parents, *refs):
+def routes_kernel(chips, hops, parents, out):
     place = Place(*chips)
-    held, outs = refs[: 2 * hops], refs[2 * hops :]
-    at = 0
+    tile = 0
     for hop in range(hops):
         for own in (True, False):
             core = place.core if own else 1 - place.core
             parent = parent_of(parents, place.child(hop, core))
-            index = 2 * place.first_hop(parent) + jnp.where(
-                lax.rem(parent, 2) == place.core, 0, 1
-            )
-            out = outs[at]
-            at += 1
-            for k in range(2 * hops):
-
-                @pl.when(index == k)
-                def _():
-                    out[...] = held[k][...]
-
-
-def settle_kernel(chips, own, parents, *refs):
-    place = Place(*chips)
-    sources, out = refs[:-1], refs[-1]
-    core = place.core if own else 1 - place.core
-    parent = parent_of(parents, place.child(0, core))
-    index = place.second_hop(parent)
-    for k, source in enumerate(sources):
-
-        @pl.when(index == k)
-        def _():
-            out[...] = source[...]
+            same = jnp.where(lax.rem(parent, 2) == place.core, 0, 1)
+            index = 2 * place.first_hop(parent) + same
+            out[pl.ds(tile * SUB, SUB), :] = jnp.full((SUB, LANES), index, jnp.int32)
+            tile += 1
+    for own in (True, False):
+        core = place.core if own else 1 - place.core
+        index = place.second_hop(parent_of(parents, place.child(0, core)))
+        out[pl.ds(tile * SUB, SUB), :] = jnp.full((SUB, LANES), index, jnp.int32)
+        tile += 1
+
+
+def choose(routes, tile, sources, out):
+    index = routes[pl.ds(tile * SUB, SUB), :]
+    takes = [index == k for k in range(1, len(sources))]
+    for row in range(0, out.shape[0], SUB):
+        for lane in range(0, out.shape[1], LANES):
+            where = (pl.ds(row, SUB), pl.ds(lane, LANES))
+            value = sources[0][where]
+            for take, source in zip(takes, sources[1:]):
+                value = jnp.where(take, source[where], value)
+            out[where] = value
+
+
+def pick_kernel(hops, routes, *refs):
+    held, outs = refs[: 2 * hops], refs[-2 * hops :]
+    for tile, out in enumerate(outs):
+        choose(routes, tile, held, out)
+
+
+def settle_kernel(hops, routes, *refs):
+    own_half, sibling_half = refs[-2:]
+    choose(routes, 2 * hops, refs[:hops], own_half)
+    choose(routes, 2 * hops + 1, refs[hops : 2 * hops], sibling_half)
 
 
 def put_edges(sizes, which, buf, origin, edge_one, edge_two, add=False):
@@ -262,7 +294,7 @@
         north(edge_two)
 
 
-def score_kernel(sizes, domains, state, edge_one, edge_two, out, *bufs):
+def score_kernel(sizes, domains, state, edge_one, edge_two, _, out, *bufs):
     rows = sizes.rows
     origin = 16
     total_rows = rows * domains
@@ -270,7 +302,7 @@
     for f in range(4):
         put(bufs[0], f, origin, rows, state.at[f], 0)
     put_edges(sizes, 0, bufs[0], origin, edge_one, edge_two)
-    advance(bufs, origin, rows, REACH, domain, domains, total_rows)
+    advance(bufs, origin, rows, REACH, domain, domains, total_rows, (3,))
     sub = lax.broadcasted_iota(jnp.int32, (SUB, LANES), 0)
     total = jnp.zeros((SUB, LANES), jnp.float32)
     for row in range(0, rows, SUB):
@@ -283,9 +315,14 @@
     out[...] = total
 
 
+def total_kernel(cells, score_one, score_two, _, out):
+    out[0, 0] = jnp.sum(score_one[...] + score_two[...]) / cells
+
+
 def final_kernel(
-    sizes, domains, own_half, far_half, near_halo, far_halo, pert, edge_one, edge_two, out, *bufs
+    sizes, domains, own_half, far_half, near_halo, far_halo, pert, edge_one, edge_two, out, last, *bufs
 ):
+    last[...] = jnp.zeros((SUB, LANES), jnp.float32)
     rows, half, extra = sizes.rows, sizes.half, sizes.extra
     origin = 24
     total_rows = rows * domains
@@ -338,6 +375,7 @@
     hops = max(chips)
     params = pltpu.CompilerParams(vmem_limit_bytes=40 * 2**20)
     half_shape = jax.ShapeDtypeStruct((sizes.half_rows, width), jnp.float32)
+    score_shape = jax.ShapeDtypeStruct((SUB, LANES), jnp.float32)
     edge_shape = jax.ShapeDtypeStruct((sizes.edge_rows, width), jnp.float32)
 
     def member(a, b, core):
@@ -367,84 +405,111 @@
     def flat(m, z):
         return m * domains + z
 
-    south_north = []
-    for chip in range(members // 2):
-        for z in range(1, domains):
-            south_north.append((flat(2 * chip, z), flat(2 * chip + 1, z - 1)))
-            south_north.append((flat(2 * chip + 1, z - 1), flat(2 * chip, z)))
+    levels = range(domains)
+    near = members // 2 % 2 == 0
+
+    def matched(partner):
+        return [
+            (flat(m, z), flat(m, partner(z)) if 0 <= partner(z) < domains else flat(m ^ 1, z))
+            for m in range(members)
+            for z in levels
+        ]
+
+    pair_one = matched(lambda z: z ^ 1)
+    pair_two = matched(lambda z: ((z + 1) ^ 1) - 1)
+    to_other, to_same = [], []
+    for m in range(members):
+        core = m % 2
+        for z in levels:
+            level = z + 1 if core else z - 1
+            if 0 <= level < domains:
+                to_other.append((flat(m, z), flat(m ^ 1, level)))
+                to_same.append((flat(m, z), flat(m, level)))
+            else:
+                if near:
+                    to_other.append((flat(m, z), flat(m ^ 2, z)))
+                to_same.append((flat(m, z), flat(m ^ 1, z)))
     both = ("member", "domain")
-    pair_one = [(z, z ^ 1) for z in range(domains) if z ^ 1 < domains]
-    pair_two = [(z, ((z + 1) ^ 1) - 1) for z in range(domains) if 0 <= ((z + 1) ^ 1) - 1 < domains]
-
-    mine, other, edge_one, edge_two = pl.pallas_call(
-        functools.partial(pack_kernel, sizes),
-        out_shape=(half_shape, half_shape, edge_shape, edge_shape),
-        in_specs=[VMEM, VMEM],
-        out_specs=(VMEM,) * 4,
-        compiler_params=params,
-    )(state, perturbation)
-
-    held = [mine, None]
+
+    def call(kernel, out_shape, in_specs, out_specs, scratch=()):
+        return pl.pallas_call(
+            kernel,
+            out_shape=out_shape,
+            in_specs=in_specs,
+            out_specs=out_specs,
+            scratch_shapes=scratch,
+            compiler_params=params,
+        )
+
+    mine, other = call(
+        functools.partial(pack_kernel, sizes), (half_shape,) * 2, [VMEM], (VMEM,) * 2
+    )(state)
+    held = [mine, lax.ppermute(other, "member", sibling)]
     for k in range(1, hops):
         held.append(lax.ppermute(mine, "member", same_core(True, k)))
         held.append(lax.ppermute(other, "member", other_core(k)))
-    held[1] = lax.ppermute(other, "member", sibling)
-    edge_one = lax.ppermute(edge_one, "domain", pair_one)
-    edge_two = lax.ppermute(edge_two, "domain", pair_two)
-
-    picked = pl.pallas_call(
-        functools.partial(pick_kernel, chips, hops),
-        out_shape=(half_shape,) * (2 * hops),
-        in_specs=[SMEM] + [VMEM] * (2 * hops),
-        out_specs=(VMEM,) * (2 * hops),
-        compiler_params=params,
-    )(parents, *held)
-
-    def settle(own):
-        which = 0 if own else 1
-        sources = [picked[which]]
-        for k in range(1, hops):
-            sources.append(lax.ppermute(picked[2 * k + which], "member", same_core(False, k)))
-        return pl.pallas_call(
-            functools.partial(settle_kernel, chips, own),
-            out_shape=half_shape,
-            in_specs=[SMEM] + [VMEM] * hops,
-            out_specs=VMEM,
-            compiler_params=params,
-        )(parents, *sources)
-
-    own_half = settle(True)
-    sibling_halo = lax.ppermute(own_half, both, south_north)
-    sibling_half = settle(False)
-    near_halo = lax.ppermute(sibling_half, both, south_north)
+    edge_one, edge_two = call(
+        functools.partial(edges_kernel, sizes), (edge_shape,) * 2, [VMEM] * 3, (VMEM,) * 2
+    )(state, perturbation, held[1])
+    edge_one = lax.ppermute(edge_one, both, pair_one)
+    edge_two = lax.ppermute(edge_two, both, pair_two)
+    routes = call(
+        functools.partial(routes_kernel, chips, hops),
+        jax.ShapeDtypeStruct(((2 * hops + 2) * SUB, LANES), jnp.int32),
+        [SMEM],
+        VMEM,
+    )(parents)
+
+    picked = call(
+        functools.partial(pick_kernel, hops),
+        (half_shape,) * (2 * hops),
+        [VMEM] * (2 * hops + 1),
+        (VMEM,) * (2 * hops),
+    )(routes, *held)
+
+    score = call(
+        functools.partial(score_kernel, sizes, domains),
+        score_shape,
+        [VMEM] * 4,
+        VMEM,
+        [pltpu.VMEM((4, chunks, rows + 32, LANES), jnp.float32)] * 3,
+    )(state, edge_one, edge_two, picked[0])
+    scores = [score, jnp.zeros_like(score)]
+    bit = 1
+    if domains & (domains - 1):
+        scores[0] = lax.psum(score, "domain")
+    while bit < domains and domains & (domains - 1) == 0:
+        score = scores[0] if bit == 1 else scores[0] + scores[1]
+        pairs = [(z, z ^ bit) for z in range(domains)]
+        scores = [score, lax.ppermute(score, "domain", pairs)]
+        bit *= 2
+
+    own, other = [picked[0]], [picked[1]]
+    for k in range(1, hops):
+        own.append(lax.ppermute(picked[2 * k], "member", same_core(False, k)))
+        other.append(lax.ppermute(picked[2 * k + 1], "member", same_core(False, k)))
+    own_half, sibling_half = call(
+        functools.partial(settle_kernel, hops),
+        (half_shape, half_shape),
+        [VMEM] * (2 * hops + 2),
+        (VMEM,) * 2,
+    )(routes, *own, *other, score)
+    near_halo = lax.ppermute(sibling_half, both, to_other)
+    far_halo = lax.ppermute(own_half, both, to_same)
     far_half = lax.ppermute(sibling_half, "member", sibling)
-    far_halo = lax.ppermute(sibling_halo, "member", sibling)
-
-    score = pl.pallas_call(
-        functools.partial(score_kernel, sizes, domains),
-        out_shape=jax.ShapeDtypeStruct((SUB, LANES), jnp.float32),
-        in_specs=[VMEM] * 3,
-        out_specs=VMEM,
-        scratch_shapes=[pltpu.VMEM((4, chunks, rows + 32, LANES), jnp.float32)] * 3,
-        compiler_params=params,
-    )(state, edge_one, edge_two)
-    if domains & (domains - 1) == 0:
-        bit = 1
-        while bit < domains:
-            score = score + lax.ppermute(score, "domain", [(z, z ^ bit) for z in range(domains)])
-            bit *= 2
-    else:
-        score = lax.psum(score, "domain")
-    score = jnp.sum(score) / (rows * domains * width)
-
-    after = pl.pallas_call(
+    after, last = call(
         functools.partial(final_kernel, sizes, domains),
-        out_shape=jax.ShapeDtypeStruct((4, rows, width), jnp.float32),
-        in_specs=[VMEM] * 7,
-        out_specs=VMEM,
-        scratch_shapes=[pltpu.VMEM((4, chunks, rows + 48, LANES), jnp.float32)] * 3,
-        compiler_params=params,
+        (jax.ShapeDtypeStruct((4, rows, width), jnp.float32), score_shape),
+        [VMEM] * 7,
+        (VMEM,) * 2,
+        [pltpu.VMEM((4, chunks, rows + 48, LANES), jnp.float32)] * 3,
     )(own_half, far_half, near_halo, far_halo, perturbation, edge_one, edge_two)
+    score = call(
+        functools.partial(total_kernel, rows * domains * width),
+        jax.ShapeDtypeStruct((1, 1), jnp.float32),
+        [VMEM] * 3,
+        SMEM,
+    )(*scores, last)
     return after[None], jnp.reshape(score, (1,))
 
 

time: 50.3 us -> 31.8 us (0.63)
  the two profiles are of different devices: /device:TPU:0 before, /device:TPU:1 now
where the time goes in v4:
time: 31.8 us; the launch traced here: 31.6 us
  starting transfers between devices  14.8 us (47%)
  Pallas kernels  10.7 us (34%)
  waiting for transfers between devices  4.39 us (14%)
  local copies, waits for them, and re-layouts  0.96 us (3%)
  between operations  0.71 us (2%)
    pallas_call x1, Pallas kernels, on_device(): call(functools.partial(final_kernel, sizes, domains), (jax.ShapeDtypeStru...  6.42 us
    ppermute x2, starting transfers between devices, on_device(): scores = [score, lax.ppermute(score, 'domain', pairs)]  4.6 us
    pallas_call x1, Pallas kernels, on_device(): call(functools.partial(score_kernel, sizes, domains), score_shape, [VMEM]...  2.75 us
    ppermute x1, starting transfers between devices, on_device(): held.append(lax.ppermute(mine, 'member', same_core(True, k)))  2.69 us
    ppermute x1, starting transfers between devices, on_device(): edge_one = lax.ppermute(edge_one, both, pair_one)  1.81 us
    ppermute x1, waiting for transfers between devices, on_device(): held.append(lax.ppermute(other, 'member', other_core(k)))  1.75 us
    ppermute x1, starting transfers between devices, on_device(): near_halo = lax.ppermute(sibling_half, both, to_other)  1.7 us
    ppermute x1, waiting for transfers between devices, on_device(): near_halo = lax.ppermute(sibling_half, both, to_other)  1.52 us
  transfers between devices with their start and end apart: 12, of which 4 were waited for; matrix products, arithmetic and copies ran while one was open for 0% of the time, Pallas kernels for 32%

profile of v4, /device:TPU:1, one launch (start us, length us, event | category | flops | bytes accessed | tf_op | source)
XLA Modules:
  0.0 31.6 jit_solution(4905440080935801953)
XLA Ops:
  0.6 0.0 copy-start
  0.6 0.9 %copy-done = f32[1,4,32,512]{3,2,1,0:T(8,128)S(1)} copy-done((f32[1,4,32,512]{3,2,1,0:T(8,128)S(1)}, f32[1,4,32,512]{3,2,1,0:T(8,128)}, u32[]{:S(2)}) %copy-start) | copy-done | bytes 262168
  1.6 0.0 copy-start.2
  1.6 0.1 collective-permute-start
  1.7 2.7 %collective-permute-start.1 = (f32[72,512]{1,0:T(8,128)S(1)}, f32[72,512]{1,0:T(8,128)S(1)}, u32[]{:S(2)}, u32[]{:S(2)}) collective-permute-start(f32[72,512]{1,0:T(8,128)S(1)} %get-tuple-element.14.refs_0_), channel_id=1, source_target_pairs={{0,8},{4,20},{8,0},{12,28},{16,24},{20,4},{24,16},{28,12},{1,9},{5... | collective-permute-start | bytes 442376 | tf_op jit(solution)/shard_map/ppermute | solution.py:449
  4.4 0.0 collective-permute-start.2
  4.4 0.0 collective-permute-done.refs_1_._
  4.4 0.0 copy-done.2
  4.5 0.0 copy-start.3
  4.5 1.8 %collective-permute-start.5 = (f32[72,512]{1,0:T(8,128)S(1)}, f32[72,512]{1,0:T(8,128)S(1)}, u32[]{:S(2)}, u32[]{:S(2)}) collective-permute-start(f32[72,512]{1,0:T(8,128)S(1)} %get-tuple-element.20), channel_id=1, source_target_pairs={{0,1},{1,0},{2,3},{3,2},{4,5},{5,4},{6,7},{7,6},{8,9},{9,8},{10,11... | collective-permute-start | bytes 442376 | tf_op jit(solution)/shard_map/ppermute | solution.py:454
  6.3 0.4 %collective-permute-start.6 = (f32[72,512]{1,0:T(8,128)S(1)}, f32[72,512]{1,0:T(8,128)S(1)}, u32[]{:S(2)}, u32[]{:S(2)}) collective-permute-start(f32[72,512]{1,0:T(8,128)S(1)} %get-tuple-element.21), channel_id=1, source_target_pairs={{0,4},{1,2},{2,1},{3,7},{4,0},{5,6},{6,5},{7,3},{8,12},{9,10},{10,... | collective-permute-start | bytes 442376 | tf_op jit(solution)/shard_map/ppermute | solution.py:455
  6.8 0.0 copy-done.3
  6.8 0.7 %shard_map.50.routes = s32[48,128]{1,0:T(8,128)S(1)} custom-call(s32[8]{0:T(128)S(1)} %copy-done.3), custom_call_target="tpu_custom_call" | custom-call | tf_op jit(solution)/shard_map/pallas_call | solution.py:456
  7.4 0.0 copy-start.1
  7.4 0.1 collective-permute-done.1.refs_2_
  7.5 1.7 %collective-permute-done.2.refs_3_ = f32[72,512]{1,0:T(8,128)S(1)} collective-permute-done((f32[72,512]{1,0:T(8,128)S(1)}, f32[72,512]{1,0:T(8,128)S(1)}, u32[]{:S(2)}, u32[]{:S(2)}) %collective-permute-start.2) | collective-permute-done | bytes 147488 | tf_op jit(solution)/shard_map/ppermute | solution.py:450
  9.3 0.1 shard_map.52
  9.4 1.3 %collective-permute-start.3 = (f32[72,512]{1,0:T(8,128)S(1)}, f32[72,512]{1,0:T(8,128)S(1)}, u32[]{:S(2)}, u32[]{:S(2)}) collective-permute-start(f32[72,512]{1,0:T(8,128)S(1)} %get-tuple-element.17), channel_id=1, source_target_pairs={{0,16},{4,12},{8,24},{12,4},{16,0},{20,28},{24,8},{28,20},{1,17},{... | collective-permute-start | bytes 442376 | tf_op jit(solution)/shard_map/ppermute | solution.py:489
  10.7 0.3 collective-permute-start.4
  11.0 0.0 collective-permute-done.5.edge_one
  11.0 0.0 collective-permute-done.6.edge_two
  11.0 0.0 copy-done.1
  11.0 2.8 %shard_map.54 = f32[8,128]{1,0:T(8,128)S(1)} custom-call(f32[4,32,512]{2,1,0:T(8,128)S(1)} %bitcast.6, f32[72,512]{1,0:T(8,128)S(1)} %collective-permute-done.5.edge_one, f32[72,512]{1,0:T(8,128)S(1)} %collective-permute-done.6.edge_two, f32[72,512]{1,0:T(8,128)S(1)} %get-tuple-element.16._.refs_0_), custom_call_target="tpu_custom_call" | custom-call | tf_op jit(solution)/shard_map/pallas_call | solution.py:470
  13.7 1.8 %collective-permute-start.7 = (f32[8,128]{1,0:T(8,128)S(1)}, f32[8,128]{1,0:T(8,128)S(1)}, u32[]{:S(2)}, u32[]{:S(2)}) collective-permute-start(f32[8,128]{1,0:T(8,128)S(1)} %shard_map.54), channel_id=1, source_target_pairs={{0,1},{1,0},{2,3},{3,2},{4,5},{5,4},{6,7},{7,6},{8,9},{9,8},{10,11... | collective-permute-start | bytes 12296 | tf_op jit(solution)/shard_map/ppermute | solution.py:484
  15.6 1.0 %collective-permute-done.7 = f32[8,128]{1,0:T(8,128)S(1)} collective-permute-done((f32[8,128]{1,0:T(8,128)S(1)}, f32[8,128]{1,0:T(8,128)S(1)}, u32[]{:S(2)}, u32[]{:S(2)}) %collective-permute-start.7) | collective-permute-done | bytes 4128 | tf_op jit(solution)/shard_map/ppermute | solution.py:484
  16.6 0.0 collective-permute-done.3.refs_1_
  16.6 0.0 collective-permute-done.4.refs_3_
  16.6 1.5 %collective-permute-start.10 = (f32[72,512]{1,0:T(8,128)S(1)}, f32[72,512]{1,0:T(8,128)S(1)}, u32[]{:S(2)}, u32[]{:S(2)}) collective-permute-start(f32[72,512]{1,0:T(8,128)S(1)} %get-tuple-element.22.own_half), channel_id=1, source_target_pairs={{0,4},{1,0},{2,1},{3,2},{4,5},{5,6},{6,7},{7,3},{8,12},{9,8},{10,9... | collective-permute-start | bytes 442376 | tf_op jit(solution)/shard_map/ppermute | solution.py:498
  18.1 0.5 %collective-permute-start.8 = (f32[72,512]{1,0:T(8,128)S(1)}, f32[72,512]{1,0:T(8,128)S(1)}, u32[]{:S(2)}, u32[]{:S(2)}) collective-permute-start(f32[72,512]{1,0:T(8,128)S(1)} %get-tuple-element.23), channel_id=1, source_target_pairs={{0,4},{4,0},{8,12},{12,8},{16,20},{20,16},{24,28},{28,24},{1,5},{5... | collective-permute-start | bytes 442376 | tf_op jit(solution)/shard_map/ppermute | solution.py:499
  18.5 1.7 %collective-permute-start.9 = (f32[72,512]{1,0:T(8,128)S(1)}, f32[72,512]{1,0:T(8,128)S(1)}, u32[]{:S(2)}, u32[]{:S(2)}) collective-permute-start(f32[72,512]{1,0:T(8,128)S(1)} %get-tuple-element.23), channel_id=1, source_target_pairs={{0,8},{1,4},{2,5},{3,6},{4,1},{5,2},{6,3},{7,15},{8,0},{9,12},{10,... | collective-permute-start | bytes 442376 | tf_op jit(solution)/shard_map/ppermute | solution.py:497
  20.2 2.8 %collective-permute-start.11 = (f32[8,128]{1,0:T(8,128)S(1)}, f32[8,128]{1,0:T(8,128)S(1)}, u32[]{:S(2)}, u32[]{:S(2)}) collective-permute-start(f32[8,128]{1,0:T(8,128)S(1)} %add.3.refs_4_.score_one), channel_id=1, source_target_pairs={{0,2},{1,3},{2,0},{3,1},{4,6},{5,7},{6,4},{7,5},{8,10},{9,11},{10,... | collective-permute-start | bytes 12296 | tf_op jit(solution)/shard_map/ppermute | solution.py:484
  23.0 0.0 collective-permute-done.10.far_halo
  23.0 0.0 collective-permute-done.8.far_half
  23.0 1.5 %collective-permute-done.9.near_halo = f32[72,512]{1,0:T(8,128)S(1)} collective-permute-done((f32[72,512]{1,0:T(8,128)S(1)}, f32[72,512]{1,0:T(8,128)S(1)}, u32[]{:S(2)}, u32[]{:S(2)}) %collective-permute-start.9) | collective-permute-done | bytes 147488 | tf_op jit(solution)/shard_map/ppermute | solution.py:497
  24.5 6.4 %shard_map.56 = (f32[4,32,512]{2,1,0:T(8,128)}, f32[8,128]{1,0:T(8,128)S(1)}) custom-call(f32[72,512]{1,0:T(8,128)S(1)} %get-tuple-element.22.own_half, f32[72,512]{1,0:T(8,128)S(1)} %collective-permute-done.8.far_half, f32[72,512]{1,0:T(8,128)S(1)} %collective-permute-done.9.near_halo, f32[72,512]{1,0:T(8,128)S(1)} %collective-permute-done.10.far_halo, ...), custom_call_target="tpu_custom_call" | custom-call | tf_op jit(solution)/shard_map/pallas_call | solution.py:500
  31.0 0.0 collective-permute-done.11.score_two
  31.0 0.6 %shard_map.57 = f32[1,1]{1,0:T(1,128)} custom-call(f32[8,128]{1,0:T(8,128)S(1)} %add.3.refs_4_.score_one, f32[8,128]{1,0:T(8,128)S(1)} %collective-permute-done.11.score_two, f32[8,128]{1,0:T(8,128)S(1)} %get-tuple-element.25._), custom_call_target="tpu_custom_call" | custom-call | tf_op jit(solution)/shard_map/pallas_call | solution.py:507
  (4 shorter events, 0.1 us)
Async XLA Ops:
  0.6 1.0 %copy-start = (f32[1,4,32,512]{3,2,1,0:T(8,128)S(1)}, f32[1,4,32,512]{3,2,1,0:T(8,128)}, u32[]{:S(2)}) copy-start(f32[1,4,32,512]{3,2,1,0:T(8,128)} %param.3) | copy-start | bytes 786436
  1.6 2.9 %copy-start.2 = (f32[1,4,32,512]{3,2,1,0:T(8,128)S(1)}, f32[1,4,32,512]{3,2,1,0:T(8,128)}, u32[]{:S(2)}) copy-start(f32[1,4,32,512]{3,2,1,0:T(8,128)} %param.4) | copy-start | bytes 786436
  1.6 2.8 %collective-permute-start = (f32[72,512]{1,0:T(8,128)S(1)}, f32[72,512]{1,0:T(8,128)S(1)}, u32[]{:S(2)}, u32[]{:S(2)}) collective-permute-start(f32[72,512]{1,0:T(8,128)S(1)} %get-tuple-element.15), channel_id=1, source_target_pairs={{0,4},{4,0},{8,12},{12,8},{16,20},{20,16},{24,28},{28,24},{1,5},{5... | collective-permute-start | bytes 442376 | tf_op jit(solution)/shard_map/ppermute | solution.py:447
  1.7 5.8 %collective-permute-start.1 = (f32[72,512]{1,0:T(8,128)S(1)}, f32[72,512]{1,0:T(8,128)S(1)}, u32[]{:S(2)}, u32[]{:S(2)}) collective-permute-start(f32[72,512]{1,0:T(8,128)S(1)} %get-tuple-element.14.refs_0_), channel_id=1, source_target_pairs={{0,8},{4,20},{8,0},{12,28},{16,24},{20,4},{24,16},{28,12},{1,9},{5... | collective-permute-start | bytes 442376 | tf_op jit(solution)/shard_map/ppermute | solution.py:449
  4.4 4.9 %collective-permute-start.2 = (f32[72,512]{1,0:T(8,128)S(1)}, f32[72,512]{1,0:T(8,128)S(1)}, u32[]{:S(2)}, u32[]{:S(2)}) collective-permute-start(f32[72,512]{1,0:T(8,128)S(1)} %get-tuple-element.15), channel_id=1, source_target_pairs={{0,20},{4,8},{8,28},{12,0},{16,4},{20,24},{24,12},{28,16},{1,21},{... | collective-permute-start | bytes 442376 | tf_op jit(solution)/shard_map/ppermute | solution.py:450
  4.5 2.3 %copy-start.3 = (s32[8]{0:T(128)S(1)}, s32[8]{0:T(128)}, u32[]{:S(2)}) copy-start(s32[8]{0:T(128)} %parents.1) | copy-start | bytes 100
  4.5 6.5 %collective-permute-start.5 = (f32[72,512]{1,0:T(8,128)S(1)}, f32[72,512]{1,0:T(8,128)S(1)}, u32[]{:S(2)}, u32[]{:S(2)}) collective-permute-start(f32[72,512]{1,0:T(8,128)S(1)} %get-tuple-element.20), channel_id=1, source_target_pairs={{0,1},{1,0},{2,3},{3,2},{4,5},{5,4},{6,7},{7,6},{8,9},{9,8},{10,11... | collective-permute-start | bytes 442376 | tf_op jit(solution)/shard_map/ppermute | solution.py:454
  6.3 4.7 %collective-permute-start.6 = (f32[72,512]{1,0:T(8,128)S(1)}, f32[72,512]{1,0:T(8,128)S(1)}, u32[]{:S(2)}, u32[]{:S(2)}) collective-permute-start(f32[72,512]{1,0:T(8,128)S(1)} %get-tuple-element.21), channel_id=1, source_target_pairs={{0,4},{1,2},{2,1},{3,7},{4,0},{5,6},{6,5},{7,3},{8,12},{9,10},{10,... | collective-permute-start | bytes 442376 | tf_op jit(solution)/shard_map/ppermute | solution.py:455
  7.4 3.5 %copy-start.1 = (f32[1,4,32,512]{3,2,1,0:T(8,128)S(1)}, f32[1,4,32,512]{3,2,1,0:T(8,128)}, u32[]{:S(2)}) copy-start(f32[1,4,32,512]{3,2,1,0:T(8,128)} %param.3) | copy-start | bytes 786436
  9.4 7.1 %collective-permute-start.3 = (f32[72,512]{1,0:T(8,128)S(1)}, f32[72,512]{1,0:T(8,128)S(1)}, u32[]{:S(2)}, u32[]{:S(2)}) collective-permute-start(f32[72,512]{1,0:T(8,128)S(1)} %get-tuple-element.17), channel_id=1, source_target_pairs={{0,16},{4,12},{8,24},{12,4},{16,0},{20,28},{24,8},{28,20},{1,17},{... | collective-permute-start | bytes 442376 | tf_op jit(solution)/shard_map/ppermute | solution.py:489
  10.7 5.9 %collective-permute-start.4 = (f32[72,512]{1,0:T(8,128)S(1)}, f32[72,512]{1,0:T(8,128)S(1)}, u32[]{:S(2)}, u32[]{:S(2)}) collective-permute-start(f32[72,512]{1,0:T(8,128)S(1)} %get-tuple-element.19), channel_id=1, source_target_pairs={{0,16},{4,12},{8,24},{12,4},{16,0},{20,28},{24,8},{28,20},{1,17},{... | collective-permute-start | bytes 442376 | tf_op jit(solution)/shard_map/ppermute | solution.py:490
  13.7 2.8 %collective-permute-start.7 = (f32[8,128]{1,0:T(8,128)S(1)}, f32[8,128]{1,0:T(8,128)S(1)}, u32[]{:S(2)}, u32[]{:S(2)}) collective-permute-start(f32[8,128]{1,0:T(8,128)S(1)} %shard_map.54), channel_id=1, source_target_pairs={{0,1},{1,0},{2,3},{3,2},{4,5},{5,4},{6,7},{7,6},{8,9},{9,8},{10,11... | collective-permute-start | bytes 12296 | tf_op jit(solution)/shard_map/ppermute | solution.py:484
  16.6 6.4 %collective-permute-start.10 = (f32[72,512]{1,0:T(8,128)S(1)}, f32[72,512]{1,0:T(8,128)S(1)}, u32[]{:S(2)}, u32[]{:S(2)}) collective-permute-start(f32[72,512]{1,0:T(8,128)S(1)} %get-tuple-element.22.own_half), channel_id=1, source_target_pairs={{0,4},{1,0},{2,1},{3,2},{4,5},{5,6},{6,7},{7,3},{8,12},{9,8},{10,9... | collective-permute-start | bytes 442376 | tf_op jit(solution)/shard_map/ppermute | solution.py:498
  18.1 4.9 %collective-permute-start.8 = (f32[72,512]{1,0:T(8,128)S(1)}, f32[72,512]{1,0:T(8,128)S(1)}, u32[]{:S(2)}, u32[]{:S(2)}) collective-permute-start(f32[72,512]{1,0:T(8,128)S(1)} %get-tuple-element.23), channel_id=1, source_target_pairs={{0,4},{4,0},{8,12},{12,8},{16,20},{20,16},{24,28},{28,24},{1,5},{5... | collective-permute-start | bytes 442376 | tf_op jit(solution)/shard_map/ppermute | solution.py:499
  18.5 6.0 %collective-permute-start.9 = (f32[72,512]{1,0:T(8,128)S(1)}, f32[72,512]{1,0:T(8,128)S(1)}, u32[]{:S(2)}, u32[]{:S(2)}) collective-permute-start(f32[72,512]{1,0:T(8,128)S(1)} %get-tuple-element.23), channel_id=1, source_target_pairs={{0,8},{1,4},{2,5},{3,6},{4,1},{5,2},{6,3},{7,15},{8,0},{9,12},{10,... | collective-permute-start | bytes 442376 | tf_op jit(solution)/shard_map/ppermute | solution.py:497
  20.2 10.7 %collective-permute-start.11 = (f32[8,128]{1,0:T(8,128)S(1)}, f32[8,128]{1,0:T(8,128)S(1)}, u32[]{:S(2)}, u32[]{:S(2)}) collective-permute-start(f32[8,128]{1,0:T(8,128)S(1)} %add.3.refs_4_.score_one), channel_id=1, source_target_pairs={{0,2},{1,3},{2,0},{3,1},{4,6},{5,7},{6,4},{7,5},{8,10},{9,11},{10,... | collective-permute-start | bytes 12296 | tf_op jit(solution)/shard_map/ppermute | solution.py:484

commit v5 on v4

--- a/solution.py
+++ b/solution.py
@@ -9,6 +9,7 @@
 
 STEPS = 3
 REACH = 3 * STEPS
+WIDE = 16
 
 time_step = 0.1
 viscous = 0.05
@@ -312,7 +313,8 @@
             line = line + q * q
         place = (sub + (row + domain * rows)).astype(jnp.float32)
         total = total + (1.0 + 2.0 * place / (total_rows - 1)) * line
-    out[...] = total
+    out[...] = jnp.zeros(out.shape, jnp.float32)
+    out[pl.ds(0, SUB), pl.ds(0, LANES)] = total
 
 
 def total_kernel(cells, score_one, score_two, _, out):
@@ -375,6 +377,7 @@
     hops = max(chips)
     params = pltpu.CompilerParams(vmem_limit_bytes=40 * 2**20)
     half_shape = jax.ShapeDtypeStruct((sizes.half_rows, width), jnp.float32)
+    wide_shape = jax.ShapeDtypeStruct((WIDE, width), jnp.float32)
     score_shape = jax.ShapeDtypeStruct((SUB, LANES), jnp.float32)
     edge_shape = jax.ShapeDtypeStruct((sizes.edge_rows, width), jnp.float32)
 
@@ -469,7 +472,7 @@
 
     score = call(
         functools.partial(score_kernel, sizes, domains),
-        score_shape,
+        wide_shape,
         [VMEM] * 4,
         VMEM,
         [pltpu.VMEM((4, chunks, rows + 32, LANES), jnp.float32)] * 3,
@@ -478,11 +481,9 @@
     bit = 1
     if domains & (domains - 1):
         scores[0] = lax.psum(score, "domain")
-    while bit < domains and domains & (domains - 1) == 0:
-        score = scores[0] if bit == 1 else scores[0] + scores[1]
-        pairs = [(z, z ^ bit) for z in range(domains)]
-        scores = [score, lax.ppermute(score, "domain", pairs)]
-        bit *= 2
+    elif domains > 1:
+        scores[1] = lax.ppermute(score, "domain", [(z, z ^ 1) for z in range(domains)])
+    scores = [part[:SUB, :LANES] for part in scores]
 
     own, other = [picked[0]], [picked[1]]
     for k in range(1, hops):
@@ -491,12 +492,17 @@
     own_half, sibling_half = call(
         functools.partial(settle_kernel, hops),
         (half_shape, half_shape),
-        [VMEM] * (2 * hops + 2),
+        [VMEM] * (2 * hops + 1),
         (VMEM,) * 2,
-    )(routes, *own, *other, score)
+    )(routes, *own, *other)
     near_halo = lax.ppermute(sibling_half, both, to_other)
     far_halo = lax.ppermute(own_half, both, to_same)
     far_half = lax.ppermute(sibling_half, "member", sibling)
+    while bit * 2 < domains and domains & (domains - 1) == 0:
+        bit *= 2
+        score = scores[0] + scores[1]
+        pairs = [(z, z ^ bit) for z in range(domains)]
+        scores = [score, lax.ppermute(score, "domain", pairs)]
     after, last = call(
         functools.partial(final_kernel, sizes, domains),
         (jax.ShapeDtypeStruct((4, rows, width), jnp.float32), score_shape),

time: 31.8 us -> 31.1 us (0.978)
  the two profiles are of different devices: /device:TPU:1 before, /device:TPU:0 now
where the time goes in v5:
time: 31.1 us; the launch traced here: 30.9 us
  starting transfers between devices  14.5 us (47%)
  Pallas kernels  10.7 us (34%)
  waiting for transfers between devices  4.02 us (13%)
  local copies, waits for them, and re-layouts  0.96 us (3%)
  between operations  0.71 us (2%)
    pallas_call x1, Pallas kernels, on_device(): call(functools.partial(final_kernel, sizes, domains), (jax.ShapeDtypeStru...  6.43 us
    ppermute x1, starting transfers between devices, on_device(): scores = [score, lax.ppermute(score, 'domain', pairs)]  2.97 us
    pallas_call x1, Pallas kernels, on_device(): call(functools.partial(score_kernel, sizes, domains), wide_shape, [VMEM]...  2.75 us
    ppermute x1, starting transfers between devices, on_device(): held.append(lax.ppermute(mine, 'member', same_core(True, k)))  2.57 us
    ppermute x1, starting transfers between devices, on_device(): lax.ppermute(score, 'domain', [(z, z ^ 1) for z in range(domains)])  2.24 us
    ppermute x1, starting transfers between devices, on_device(): own.append(lax.ppermute(picked[2 * k], 'member', same_core(False, k)))  2.11 us
    ppermute x1, waiting for transfers between devices, on_device(): far_halo = lax.ppermute(own_half, both, to_same)  2 us
    ppermute x1, starting transfers between devices, on_device(): edge_one = lax.ppermute(edge_one, both, pair_one)  1.84 us
  transfers between devices with their start and end apart: 12, of which 3 were waited for; matrix products, arithmetic and copies ran while one was open for 0% of the time, Pallas kernels for 32%

profile of v5, /device:TPU:0, one launch (start us, length us, event | category | flops | bytes accessed | tf_op | source)
XLA Modules:
  0.0 30.9 jit_solution(13335734203820895025)
XLA Ops:
  0.6 0.0 copy-start
  0.6 0.9 %copy-done = f32[1,4,32,512]{3,2,1,0:T(8,128)S(1)} copy-done((f32[1,4,32,512]{3,2,1,0:T(8,128)S(1)}, f32[1,4,32,512]{3,2,1,0:T(8,128)}, u32[]{:S(2)}) %copy-start) | copy-done | bytes 262168
  1.6 0.0 copy-start.2
  1.6 0.5 %collective-permute-start = (f32[72,512]{1,0:T(8,128)S(1)}, f32[72,512]{1,0:T(8,128)S(1)}, u32[]{:S(2)}, u32[]{:S(2)}) collective-permute-start(f32[72,512]{1,0:T(8,128)S(1)} %get-tuple-element.15), channel_id=1, source_target_pairs={{0,4},{4,0},{8,12},{12,8},{16,20},{20,16},{24,28},{28,24},{1,5},{5... | collective-permute-start | bytes 442376 | tf_op jit(solution)/shard_map/ppermute | solution.py:450
  2.1 2.6 %collective-permute-start.1 = (f32[72,512]{1,0:T(8,128)S(1)}, f32[72,512]{1,0:T(8,128)S(1)}, u32[]{:S(2)}, u32[]{:S(2)}) collective-permute-start(f32[72,512]{1,0:T(8,128)S(1)} %get-tuple-element.14.refs_0_), channel_id=1, source_target_pairs={{0,8},{4,20},{8,0},{12,28},{16,24},{20,4},{24,16},{28,12},{1,9},{5... | collective-permute-start | bytes 442376 | tf_op jit(solution)/shard_map/ppermute | solution.py:452
  4.7 0.1 collective-permute-start.2
  4.8 0.0 collective-permute-done.refs_1_._
  4.8 0.0 copy-done.2
  4.8 0.0 copy-start.3
  4.9 1.8 %collective-permute-start.8 = (f32[72,512]{1,0:T(8,128)S(1)}, f32[72,512]{1,0:T(8,128)S(1)}, u32[]{:S(2)}, u32[]{:S(2)}) collective-permute-start(f32[72,512]{1,0:T(8,128)S(1)} %get-tuple-element.22), channel_id=1, source_target_pairs={{0,1},{1,0},{2,3},{3,2},{4,5},{5,4},{6,7},{7,6},{8,9},{9,8},{10,11... | collective-permute-start | bytes 442376 | tf_op jit(solution)/shard_map/ppermute | solution.py:457
  6.7 0.1 collective-permute-start.9
  6.8 0.0 copy-done.3
  6.8 0.7 %shard_map.50.routes = s32[48,128]{1,0:T(8,128)S(1)} custom-call(s32[8]{0:T(128)S(1)} %copy-done.3), custom_call_target="tpu_custom_call" | custom-call | tf_op jit(solution)/shard_map/pallas_call | solution.py:459
  7.4 0.0 copy-start.1
  7.5 1.0 %collective-permute-done.1.refs_2_ = f32[72,512]{1,0:T(8,128)S(1)} collective-permute-done((f32[72,512]{1,0:T(8,128)S(1)}, f32[72,512]{1,0:T(8,128)S(1)}, u32[]{:S(2)}, u32[]{:S(2)}) %collective-permute-start.1) | collective-permute-done | bytes 147488 | tf_op jit(solution)/shard_map/ppermute | solution.py:452
  8.4 1.0 %collective-permute-done.2.refs_3_ = f32[72,512]{1,0:T(8,128)S(1)} collective-permute-done((f32[72,512]{1,0:T(8,128)S(1)}, f32[72,512]{1,0:T(8,128)S(1)}, u32[]{:S(2)}, u32[]{:S(2)}) %collective-permute-start.2) | collective-permute-done | bytes 147488 | tf_op jit(solution)/shard_map/ppermute | solution.py:453
  9.4 0.1 shard_map.52
  9.5 2.1 %collective-permute-start.3 = (f32[72,512]{1,0:T(8,128)S(1)}, f32[72,512]{1,0:T(8,128)S(1)}, u32[]{:S(2)}, u32[]{:S(2)}) collective-permute-start(f32[72,512]{1,0:T(8,128)S(1)} %get-tuple-element.17), channel_id=1, source_target_pairs={{0,16},{4,12},{8,24},{12,4},{16,0},{20,28},{24,8},{28,20},{1,17},{... | collective-permute-start | bytes 442376 | tf_op jit(solution)/shard_map/ppermute | solution.py:490
  11.7 0.1 collective-permute-start.4
  11.7 0.0 collective-permute-done.8.edge_one
  11.7 0.0 collective-permute-done.9.edge_two
  11.7 0.0 copy-done.1
  11.7 2.8 %shard_map.56 = f32[16,512]{1,0:T(8,128)S(1)} custom-call(f32[4,32,512]{2,1,0:T(8,128)S(1)} %bitcast.6, f32[72,512]{1,0:T(8,128)S(1)} %collective-permute-done.8.edge_one, f32[72,512]{1,0:T(8,128)S(1)} %collective-permute-done.9.edge_two, f32[72,512]{1,0:T(8,128)S(1)} %get-tuple-element.16.refs_0_._), custom_call_target="tpu_custom_call" | custom-call | tf_op jit(solution)/shard_map/pallas_call | solution.py:473
  14.5 2.2 %collective-permute-start.10 = (f32[16,512]{1,0:T(8,128)S(1)}, f32[16,512]{1,0:T(8,128)S(1)}, u32[]{:S(2)}, u32[]{:S(2)}) collective-permute-start(f32[16,512]{1,0:T(8,128)S(1)} %shard_map.56), channel_id=1, source_target_pairs={{0,1},{1,0},{2,3},{3,2},{4,5},{5,4},{6,7},{7,6},{8,9},{9,8},{10,11... | collective-permute-start | bytes 98312 | tf_op jit(solution)/shard_map/ppermute | solution.py:485
  16.7 0.0 collective-permute-done.3.refs_1_
  16.7 0.0 collective-permute-done.4.refs_3_
  16.8 1.5 %collective-permute-start.6 = (f32[72,512]{1,0:T(8,128)S(1)}, f32[72,512]{1,0:T(8,128)S(1)}, u32[]{:S(2)}, u32[]{:S(2)}) collective-permute-start(f32[72,512]{1,0:T(8,128)S(1)} %get-tuple-element.21), channel_id=1, source_target_pairs={{0,8},{1,4},{2,5},{3,6},{4,1},{5,2},{6,3},{7,15},{8,0},{9,12},{10,... | collective-permute-start | bytes 442376 | tf_op jit(solution)/shard_map/ppermute | solution.py:498
  18.4 0.3 collective-permute-start.5
  18.7 0.2 collective-permute-start.7
  18.9 0.0 collective-permute-done.10
  18.9 3.0 %collective-permute-start.11 = (f32[8,128]{1,0:T(8,128)S(1)}, f32[8,128]{1,0:T(8,128)S(1)}, u32[]{:S(2)}, u32[]{:S(2)}) collective-permute-start(f32[8,128]{1,0:T(8,128)S(1)} %slice_add_fusion.score_one), channel_id=1, source_target_pairs={{0,2},{1,3},{2,0},{3,1},{4,6},{5,7},{6,4},{7,5},{8,10},{9,11},{10,... | collective-permute-start | bytes 12296 | tf_op jit(solution)/shard_map/ppermute | solution.py:505
  21.8 2.0 %collective-permute-done.7.far_halo = f32[72,512]{1,0:T(8,128)S(1)} collective-permute-done((f32[72,512]{1,0:T(8,128)S(1)}, f32[72,512]{1,0:T(8,128)S(1)}, u32[]{:S(2)}, u32[]{:S(2)}) %collective-permute-start.7) | collective-permute-done | bytes 147488 | tf_op jit(solution)/shard_map/ppermute | solution.py:499
  23.8 0.0 collective-permute-done.6.near_halo
  23.8 0.0 collective-permute-done.5.far_half
  23.8 6.4 %shard_map.55 = (f32[4,32,512]{2,1,0:T(8,128)}, f32[8,128]{1,0:T(8,128)S(1)}) custom-call(f32[72,512]{1,0:T(8,128)S(1)} %get-tuple-element.20.own_half, f32[72,512]{1,0:T(8,128)S(1)} %collective-permute-done.5.far_half, f32[72,512]{1,0:T(8,128)S(1)} %collective-permute-done.6.near_halo, f32[72,512]{1,0:T(8,128)S(1)} %collective-permute-done.7.far_halo, ...), custom_call_target="tpu_custom_call" | custom-call | tf_op jit(solution)/shard_map/pallas_call | solution.py:506
  30.3 0.0 collective-permute-done.11.score_two
  30.3 0.6 %shard_map.57 = f32[1,1]{1,0:T(1,128)} custom-call(f32[8,128]{1,0:T(8,128)S(1)} %slice_add_fusion.score_one, f32[8,128]{1,0:T(8,128)S(1)} %collective-permute-done.11.score_two, f32[8,128]{1,0:T(8,128)S(1)} %get-tuple-element.25._), custom_call_target="tpu_custom_call" | custom-call | tf_op jit(solution)/shard_map/pallas_call | solution.py:513
  (4 shorter events, 0.1 us)
Async XLA Ops:
  0.6 1.0 %copy-start = (f32[1,4,32,512]{3,2,1,0:T(8,128)S(1)}, f32[1,4,32,512]{3,2,1,0:T(8,128)}, u32[]{:S(2)}) copy-start(f32[1,4,32,512]{3,2,1,0:T(8,128)} %param.3) | copy-start | bytes 786436
  1.6 3.2 %copy-start.2 = (f32[1,4,32,512]{3,2,1,0:T(8,128)S(1)}, f32[1,4,32,512]{3,2,1,0:T(8,128)}, u32[]{:S(2)}) copy-start(f32[1,4,32,512]{3,2,1,0:T(8,128)} %param.4) | copy-start | bytes 786436
  1.6 3.2 %collective-permute-start = (f32[72,512]{1,0:T(8,128)S(1)}, f32[72,512]{1,0:T(8,128)S(1)}, u32[]{:S(2)}, u32[]{:S(2)}) collective-permute-start(f32[72,512]{1,0:T(8,128)S(1)} %get-tuple-element.15), channel_id=1, source_target_pairs={{0,4},{4,0},{8,12},{12,8},{16,20},{20,16},{24,28},{28,24},{1,5},{5... | collective-permute-start | bytes 442376 | tf_op jit(solution)/shard_map/ppermute | solution.py:450
  2.1 6.3 %collective-permute-start.1 = (f32[72,512]{1,0:T(8,128)S(1)}, f32[72,512]{1,0:T(8,128)S(1)}, u32[]{:S(2)}, u32[]{:S(2)}) collective-permute-start(f32[72,512]{1,0:T(8,128)S(1)} %get-tuple-element.14.refs_0_), channel_id=1, source_target_pairs={{0,8},{4,20},{8,0},{12,28},{16,24},{20,4},{24,16},{28,12},{1,9},{5... | collective-permute-start | bytes 442376 | tf_op jit(solution)/shard_map/ppermute | solution.py:452
  4.7 4.7 %collective-permute-start.2 = (f32[72,512]{1,0:T(8,128)S(1)}, f32[72,512]{1,0:T(8,128)S(1)}, u32[]{:S(2)}, u32[]{:S(2)}) collective-permute-start(f32[72,512]{1,0:T(8,128)S(1)} %get-tuple-element.15), channel_id=1, source_target_pairs={{0,20},{4,8},{8,28},{12,0},{16,4},{20,24},{24,12},{28,16},{1,21},{... | collective-permute-start | bytes 442376 | tf_op jit(solution)/shard_map/ppermute | solution.py:453
  4.8 1.9 %copy-start.3 = (s32[8]{0:T(128)S(1)}, s32[8]{0:T(128)}, u32[]{:S(2)}) copy-start(s32[8]{0:T(128)} %parents.1) | copy-start | bytes 100
  4.9 6.9 %collective-permute-start.8 = (f32[72,512]{1,0:T(8,128)S(1)}, f32[72,512]{1,0:T(8,128)S(1)}, u32[]{:S(2)}, u32[]{:S(2)}) collective-permute-start(f32[72,512]{1,0:T(8,128)S(1)} %get-tuple-element.22), channel_id=1, source_target_pairs={{0,1},{1,0},{2,3},{3,2},{4,5},{5,4},{6,7},{7,6},{8,9},{9,8},{10,11... | collective-permute-start | bytes 442376 | tf_op jit(solution)/shard_map/ppermute | solution.py:457
  6.7 5.0 %collective-permute-start.9 = (f32[72,512]{1,0:T(8,128)S(1)}, f32[72,512]{1,0:T(8,128)S(1)}, u32[]{:S(2)}, u32[]{:S(2)}) collective-permute-start(f32[72,512]{1,0:T(8,128)S(1)} %get-tuple-element.23), channel_id=1, source_target_pairs={{0,4},{1,2},{2,1},{3,7},{4,0},{5,6},{6,5},{7,3},{8,12},{9,10},{10,... | collective-permute-start | bytes 442376 | tf_op jit(solution)/shard_map/ppermute | solution.py:458
  7.4 4.3 %copy-start.1 = (f32[1,4,32,512]{3,2,1,0:T(8,128)S(1)}, f32[1,4,32,512]{3,2,1,0:T(8,128)}, u32[]{:S(2)}) copy-start(f32[1,4,32,512]{3,2,1,0:T(8,128)} %param.3) | copy-start | bytes 786436
  9.5 7.2 %collective-permute-start.3 = (f32[72,512]{1,0:T(8,128)S(1)}, f32[72,512]{1,0:T(8,128)S(1)}, u32[]{:S(2)}, u32[]{:S(2)}) collective-permute-start(f32[72,512]{1,0:T(8,128)S(1)} %get-tuple-element.17), channel_id=1, source_target_pairs={{0,16},{4,12},{8,24},{12,4},{16,0},{20,28},{24,8},{28,20},{1,17},{... | collective-permute-start | bytes 442376 | tf_op jit(solution)/shard_map/ppermute | solution.py:490
  11.7 5.1 %collective-permute-start.4 = (f32[72,512]{1,0:T(8,128)S(1)}, f32[72,512]{1,0:T(8,128)S(1)}, u32[]{:S(2)}, u32[]{:S(2)}) collective-permute-start(f32[72,512]{1,0:T(8,128)S(1)} %get-tuple-element.19), channel_id=1, source_target_pairs={{0,16},{4,12},{8,24},{12,4},{16,0},{20,28},{24,8},{28,20},{1,17},{... | collective-permute-start | bytes 442376 | tf_op jit(solution)/shard_map/ppermute | solution.py:491
  14.5 4.4 %collective-permute-start.10 = (f32[16,512]{1,0:T(8,128)S(1)}, f32[16,512]{1,0:T(8,128)S(1)}, u32[]{:S(2)}, u32[]{:S(2)}) collective-permute-start(f32[16,512]{1,0:T(8,128)S(1)} %shard_map.56), channel_id=1, source_target_pairs={{0,1},{1,0},{2,3},{3,2},{4,5},{5,4},{6,7},{7,6},{8,9},{9,8},{10,11... | collective-permute-start | bytes 98312 | tf_op jit(solution)/shard_map/ppermute | solution.py:485
  16.8 7.0 %collective-permute-start.6 = (f32[72,512]{1,0:T(8,128)S(1)}, f32[72,512]{1,0:T(8,128)S(1)}, u32[]{:S(2)}, u32[]{:S(2)}) collective-permute-start(f32[72,512]{1,0:T(8,128)S(1)} %get-tuple-element.21), channel_id=1, source_target_pairs={{0,8},{1,4},{2,5},{3,6},{4,1},{5,2},{6,3},{7,15},{8,0},{9,12},{10,... | collective-permute-start | bytes 442376 | tf_op jit(solution)/shard_map/ppermute | solution.py:498
  18.4 5.5 %collective-permute-start.5 = (f32[72,512]{1,0:T(8,128)S(1)}, f32[72,512]{1,0:T(8,128)S(1)}, u32[]{:S(2)}, u32[]{:S(2)}) collective-permute-start(f32[72,512]{1,0:T(8,128)S(1)} %get-tuple-element.21), channel_id=1, source_target_pairs={{0,4},{4,0},{8,12},{12,8},{16,20},{20,16},{24,28},{28,24},{1,5},{5... | collective-permute-start | bytes 442376 | tf_op jit(solution)/shard_map/ppermute | solution.py:500
  18.7 5.2 %collective-permute-start.7 = (f32[72,512]{1,0:T(8,128)S(1)}, f32[72,512]{1,0:T(8,128)S(1)}, u32[]{:S(2)}, u32[]{:S(2)}) collective-permute-start(f32[72,512]{1,0:T(8,128)S(1)} %get-tuple-element.20.own_half), channel_id=1, source_target_pairs={{0,4},{1,0},{2,1},{3,2},{4,5},{5,6},{6,7},{7,3},{8,12},{9,8},{10,9... | collective-permute-start | bytes 442376 | tf_op jit(solution)/shard_map/ppermute | solution.py:499
  18.9 11.4 %collective-permute-start.11 = (f32[8,128]{1,0:T(8,128)S(1)}, f32[8,128]{1,0:T(8,128)S(1)}, u32[]{:S(2)}, u32[]{:S(2)}) collective-permute-start(f32[8,128]{1,0:T(8,128)S(1)} %slice_add_fusion.score_one), channel_id=1, source_target_pairs={{0,2},{1,3},{2,0},{3,1},{4,6},{5,7},{6,4},{7,5},{8,10},{9,11},{10,... | collective-permute-start | bytes 12296 | tf_op jit(solution)/shard_map/ppermute | solution.py:505

commit v6 on v5

--- a/solution.py
+++ b/solution.py
@@ -213,16 +213,6 @@
             lax.rem(self.a - a + chips_a, chips_a),
         )
 
-    def second_hop(self, parent):
-        chips_a, chips_b = self.sizes
-        chip = parent // 2
-        a, b = chip // chips_b, lax.rem(chip, chips_b)
-        return jnp.where(
-            self.core == 0,
-            lax.rem(self.a - a + chips_a, chips_a),
-            lax.rem(self.b - b + chips_b, chips_b),
-        )
-
 
 def parent_of(parents, member):
     return jnp.clip(parents[member], 0, parents.shape[0] - 1)
@@ -233,7 +223,7 @@
     tile = 0
     for hop in range(hops):
         for own in (True, False):
-            core = place.core if own else 1 - place.core
+            core = 1 - place.core if own else place.core
             parent = parent_of(parents, place.child(hop, core))
             same = jnp.where(lax.rem(parent, 2) == place.core, 0, 1)
             index = 2 * place.first_hop(parent) + same
@@ -241,7 +231,7 @@
             tile += 1
     for own in (True, False):
         core = place.core if own else 1 - place.core
-        index = place.second_hop(parent_of(parents, place.child(0, core)))
+        index = place.first_hop(parent_of(parents, place.child(0, core)))
         out[pl.ds(tile * SUB, SUB), :] = jnp.full((SUB, LANES), index, jnp.int32)
         tile += 1
 
@@ -342,11 +332,11 @@
             put(start, f, origin + rows, half, north_halo, at)
             put(start, f, origin + rows + half, extra, north_halo, more)
 
+    @pl.when(core == 1)
+    def _():
+        fill(own_half, far_half, near_halo, far_halo)
+
     @pl.when(core == 0)
-    def _():
-        fill(own_half, far_half, near_halo, far_halo)
-
-    @pl.when(core == 1)
     def _():
         fill(far_half, own_half, far_halo, near_halo)
 
@@ -424,7 +414,7 @@
     for m in range(members):
         core = m % 2
         for z in levels:
-            level = z + 1 if core else z - 1
+            level = z - 1 if core else z + 1
             if 0 <= level < domains:
                 to_other.append((flat(m, z), flat(m ^ 1, level)))
                 to_same.append((flat(m, z), flat(m, level)))
@@ -485,10 +475,12 @@
         scores[1] = lax.ppermute(score, "domain", [(z, z ^ 1) for z in range(domains)])
     scores = [part[:SUB, :LANES] for part in scores]
 
-    own, other = [picked[0]], [picked[1]]
+    own, other = [], []
     for k in range(1, hops):
-        own.append(lax.ppermute(picked[2 * k], "member", same_core(False, k)))
-        other.append(lax.ppermute(picked[2 * k + 1], "member", same_core(False, k)))
+        own.append(lax.ppermute(picked[2 * k], "member", other_core(k)))
+        other.append(lax.ppermute(picked[2 * k + 1], "member", other_core(k)))
+    own.insert(0, lax.ppermute(picked[0], "member", sibling))
+    other.insert(0, lax.ppermute(picked[1], "member", sibling))
     own_half, sibling_half = call(
         functools.partial(settle_kernel, hops),
         (half_shape, half_shape),

time: 31.1 us -> 30.3 us (0.974)
  waiting for transfers between devices: 4.02 us -> 2.87 us
  starting transfers between devices: 14.5 us -> 14.9 us
    ppermute x1, starting transfers between devices: 0.21 us -> 2.47 us  [on_device(): far_halo = lax.ppermute(own_half, both, to_same)]
    ppermute x1, starting transfers between devices: 2.97 us -> 1.82 us  [on_device(): scores = [score, lax.ppermute(score, 'domain', pairs)]]
    ppermute x1, starting transfers between devices: 1.52 us -> 0.37 us  [on_device(): near_halo = lax.ppermute(sibling_half, both, to_other)]
    ppermute x1, waiting for transfers between devices: 2 us -> 0.88 us  [on_device(): far_halo = lax.ppermute(own_half, both, to_same)]
    ppermute x2 -> x4, starting transfers between devices: 2.19 us -> 3.28 us  [the longest x1 1.59 us: on_device(): other.append(lax.ppermute(picked[2 * k + 1], 'member', other_core(k)))]
    ppermute x1, starting transfers between devices: 2.24 us -> 1.64 us  [on_device(): lax.ppermute(score, 'domain', [(z, z ^ 1) for z in range(domains)])]
  transfers between devices with their start and end apart: 12 -> 14, of which waited for: 3 -> 3; matrix products, arithmetic and copies ran while one was open for 0% -> 0% of each run, Pallas kernels for 32% -> 33%
where the time goes in v6:
time: 30.3 us; the launch traced here: 30.1 us
  starting transfers between devices  14.9 us (49%)
  Pallas kernels  10.7 us (35%)
  waiting for transfers between devices  2.87 us (9%)
  local copies, waits for them, and re-layouts  0.96 us (3%)
  between operations  0.73 us (2%)
    pallas_call x1, Pallas kernels, on_device(): call(functools.partial(final_kernel, sizes, domains), (jax.ShapeDtypeStru...  6.42 us
    pallas_call x1, Pallas kernels, on_device(): call(functools.partial(score_kernel, sizes, domains), wide_shape, [VMEM]...  2.75 us
    ppermute x1, starting transfers between devices, on_device(): held.append(lax.ppermute(mine, 'member', same_core(True, k)))  2.57 us
    ppermute x1, starting transfers between devices, on_device(): far_halo = lax.ppermute(own_half, both, to_same)  2.47 us
    ppermute x1, starting transfers between devices, on_device(): edge_one = lax.ppermute(edge_one, both, pair_one)  1.84 us
    ppermute x1, starting transfers between devices, on_device(): scores = [score, lax.ppermute(score, 'domain', pairs)]  1.82 us
    ppermute x1, starting transfers between devices, on_device(): lax.ppermute(score, 'domain', [(z, z ^ 1) for z in range(domains)])  1.64 us
    ppermute x1, starting transfers between devices, on_device(): other.append(lax.ppermute(picked[2 * k + 1], 'member', other_core(k)))  1.59 us
  transfers between devices with their start and end apart: 14, of which 3 were waited for; matrix products, arithmetic and copies ran while one was open for 0% of the time, Pallas kernels for 33%

profile of v6, /device:TPU:0, one launch (start us, length us, event | category | flops | bytes accessed | tf_op | source)
XLA Modules:
  0.0 30.1 jit_solution(8852817648107296557)
XLA Ops:
  0.6 0.0 copy-start
  0.6 0.9 %copy-done = f32[1,4,32,512]{3,2,1,0:T(8,128)S(1)} copy-done((f32[1,4,32,512]{3,2,1,0:T(8,128)S(1)}, f32[1,4,32,512]{3,2,1,0:T(8,128)}, u32[]{:S(2)}) %copy-start) | copy-done | bytes 262168
  1.6 0.0 copy-start.2
  1.6 0.5 %collective-permute-start = (f32[72,512]{1,0:T(8,128)S(1)}, f32[72,512]{1,0:T(8,128)S(1)}, u32[]{:S(2)}, u32[]{:S(2)}) collective-permute-start(f32[72,512]{1,0:T(8,128)S(1)} %get-tuple-element.15), channel_id=1, source_target_pairs={{0,4},{4,0},{8,12},{12,8},{16,20},{20,16},{24,28},{28,24},{1,5},{5... | collective-permute-start | bytes 442376 | tf_op jit(solution)/shard_map/ppermute | solution.py:440
  2.1 2.6 %collective-permute-start.1 = (f32[72,512]{1,0:T(8,128)S(1)}, f32[72,512]{1,0:T(8,128)S(1)}, u32[]{:S(2)}, u32[]{:S(2)}) collective-permute-start(f32[72,512]{1,0:T(8,128)S(1)} %get-tuple-element.14.refs_0_), channel_id=1, source_target_pairs={{0,8},{4,20},{8,0},{12,28},{16,24},{20,4},{24,16},{28,12},{1,9},{5... | collective-permute-start | bytes 442376 | tf_op jit(solution)/shard_map/ppermute | solution.py:442
  4.7 0.1 collective-permute-start.2
  4.8 0.0 collective-permute-done.refs_1_._
  4.8 0.0 copy-done.2
  4.8 0.0 copy-start.3
  4.9 1.8 %collective-permute-start.10 = (f32[72,512]{1,0:T(8,128)S(1)}, f32[72,512]{1,0:T(8,128)S(1)}, u32[]{:S(2)}, u32[]{:S(2)}) collective-permute-start(f32[72,512]{1,0:T(8,128)S(1)} %get-tuple-element.22), channel_id=1, source_target_pairs={{0,1},{1,0},{2,3},{3,2},{4,5},{5,4},{6,7},{7,6},{8,9},{9,8},{10,11... | collective-permute-start | bytes 442376 | tf_op jit(solution)/shard_map/ppermute | solution.py:447
  6.7 0.1 collective-permute-start.11
  6.8 0.0 copy-done.3
  6.8 0.7 %shard_map.50.routes = s32[48,128]{1,0:T(8,128)S(1)} custom-call(s32[8]{0:T(128)S(1)} %copy-done.3), custom_call_target="tpu_custom_call" | custom-call | tf_op jit(solution)/shard_map/pallas_call | solution.py:449
  7.4 0.0 copy-start.1
  7.5 1.0 %collective-permute-done.1.refs_2_ = f32[72,512]{1,0:T(8,128)S(1)} collective-permute-done((f32[72,512]{1,0:T(8,128)S(1)}, f32[72,512]{1,0:T(8,128)S(1)}, u32[]{:S(2)}, u32[]{:S(2)}) %collective-permute-start.1) | collective-permute-done | bytes 147488 | tf_op jit(solution)/shard_map/ppermute | solution.py:442
  8.4 1.0 %collective-permute-done.2.refs_3_ = f32[72,512]{1,0:T(8,128)S(1)} collective-permute-done((f32[72,512]{1,0:T(8,128)S(1)}, f32[72,512]{1,0:T(8,128)S(1)}, u32[]{:S(2)}, u32[]{:S(2)}) %collective-permute-start.2) | collective-permute-done | bytes 147488 | tf_op jit(solution)/shard_map/ppermute | solution.py:443
  9.4 0.1 shard_map.52
  9.5 1.3 %collective-permute-start.4 = (f32[72,512]{1,0:T(8,128)S(1)}, f32[72,512]{1,0:T(8,128)S(1)}, u32[]{:S(2)}, u32[]{:S(2)}) collective-permute-start(f32[72,512]{1,0:T(8,128)S(1)} %get-tuple-element.17), channel_id=1, source_target_pairs={{0,20},{4,8},{8,28},{12,0},{16,4},{20,24},{24,12},{28,16},{1,21},{... | collective-permute-start | bytes 442376 | tf_op jit(solution)/shard_map/ppermute | solution.py:480
  10.8 0.4 %collective-permute-start.5 = (f32[72,512]{1,0:T(8,128)S(1)}, f32[72,512]{1,0:T(8,128)S(1)}, u32[]{:S(2)}, u32[]{:S(2)}) collective-permute-start(f32[72,512]{1,0:T(8,128)S(1)} %get-tuple-element.18), channel_id=1, source_target_pairs={{0,4},{4,0},{8,12},{12,8},{16,20},{20,16},{24,28},{28,24},{1,5},{5... | collective-permute-start | bytes 442376 | tf_op jit(solution)/shard_map/ppermute | solution.py:483
  11.2 1.6 %collective-permute-start.6 = (f32[72,512]{1,0:T(8,128)S(1)}, f32[72,512]{1,0:T(8,128)S(1)}, u32[]{:S(2)}, u32[]{:S(2)}) collective-permute-start(f32[72,512]{1,0:T(8,128)S(1)} %get-tuple-element.19), channel_id=1, source_target_pairs={{0,20},{4,8},{8,28},{12,0},{16,4},{20,24},{24,12},{28,16},{1,21},{... | collective-permute-start | bytes 442376 | tf_op jit(solution)/shard_map/ppermute | solution.py:481
  12.8 0.0 collective-permute-done.10.edge_one
  12.8 0.0 collective-permute-start.3
  12.8 0.0 collective-permute-done.11.edge_two
  12.8 0.0 copy-done.1
  12.8 2.7 %shard_map.56 = f32[16,512]{1,0:T(8,128)S(1)} custom-call(f32[4,32,512]{2,1,0:T(8,128)S(1)} %bitcast.6, f32[72,512]{1,0:T(8,128)S(1)} %collective-permute-done.10.edge_one, f32[72,512]{1,0:T(8,128)S(1)} %collective-permute-done.11.edge_two, f32[72,512]{1,0:T(8,128)S(1)} %get-tuple-element.16._), custom_call_target="tpu_custom_call" | custom-call | tf_op jit(solution)/shard_map/pallas_call | solution.py:463
  15.6 1.6 %collective-permute-start.12 = (f32[16,512]{1,0:T(8,128)S(1)}, f32[16,512]{1,0:T(8,128)S(1)}, u32[]{:S(2)}, u32[]{:S(2)}) collective-permute-start(f32[16,512]{1,0:T(8,128)S(1)} %shard_map.56), channel_id=1, source_target_pairs={{0,1},{1,0},{2,3},{3,2},{4,5},{5,4},{6,7},{7,6},{8,9},{9,8},{10,11... | collective-permute-start | bytes 98312 | tf_op jit(solution)/shard_map/ppermute | solution.py:475
  17.2 0.0 collective-permute-done.4.refs_1_
  17.2 0.0 collective-permute-done.5.refs_2_
  17.2 0.0 collective-permute-done.6.refs_3_
  17.2 0.0 collective-permute-done.3.refs_0_
  17.3 0.4 %collective-permute-start.8 = (f32[72,512]{1,0:T(8,128)S(1)}, f32[72,512]{1,0:T(8,128)S(1)}, u32[]{:S(2)}, u32[]{:S(2)}) collective-permute-start(f32[72,512]{1,0:T(8,128)S(1)} %get-tuple-element.21), channel_id=1, source_target_pairs={{0,5},{1,6},{2,7},{3,11},{4,12},{5,0},{6,1},{7,2},{8,13},{9,14},{1... | collective-permute-start | bytes 442376 | tf_op jit(solution)/shard_map/ppermute | solution.py:490
  17.7 0.2 collective-permute-start.7
  17.9 2.5 %collective-permute-start.9 = (f32[72,512]{1,0:T(8,128)S(1)}, f32[72,512]{1,0:T(8,128)S(1)}, u32[]{:S(2)}, u32[]{:S(2)}) collective-permute-start(f32[72,512]{1,0:T(8,128)S(1)} %get-tuple-element.20.own_half), channel_id=1, source_target_pairs={{0,1},{1,2},{2,3},{3,7},{4,0},{5,4},{6,5},{7,6},{8,9},{9,10},{10,1... | collective-permute-start | bytes 442376 | tf_op jit(solution)/shard_map/ppermute | solution.py:491
  20.3 0.0 collective-permute-done.12
  20.3 1.8 %collective-permute-start.13 = (f32[8,128]{1,0:T(8,128)S(1)}, f32[8,128]{1,0:T(8,128)S(1)}, u32[]{:S(2)}, u32[]{:S(2)}) collective-permute-start(f32[8,128]{1,0:T(8,128)S(1)} %slice_add_fusion.score_one), channel_id=1, source_target_pairs={{0,2},{1,3},{2,0},{3,1},{4,6},{5,7},{6,4},{7,5},{8,10},{9,11},{10,... | collective-permute-start | bytes 12296 | tf_op jit(solution)/shard_map/ppermute | solution.py:497
  22.2 0.9 %collective-permute-done.9.far_halo = f32[72,512]{1,0:T(8,128)S(1)} collective-permute-done((f32[72,512]{1,0:T(8,128)S(1)}, f32[72,512]{1,0:T(8,128)S(1)}, u32[]{:S(2)}, u32[]{:S(2)}) %collective-permute-start.9) | collective-permute-done | bytes 147488 | tf_op jit(solution)/shard_map/ppermute | solution.py:491
  23.0 0.0 collective-permute-done.8.near_halo
  23.1 0.0 collective-permute-done.7.far_half
  23.1 6.4 %shard_map.55 = (f32[4,32,512]{2,1,0:T(8,128)}, f32[8,128]{1,0:T(8,128)S(1)}) custom-call(f32[72,512]{1,0:T(8,128)S(1)} %get-tuple-element.20.own_half, f32[72,512]{1,0:T(8,128)S(1)} %collective-permute-done.7.far_half, f32[72,512]{1,0:T(8,128)S(1)} %collective-permute-done.8.near_halo, f32[72,512]{1,0:T(8,128)S(1)} %collective-permute-done.9.far_halo, ...), custom_call_target="tpu_custom_call" | custom-call | tf_op jit(solution)/shard_map/pallas_call | solution.py:498
  29.5 0.0 collective-permute-done.13.score_two
  29.5 0.6 %shard_map.57 = f32[1,1]{1,0:T(1,128)} custom-call(f32[8,128]{1,0:T(8,128)S(1)} %slice_add_fusion.score_one, f32[8,128]{1,0:T(8,128)S(1)} %collective-permute-done.13.score_two, f32[8,128]{1,0:T(8,128)S(1)} %get-tuple-element.25._), custom_call_target="tpu_custom_call" | custom-call | tf_op jit(solution)/shard_map/pallas_call | solution.py:505
  (4 shorter events, 0.1 us)
Async XLA Ops:
  0.6 1.0 %copy-start = (f32[1,4,32,512]{3,2,1,0:T(8,128)S(1)}, f32[1,4,32,512]{3,2,1,0:T(8,128)}, u32[]{:S(2)}) copy-start(f32[1,4,32,512]{3,2,1,0:T(8,128)} %param.3) | copy-start | bytes 786436
  1.6 3.2 %copy-start.2 = (f32[1,4,32,512]{3,2,1,0:T(8,128)S(1)}, f32[1,4,32,512]{3,2,1,0:T(8,128)}, u32[]{:S(2)}) copy-start(f32[1,4,32,512]{3,2,1,0:T(8,128)} %param.4) | copy-start | bytes 786436
  1.6 3.2 %collective-permute-start = (f32[72,512]{1,0:T(8,128)S(1)}, f32[72,512]{1,0:T(8,128)S(1)}, u32[]{:S(2)}, u32[]{:S(2)}) collective-permute-start(f32[72,512]{1,0:T(8,128)S(1)} %get-tuple-element.15), channel_id=1, source_target_pairs={{0,4},{4,0},{8,12},{12,8},{16,20},{20,16},{24,28},{28,24},{1,5},{5... | collective-permute-start | bytes 442376 | tf_op jit(solution)/shard_map/ppermute | solution.py:440
  2.1 6.3 %collective-permute-start.1 = (f32[72,512]{1,0:T(8,128)S(1)}, f32[72,512]{1,0:T(8,128)S(1)}, u32[]{:S(2)}, u32[]{:S(2)}) collective-permute-start(f32[72,512]{1,0:T(8,128)S(1)} %get-tuple-element.14.refs_0_), channel_id=1, source_target_pairs={{0,8},{4,20},{8,0},{12,28},{16,24},{20,4},{24,16},{28,12},{1,9},{5... | collective-permute-start | bytes 442376 | tf_op jit(solution)/shard_map/ppermute | solution.py:442
  4.7 4.7 %collective-permute-start.2 = (f32[72,512]{1,0:T(8,128)S(1)}, f32[72,512]{1,0:T(8,128)S(1)}, u32[]{:S(2)}, u32[]{:S(2)}) collective-permute-start(f32[72,512]{1,0:T(8,128)S(1)} %get-tuple-element.15), channel_id=1, source_target_pairs={{0,20},{4,8},{8,28},{12,0},{16,4},{20,24},{24,12},{28,16},{1,21},{... | collective-permute-start | bytes 442376 | tf_op jit(solution)/shard_map/ppermute | solution.py:443
  4.8 1.9 %copy-start.3 = (s32[8]{0:T(128)S(1)}, s32[8]{0:T(128)}, u32[]{:S(2)}) copy-start(s32[8]{0:T(128)} %parents.1) | copy-start | bytes 100
  4.9 8.0 %collective-permute-start.10 = (f32[72,512]{1,0:T(8,128)S(1)}, f32[72,512]{1,0:T(8,128)S(1)}, u32[]{:S(2)}, u32[]{:S(2)}) collective-permute-start(f32[72,512]{1,0:T(8,128)S(1)} %get-tuple-element.22), channel_id=1, source_target_pairs={{0,1},{1,0},{2,3},{3,2},{4,5},{5,4},{6,7},{7,6},{8,9},{9,8},{10,11... | collective-permute-start | bytes 442376 | tf_op jit(solution)/shard_map/ppermute | solution.py:447
  6.7 6.1 %collective-permute-start.11 = (f32[72,512]{1,0:T(8,128)S(1)}, f32[72,512]{1,0:T(8,128)S(1)}, u32[]{:S(2)}, u32[]{:S(2)}) collective-permute-start(f32[72,512]{1,0:T(8,128)S(1)} %get-tuple-element.23), channel_id=1, source_target_pairs={{0,4},{1,2},{2,1},{3,7},{4,0},{5,6},{6,5},{7,3},{8,12},{9,10},{10,... | collective-permute-start | bytes 442376 | tf_op jit(solution)/shard_map/ppermute | solution.py:448
  7.4 5.4 %copy-start.1 = (f32[1,4,32,512]{3,2,1,0:T(8,128)S(1)}, f32[1,4,32,512]{3,2,1,0:T(8,128)}, u32[]{:S(2)}) copy-start(f32[1,4,32,512]{3,2,1,0:T(8,128)} %param.3) | copy-start | bytes 786436
  9.5 7.7 %collective-permute-start.4 = (f32[72,512]{1,0:T(8,128)S(1)}, f32[72,512]{1,0:T(8,128)S(1)}, u32[]{:S(2)}, u32[]{:S(2)}) collective-permute-start(f32[72,512]{1,0:T(8,128)S(1)} %get-tuple-element.17), channel_id=1, source_target_pairs={{0,20},{4,8},{8,28},{12,0},{16,4},{20,24},{24,12},{28,16},{1,21},{... | collective-permute-start | bytes 442376 | tf_op jit(solution)/shard_map/ppermute | solution.py:480
  10.8 6.4 %collective-permute-start.5 = (f32[72,512]{1,0:T(8,128)S(1)}, f32[72,512]{1,0:T(8,128)S(1)}, u32[]{:S(2)}, u32[]{:S(2)}) collective-permute-start(f32[72,512]{1,0:T(8,128)S(1)} %get-tuple-element.18), channel_id=1, source_target_pairs={{0,4},{4,0},{8,12},{12,8},{16,20},{20,16},{24,28},{28,24},{1,5},{5... | collective-permute-start | bytes 442376 | tf_op jit(solution)/shard_map/ppermute | solution.py:483
  11.2 6.0 %collective-permute-start.6 = (f32[72,512]{1,0:T(8,128)S(1)}, f32[72,512]{1,0:T(8,128)S(1)}, u32[]{:S(2)}, u32[]{:S(2)}) collective-permute-start(f32[72,512]{1,0:T(8,128)S(1)} %get-tuple-element.19), channel_id=1, source_target_pairs={{0,20},{4,8},{8,28},{12,0},{16,4},{20,24},{24,12},{28,16},{1,21},{... | collective-permute-start | bytes 442376 | tf_op jit(solution)/shard_map/ppermute | solution.py:481
  12.8 4.4 %collective-permute-start.3 = (f32[72,512]{1,0:T(8,128)S(1)}, f32[72,512]{1,0:T(8,128)S(1)}, u32[]{:S(2)}, u32[]{:S(2)}) collective-permute-start(f32[72,512]{1,0:T(8,128)S(1)} %get-tuple-element.16._), channel_id=1, source_target_pairs={{0,4},{4,0},{8,12},{12,8},{16,20},{20,16},{24,28},{28,24},{1,5},{5... | collective-permute-start | bytes 442376 | tf_op jit(solution)/shard_map/ppermute | solution.py:482
  15.6 4.8 %collective-permute-start.12 = (f32[16,512]{1,0:T(8,128)S(1)}, f32[16,512]{1,0:T(8,128)S(1)}, u32[]{:S(2)}, u32[]{:S(2)}) collective-permute-start(f32[16,512]{1,0:T(8,128)S(1)} %shard_map.56), channel_id=1, source_target_pairs={{0,1},{1,0},{2,3},{3,2},{4,5},{5,4},{6,7},{7,6},{8,9},{9,8},{10,11... | collective-permute-start | bytes 98312 | tf_op jit(solution)/shard_map/ppermute | solution.py:475
  17.3 5.8 %collective-permute-start.8 = (f32[72,512]{1,0:T(8,128)S(1)}, f32[72,512]{1,0:T(8,128)S(1)}, u32[]{:S(2)}, u32[]{:S(2)}) collective-permute-start(f32[72,512]{1,0:T(8,128)S(1)} %get-tuple-element.21), channel_id=1, source_target_pairs={{0,5},{1,6},{2,7},{3,11},{4,12},{5,0},{6,1},{7,2},{8,13},{9,14},{1... | collective-permute-start | bytes 442376 | tf_op jit(solution)/shard_map/ppermute | solution.py:490
  17.7 5.4 %collective-permute-start.7 = (f32[72,512]{1,0:T(8,128)S(1)}, f32[72,512]{1,0:T(8,128)S(1)}, u32[]{:S(2)}, u32[]{:S(2)}) collective-permute-start(f32[72,512]{1,0:T(8,128)S(1)} %get-tuple-element.21), channel_id=1, source_target_pairs={{0,4},{4,0},{8,12},{12,8},{16,20},{20,16},{24,28},{28,24},{1,5},{5... | collective-permute-start | bytes 442376 | tf_op jit(solution)/shard_map/ppermute | solution.py:492
  17.9 5.2 %collective-permute-start.9 = (f32[72,512]{1,0:T(8,128)S(1)}, f32[72,512]{1,0:T(8,128)S(1)}, u32[]{:S(2)}, u32[]{:S(2)}) collective-permute-start(f32[72,512]{1,0:T(8,128)S(1)} %get-tuple-element.20.own_half), channel_id=1, source_target_pairs={{0,1},{1,2},{2,3},{3,7},{4,0},{5,4},{6,5},{7,6},{8,9},{9,10},{10,1... | collective-permute-start | bytes 442376 | tf_op jit(solution)/shard_map/ppermute | solution.py:491
  20.3 9.1 %collective-permute-start.13 = (f32[8,128]{1,0:T(8,128)S(1)}, f32[8,128]{1,0:T(8,128)S(1)}, u32[]{:S(2)}, u32[]{:S(2)}) collective-permute-start(f32[8,128]{1,0:T(8,128)S(1)} %slice_add_fusion.score_one), channel_id=1, source_target_pairs={{0,2},{1,3},{2,0},{3,1},{4,6},{5,7},{6,4},{7,5},{8,10},{9,11},{10,... | collective-permute-start | bytes 12296 | tf_op jit(solution)/shard_map/ppermute | solution.py:497

commit v7 on v6

--- a/solution.py
+++ b/solution.py
@@ -41,17 +41,16 @@
         def load(field, chunk, offset):
             return src[field, chunk, pl.ds(row + offset, SUB), :]
 
-        cells = [[load(f, j, 0) for j in range(chunks)] for f in range(4)]
-        to_west = [[pltpu.roll(c, LANES - 1, 1) for c in line] for line in cells]
-        to_east = [[pltpu.roll(c, 1, 1) for c in line] for line in cells]
         spin = (turn_first + row * turn_slope) * (step * linear)
         outside = [(sub == at - row) & flag for at, flag in walls if row <= at < row + SUB]
         for j in range(chunks):
-            c = [cells[f][j] for f in range(4)]
+            c = [load(f, j, 0) for f in range(4)]
             n = [load(f, j, 1) for f in range(4)]
             s = [load(f, j, -1) for f in range(4)]
-            e = [jnp.where(at_last, to_west[f][(j + 1) % chunks], to_west[f][j]) for f in range(4)]
-            w = [jnp.where(at_first, to_east[f][(j - 1) % chunks], to_east[f][j]) for f in range(4)]
+            after = [load(f, (j + 1) % chunks, 0) for f in range(4)]
+            before = [load(f, (j - 1) % chunks, 0) for f in range(4)]
+            e = [pltpu.roll(jnp.where(at_first, after[f], c[f]), LANES - 1, 1) for f in range(4)]
+            w = [pltpu.roll(jnp.where(at_last, before[f], c[f]), 1, 1) for f in range(4)]
             u = c[1] * quadratic
             v = c[2] * quadratic
             by_e, by_w, by_n, by_s = diffuse + u, diffuse - u, diffuse + v, diffuse - v

time: 30.3 us -> 28.9 us (0.954)
  Pallas kernels: 10.7 us -> 9.31 us
  starting transfers between devices: 14.9 us -> 15.5 us
  waiting for transfers between devices: 2.87 us -> 2.28 us
    pallas_call x1, Pallas kernels: 2.75 us -> 2 us  [on_device(): call(functools.partial(score_kernel, sizes, domains), wide_shape, [VMEM]...]
    ppermute x1, starting transfers between devices: 0.37 us -> 1.11 us  [on_device(): near_halo = lax.ppermute(sibling_half, both, to_other)]
    pallas_call x1, Pallas kernels: 6.42 us -> 5.79 us  [on_device(): call(functools.partial(final_kernel, sizes, domains), (jax.ShapeDtypeStru...]
    ppermute x1, starting transfers between devices: 1.82 us -> 2.4 us  [on_device(): scores = [score, lax.ppermute(score, 'domain', pairs)]]
    ppermute x1, waiting for transfers between devices: 0.88 us -> 0.3 us  [on_device(): far_halo = lax.ppermute(own_half, both, to_same)]
    ppermute x1, starting transfers between devices: 2.47 us -> 1.93 us  [on_device(): far_halo = lax.ppermute(own_half, both, to_same)]
  transfers between devices with their start and end apart: 14 -> 14, of which waited for: 3 -> 3; matrix products, arithmetic and copies ran while one was open for 0% -> 0% of each run, Pallas kernels for 33% -> 30%
where the time goes in v7:
time: 28.9 us; the launch traced here: 28.7 us
  starting transfers between devices  15.5 us (54%)
  Pallas kernels  9.31 us (32%)
  waiting for transfers between devices  2.28 us (8%)
  local copies, waits for them, and re-layouts  0.96 us (3%)
  between operations  0.73 us (3%)
    pallas_call x1, Pallas kernels, on_device(): call(functools.partial(final_kernel, sizes, domains), (jax.ShapeDtypeStru...  5.79 us
    ppermute x1, starting transfers between devices, on_device(): held.append(lax.ppermute(mine, 'member', same_core(True, k)))  2.57 us
    ppermute x1, starting transfers between devices, on_device(): scores = [score, lax.ppermute(score, 'domain', pairs)]  2.4 us
    pallas_call x1, Pallas kernels, on_device(): call(functools.partial(score_kernel, sizes, domains), wide_shape, [VMEM]...  2 us
    ppermute x1, starting transfers between devices, on_device(): far_halo = lax.ppermute(own_half, both, to_same)  1.93 us
    ppermute x1, starting transfers between devices, on_device(): edge_one = lax.ppermute(edge_one, both, pair_one)  1.84 us
    ppermute x1, starting transfers between devices, on_device(): lax.ppermute(score, 'domain', [(z, z ^ 1) for z in range(domains)])  1.64 us
    ppermute x1, starting transfers between devices, on_device(): other.append(lax.ppermute(picked[2 * k + 1], 'member', other_core(k)))  1.59 us
  transfers between devices with their start and end apart: 14, of which 3 were waited for; matrix products, arithmetic and copies ran while one was open for 0% of the time, Pallas kernels for 30%

profile of v7, /device:TPU:0, one launch (start us, length us, event | category | flops | bytes accessed | tf_op | source)
XLA Modules:
  0.0 28.7 jit_solution(385328435112818200)
XLA Ops:
  0.6 0.0 copy-start
  0.6 0.9 %copy-done = f32[1,4,32,512]{3,2,1,0:T(8,128)S(1)} copy-done((f32[1,4,32,512]{3,2,1,0:T(8,128)S(1)}, f32[1,4,32,512]{3,2,1,0:T(8,128)}, u32[]{:S(2)}) %copy-start) | copy-done | bytes 262168
  1.6 0.0 copy-start.2
  1.6 0.5 %collective-permute-start = (f32[72,512]{1,0:T(8,128)S(1)}, f32[72,512]{1,0:T(8,128)S(1)}, u32[]{:S(2)}, u32[]{:S(2)}) collective-permute-start(f32[72,512]{1,0:T(8,128)S(1)} %get-tuple-element.15), channel_id=1, source_target_pairs={{0,4},{4,0},{8,12},{12,8},{16,20},{20,16},{24,28},{28,24},{1,5},{5... | collective-permute-start | bytes 442376 | tf_op jit(solution)/shard_map/ppermute | solution.py:439
  2.1 2.6 %collective-permute-start.1 = (f32[72,512]{1,0:T(8,128)S(1)}, f32[72,512]{1,0:T(8,128)S(1)}, u32[]{:S(2)}, u32[]{:S(2)}) collective-permute-start(f32[72,512]{1,0:T(8,128)S(1)} %get-tuple-element.14.refs_0_), channel_id=1, source_target_pairs={{0,8},{4,20},{8,0},{12,28},{16,24},{20,4},{24,16},{28,12},{1,9},{5... | collective-permute-start | bytes 442376 | tf_op jit(solution)/shard_map/ppermute | solution.py:441
  4.7 0.1 collective-permute-start.2
  4.8 0.0 collective-permute-done.refs_1_._
  4.8 0.0 copy-done.2
  4.8 0.0 copy-start.3
  4.9 1.8 %collective-permute-start.10 = (f32[72,512]{1,0:T(8,128)S(1)}, f32[72,512]{1,0:T(8,128)S(1)}, u32[]{:S(2)}, u32[]{:S(2)}) collective-permute-start(f32[72,512]{1,0:T(8,128)S(1)} %get-tuple-element.22), channel_id=1, source_target_pairs={{0,1},{1,0},{2,3},{3,2},{4,5},{5,4},{6,7},{7,6},{8,9},{9,8},{10,11... | collective-permute-start | bytes 442376 | tf_op jit(solution)/shard_map/ppermute | solution.py:446
  6.7 0.1 collective-permute-start.11
  6.8 0.0 copy-done.3
  6.8 0.7 %shard_map.50.routes = s32[48,128]{1,0:T(8,128)S(1)} custom-call(s32[8]{0:T(128)S(1)} %copy-done.3), custom_call_target="tpu_custom_call" | custom-call | tf_op jit(solution)/shard_map/pallas_call | solution.py:448
  7.4 0.0 copy-start.1
  7.5 1.0 %collective-permute-done.1.refs_2_ = f32[72,512]{1,0:T(8,128)S(1)} collective-permute-done((f32[72,512]{1,0:T(8,128)S(1)}, f32[72,512]{1,0:T(8,128)S(1)}, u32[]{:S(2)}, u32[]{:S(2)}) %collective-permute-start.1) | collective-permute-done | bytes 147488 | tf_op jit(solution)/shard_map/ppermute | solution.py:441
  8.4 1.0 %collective-permute-done.2.refs_3_ = f32[72,512]{1,0:T(8,128)S(1)} collective-permute-done((f32[72,512]{1,0:T(8,128)S(1)}, f32[72,512]{1,0:T(8,128)S(1)}, u32[]{:S(2)}, u32[]{:S(2)}) %collective-permute-start.2) | collective-permute-done | bytes 147488 | tf_op jit(solution)/shard_map/ppermute | solution.py:442
  9.4 0.1 shard_map.52
  9.5 1.3 %collective-permute-start.4 = (f32[72,512]{1,0:T(8,128)S(1)}, f32[72,512]{1,0:T(8,128)S(1)}, u32[]{:S(2)}, u32[]{:S(2)}) collective-permute-start(f32[72,512]{1,0:T(8,128)S(1)} %get-tuple-element.17), channel_id=1, source_target_pairs={{0,20},{4,8},{8,28},{12,0},{16,4},{20,24},{24,12},{28,16},{1,21},{... | collective-permute-start | bytes 442376 | tf_op jit(solution)/shard_map/ppermute | solution.py:479
  10.8 0.4 %collective-permute-start.5 = (f32[72,512]{1,0:T(8,128)S(1)}, f32[72,512]{1,0:T(8,128)S(1)}, u32[]{:S(2)}, u32[]{:S(2)}) collective-permute-start(f32[72,512]{1,0:T(8,128)S(1)} %get-tuple-element.18), channel_id=1, source_target_pairs={{0,4},{4,0},{8,12},{12,8},{16,20},{20,16},{24,28},{28,24},{1,5},{5... | collective-permute-start | bytes 442376 | tf_op jit(solution)/shard_map/ppermute | solution.py:482
  11.2 1.6 %collective-permute-start.6 = (f32[72,512]{1,0:T(8,128)S(1)}, f32[72,512]{1,0:T(8,128)S(1)}, u32[]{:S(2)}, u32[]{:S(2)}) collective-permute-start(f32[72,512]{1,0:T(8,128)S(1)} %get-tuple-element.19), channel_id=1, source_target_pairs={{0,20},{4,8},{8,28},{12,0},{16,4},{20,24},{24,12},{28,16},{1,21},{... | collective-permute-start | bytes 442376 | tf_op jit(solution)/shard_map/ppermute | solution.py:480
  12.8 0.0 collective-permute-done.10.edge_one
  12.8 0.0 collective-permute-start.3
  12.8 0.0 collective-permute-done.11.edge_two
  12.8 0.0 copy-done.1
  12.8 2.0 %shard_map.56 = f32[16,512]{1,0:T(8,128)S(1)} custom-call(f32[4,32,512]{2,1,0:T(8,128)S(1)} %bitcast.6, f32[72,512]{1,0:T(8,128)S(1)} %collective-permute-done.10.edge_one, f32[72,512]{1,0:T(8,128)S(1)} %collective-permute-done.11.edge_two, f32[72,512]{1,0:T(8,128)S(1)} %get-tuple-element.16._), custom_call_target="tpu_custom_call" | custom-call | tf_op jit(solution)/shard_map/pallas_call | solution.py:462
  14.8 1.6 %collective-permute-start.12 = (f32[16,512]{1,0:T(8,128)S(1)}, f32[16,512]{1,0:T(8,128)S(1)}, u32[]{:S(2)}, u32[]{:S(2)}) collective-permute-start(f32[16,512]{1,0:T(8,128)S(1)} %shard_map.56), channel_id=1, source_target_pairs={{0,1},{1,0},{2,3},{3,2},{4,5},{5,4},{6,7},{7,6},{8,9},{9,8},{10,11... | collective-permute-start | bytes 98312 | tf_op jit(solution)/shard_map/ppermute | solution.py:474
  16.5 0.0 collective-permute-done.4.refs_1_
  16.5 0.0 collective-permute-done.5.refs_2_
  16.5 0.0 collective-permute-done.6.refs_3_
  16.5 0.0 collective-permute-done.3.refs_0_
  16.6 1.1 %collective-permute-start.8 = (f32[72,512]{1,0:T(8,128)S(1)}, f32[72,512]{1,0:T(8,128)S(1)}, u32[]{:S(2)}, u32[]{:S(2)}) collective-permute-start(f32[72,512]{1,0:T(8,128)S(1)} %get-tuple-element.21), channel_id=1, source_target_pairs={{0,5},{1,6},{2,7},{3,11},{4,12},{5,0},{6,1},{7,2},{8,13},{9,14},{1... | collective-permute-start | bytes 442376 | tf_op jit(solution)/shard_map/ppermute | solution.py:489
  17.7 0.0 collective-permute-start.7
  17.7 1.9 %collective-permute-start.9 = (f32[72,512]{1,0:T(8,128)S(1)}, f32[72,512]{1,0:T(8,128)S(1)}, u32[]{:S(2)}, u32[]{:S(2)}) collective-permute-start(f32[72,512]{1,0:T(8,128)S(1)} %get-tuple-element.20.own_half), channel_id=1, source_target_pairs={{0,1},{1,2},{2,3},{3,7},{4,0},{5,4},{6,5},{7,6},{8,9},{9,10},{10,1... | collective-permute-start | bytes 442376 | tf_op jit(solution)/shard_map/ppermute | solution.py:490
  19.6 0.0 collective-permute-done.12
  19.6 2.4 %collective-permute-start.13 = (f32[8,128]{1,0:T(8,128)S(1)}, f32[8,128]{1,0:T(8,128)S(1)}, u32[]{:S(2)}, u32[]{:S(2)}) collective-permute-start(f32[8,128]{1,0:T(8,128)S(1)} %slice_add_fusion.score_one), channel_id=1, source_target_pairs={{0,2},{1,3},{2,0},{3,1},{4,6},{5,7},{6,4},{7,5},{8,10},{9,11},{10,... | collective-permute-start | bytes 12296 | tf_op jit(solution)/shard_map/ppermute | solution.py:496
  22.0 0.3 %collective-permute-done.9.far_halo = f32[72,512]{1,0:T(8,128)S(1)} collective-permute-done((f32[72,512]{1,0:T(8,128)S(1)}, f32[72,512]{1,0:T(8,128)S(1)}, u32[]{:S(2)}, u32[]{:S(2)}) %collective-permute-start.9) | collective-permute-done | bytes 147488 | tf_op jit(solution)/shard_map/ppermute | solution.py:490
  22.3 0.0 collective-permute-done.8.near_halo
  22.3 0.0 collective-permute-done.7.far_half
  22.3 5.8 %shard_map.55 = (f32[4,32,512]{2,1,0:T(8,128)}, f32[8,128]{1,0:T(8,128)S(1)}) custom-call(f32[72,512]{1,0:T(8,128)S(1)} %get-tuple-element.20.own_half, f32[72,512]{1,0:T(8,128)S(1)} %collective-permute-done.7.far_half, f32[72,512]{1,0:T(8,128)S(1)} %collective-permute-done.8.near_halo, f32[72,512]{1,0:T(8,128)S(1)} %collective-permute-done.9.far_halo, ...), custom_call_target="tpu_custom_call" | custom-call | tf_op jit(solution)/shard_map/pallas_call | solution.py:497
  28.1 0.0 collective-permute-done.13.score_two
  28.1 0.6 %shard_map.57 = f32[1,1]{1,0:T(1,128)} custom-call(f32[8,128]{1,0:T(8,128)S(1)} %slice_add_fusion.score_one, f32[8,128]{1,0:T(8,128)S(1)} %collective-permute-done.13.score_two, f32[8,128]{1,0:T(8,128)S(1)} %get-tuple-element.25._), custom_call_target="tpu_custom_call" | custom-call | tf_op jit(solution)/shard_map/pallas_call | solution.py:504
  (4 shorter events, 0.1 us)
Async XLA Ops:
  0.6 1.0 %copy-start = (f32[1,4,32,512]{3,2,1,0:T(8,128)S(1)}, f32[1,4,32,512]{3,2,1,0:T(8,128)}, u32[]{:S(2)}) copy-start(f32[1,4,32,512]{3,2,1,0:T(8,128)} %param.3) | copy-start | bytes 786436
  1.6 3.2 %copy-start.2 = (f32[1,4,32,512]{3,2,1,0:T(8,128)S(1)}, f32[1,4,32,512]{3,2,1,0:T(8,128)}, u32[]{:S(2)}) copy-start(f32[1,4,32,512]{3,2,1,0:T(8,128)} %param.4) | copy-start | bytes 786436
  1.6 3.2 %collective-permute-start = (f32[72,512]{1,0:T(8,128)S(1)}, f32[72,512]{1,0:T(8,128)S(1)}, u32[]{:S(2)}, u32[]{:S(2)}) collective-permute-start(f32[72,512]{1,0:T(8,128)S(1)} %get-tuple-element.15), channel_id=1, source_target_pairs={{0,4},{4,0},{8,12},{12,8},{16,20},{20,16},{24,28},{28,24},{1,5},{5... | collective-permute-start | bytes 442376 | tf_op jit(solution)/shard_map/ppermute | solution.py:439
  2.1 6.3 %collective-permute-start.1 = (f32[72,512]{1,0:T(8,128)S(1)}, f32[72,512]{1,0:T(8,128)S(1)}, u32[]{:S(2)}, u32[]{:S(2)}) collective-permute-start(f32[72,512]{1,0:T(8,128)S(1)} %get-tuple-element.14.refs_0_), channel_id=1, source_target_pairs={{0,8},{4,20},{8,0},{12,28},{16,24},{20,4},{24,16},{28,12},{1,9},{5... | collective-permute-start | bytes 442376 | tf_op jit(solution)/shard_map/ppermute | solution.py:441
  4.7 4.7 %collective-permute-start.2 = (f32[72,512]{1,0:T(8,128)S(1)}, f32[72,512]{1,0:T(8,128)S(1)}, u32[]{:S(2)}, u32[]{:S(2)}) collective-permute-start(f32[72,512]{1,0:T(8,128)S(1)} %get-tuple-element.15), channel_id=1, source_target_pairs={{0,20},{4,8},{8,28},{12,0},{16,4},{20,24},{24,12},{28,16},{1,21},{... | collective-permute-start | bytes 442376 | tf_op jit(solution)/shard_map/ppermute | solution.py:442
  4.8 1.9 %copy-start.3 = (s32[8]{0:T(128)S(1)}, s32[8]{0:T(128)}, u32[]{:S(2)}) copy-start(s32[8]{0:T(128)} %parents.1) | copy-start | bytes 100
  4.9 8.0 %collective-permute-start.10 = (f32[72,512]{1,0:T(8,128)S(1)}, f32[72,512]{1,0:T(8,128)S(1)}, u32[]{:S(2)}, u32[]{:S(2)}) collective-permute-start(f32[72,512]{1,0:T(8,128)S(1)} %get-tuple-element.22), channel_id=1, source_target_pairs={{0,1},{1,0},{2,3},{3,2},{4,5},{5,4},{6,7},{7,6},{8,9},{9,8},{10,11... | collective-permute-start | bytes 442376 | tf_op jit(solution)/shard_map/ppermute | solution.py:446
  6.7 6.1 %collective-permute-start.11 = (f32[72,512]{1,0:T(8,128)S(1)}, f32[72,512]{1,0:T(8,128)S(1)}, u32[]{:S(2)}, u32[]{:S(2)}) collective-permute-start(f32[72,512]{1,0:T(8,128)S(1)} %get-tuple-element.23), channel_id=1, source_target_pairs={{0,4},{1,2},{2,1},{3,7},{4,0},{5,6},{6,5},{7,3},{8,12},{9,10},{10,... | collective-permute-start | bytes 442376 | tf_op jit(solution)/shard_map/ppermute | solution.py:447
  7.4 5.4 %copy-start.1 = (f32[1,4,32,512]{3,2,1,0:T(8,128)S(1)}, f32[1,4,32,512]{3,2,1,0:T(8,128)}, u32[]{:S(2)}) copy-start(f32[1,4,32,512]{3,2,1,0:T(8,128)} %param.3) | copy-start | bytes 786436
  9.5 7.0 %collective-permute-start.4 = (f32[72,512]{1,0:T(8,128)S(1)}, f32[72,512]{1,0:T(8,128)S(1)}, u32[]{:S(2)}, u32[]{:S(2)}) collective-permute-start(f32[72,512]{1,0:T(8,128)S(1)} %get-tuple-element.17), channel_id=1, source_target_pairs={{0,20},{4,8},{8,28},{12,0},{16,4},{20,24},{24,12},{28,16},{1,21},{... | collective-permute-start | bytes 442376 | tf_op jit(solution)/shard_map/ppermute | solution.py:479
  10.8 5.7 %collective-permute-start.5 = (f32[72,512]{1,0:T(8,128)S(1)}, f32[72,512]{1,0:T(8,128)S(1)}, u32[]{:S(2)}, u32[]{:S(2)}) collective-permute-start(f32[72,512]{1,0:T(8,128)S(1)} %get-tuple-element.18), channel_id=1, source_target_pairs={{0,4},{4,0},{8,12},{12,8},{16,20},{20,16},{24,28},{28,24},{1,5},{5... | collective-permute-start | bytes 442376 | tf_op jit(solution)/shard_map/ppermute | solution.py:482
  11.2 5.3 %collective-permute-start.6 = (f32[72,512]{1,0:T(8,128)S(1)}, f32[72,512]{1,0:T(8,128)S(1)}, u32[]{:S(2)}, u32[]{:S(2)}) collective-permute-start(f32[72,512]{1,0:T(8,128)S(1)} %get-tuple-element.19), channel_id=1, source_target_pairs={{0,20},{4,8},{8,28},{12,0},{16,4},{20,24},{24,12},{28,16},{1,21},{... | collective-permute-start | bytes 442376 | tf_op jit(solution)/shard_map/ppermute | solution.py:480
  12.8 3.7 %collective-permute-start.3 = (f32[72,512]{1,0:T(8,128)S(1)}, f32[72,512]{1,0:T(8,128)S(1)}, u32[]{:S(2)}, u32[]{:S(2)}) collective-permute-start(f32[72,512]{1,0:T(8,128)S(1)} %get-tuple-element.16._), channel_id=1, source_target_pairs={{0,4},{4,0},{8,12},{12,8},{16,20},{20,16},{24,28},{28,24},{1,5},{5... | collective-permute-start | bytes 442376 | tf_op jit(solution)/shard_map/ppermute | solution.py:481
  14.8 4.8 %collective-permute-start.12 = (f32[16,512]{1,0:T(8,128)S(1)}, f32[16,512]{1,0:T(8,128)S(1)}, u32[]{:S(2)}, u32[]{:S(2)}) collective-permute-start(f32[16,512]{1,0:T(8,128)S(1)} %shard_map.56), channel_id=1, source_target_pairs={{0,1},{1,0},{2,3},{3,2},{4,5},{5,4},{6,7},{7,6},{8,9},{9,8},{10,11... | collective-permute-start | bytes 98312 | tf_op jit(solution)/shard_map/ppermute | solution.py:474
  16.6 5.8 %collective-permute-start.8 = (f32[72,512]{1,0:T(8,128)S(1)}, f32[72,512]{1,0:T(8,128)S(1)}, u32[]{:S(2)}, u32[]{:S(2)}) collective-permute-start(f32[72,512]{1,0:T(8,128)S(1)} %get-tuple-element.21), channel_id=1, source_target_pairs={{0,5},{1,6},{2,7},{3,11},{4,12},{5,0},{6,1},{7,2},{8,13},{9,14},{1... | collective-permute-start | bytes 442376 | tf_op jit(solution)/shard_map/ppermute | solution.py:489
  17.7 4.6 %collective-permute-start.7 = (f32[72,512]{1,0:T(8,128)S(1)}, f32[72,512]{1,0:T(8,128)S(1)}, u32[]{:S(2)}, u32[]{:S(2)}) collective-permute-start(f32[72,512]{1,0:T(8,128)S(1)} %get-tuple-element.21), channel_id=1, source_target_pairs={{0,4},{4,0},{8,12},{12,8},{16,20},{20,16},{24,28},{28,24},{1,5},{5... | collective-permute-start | bytes 442376 | tf_op jit(solution)/shard_map/ppermute | solution.py:491
  17.7 4.6 %collective-permute-start.9 = (f32[72,512]{1,0:T(8,128)S(1)}, f32[72,512]{1,0:T(8,128)S(1)}, u32[]{:S(2)}, u32[]{:S(2)}) collective-permute-start(f32[72,512]{1,0:T(8,128)S(1)} %get-tuple-element.20.own_half), channel_id=1, source_target_pairs={{0,1},{1,2},{2,3},{3,7},{4,0},{5,4},{6,5},{7,6},{8,9},{9,10},{10,1... | collective-permute-start | bytes 442376 | tf_op jit(solution)/shard_map/ppermute | solution.py:490
  19.6 8.5 %collective-permute-start.13 = (f32[8,128]{1,0:T(8,128)S(1)}, f32[8,128]{1,0:T(8,128)S(1)}, u32[]{:S(2)}, u32[]{:S(2)}) collective-permute-start(f32[8,128]{1,0:T(8,128)S(1)} %slice_add_fusion.score_one), channel_id=1, source_target_pairs={{0,2},{1,3},{2,0},{3,1},{4,6},{5,7},{6,4},{7,5},{8,10},{9,11},{10,... | collective-permute-start | bytes 12296 | tf_op jit(solution)/shard_map/ppermute | solution.py:496

commit v8 on v7

--- a/solution.py
+++ b/solution.py
@@ -247,16 +247,16 @@
             out[where] = value
 
 
-def pick_kernel(hops, routes, *refs):
-    held, outs = refs[: 2 * hops], refs[-2 * hops :]
-    for tile, out in enumerate(outs):
+def pick_kernel(first, hops, routes, *refs):
+    held, outs = refs[: 2 * hops], refs[2 * hops :]
+    if first == 0:
+        outs = outs[1:]
+    for tile, out in enumerate(outs, 2 * first):
         choose(routes, tile, held, out)
 
 
-def settle_kernel(hops, routes, *refs):
-    own_half, sibling_half = refs[-2:]
-    choose(routes, 2 * hops, refs[:hops], own_half)
-    choose(routes, 2 * hops + 1, refs[hops : 2 * hops], sibling_half)
+def settle_kernel(hops, which, routes, *refs):
+    choose(routes, 2 * hops + which, refs[:hops], refs[-1])
 
 
 def put_edges(sizes, which, buf, origin, edge_one, edge_two, add=False):
@@ -306,8 +306,13 @@
     out[pl.ds(0, SUB), pl.ds(0, LANES)] = total
 
 
+def late_kernel(half, _, out):
+    out[...] = half[...]
+
+
 def total_kernel(cells, score_one, score_two, _, out):
-    out[0, 0] = jnp.sum(score_one[...] + score_two[...]) / cells
+    summed = jnp.sum(score_one[...] + score_two[...], axis=0, keepdims=True)
+    out[...] = jnp.sum(summed, axis=1, keepdims=True) / cells
 
 
 def final_kernel(
@@ -453,11 +458,17 @@
     )(parents)
 
     picked = call(
-        functools.partial(pick_kernel, hops),
-        (half_shape,) * (2 * hops),
+        functools.partial(pick_kernel, 1, hops),
+        (half_shape,) * (2 * hops - 2),
         [VMEM] * (2 * hops + 1),
-        (VMEM,) * (2 * hops),
+        (VMEM,) * (2 * hops - 2),
     )(routes, *held)
+    stay = call(
+        functools.partial(pick_kernel, 0, hops),
+        (half_shape,) * 2,
+        [VMEM] * (2 * hops + 2),
+        (VMEM,) * 2,
+    )(routes, *held, picked[0])
 
     score = call(
         functools.partial(score_kernel, sizes, domains),
@@ -465,7 +476,7 @@
         [VMEM] * 4,
         VMEM,
         [pltpu.VMEM((4, chunks, rows + 32, LANES), jnp.float32)] * 3,
-    )(state, edge_one, edge_two, picked[0])
+    )(state, edge_one, edge_two, stay[0])
     scores = [score, jnp.zeros_like(score)]
     bit = 1
     if domains & (domains - 1):
@@ -474,21 +485,24 @@
         scores[1] = lax.ppermute(score, "domain", [(z, z ^ 1) for z in range(domains)])
     scores = [part[:SUB, :LANES] for part in scores]
 
-    own, other = [], []
-    for k in range(1, hops):
-        own.append(lax.ppermute(picked[2 * k], "member", other_core(k)))
-        other.append(lax.ppermute(picked[2 * k + 1], "member", other_core(k)))
-    own.insert(0, lax.ppermute(picked[0], "member", sibling))
-    other.insert(0, lax.ppermute(picked[1], "member", sibling))
-    own_half, sibling_half = call(
-        functools.partial(settle_kernel, hops),
-        (half_shape, half_shape),
-        [VMEM] * (2 * hops + 1),
-        (VMEM,) * 2,
-    )(routes, *own, *other)
+    own = [lax.ppermute(stay[0], "member", sibling)]
+    other = [lax.ppermute(stay[1], "member", sibling)]
+    for k in range(hops - 1):
+        own.append(lax.ppermute(picked[2 * k], "member", other_core(k + 1)))
+        other.append(lax.ppermute(picked[2 * k + 1], "member", other_core(k + 1)))
+    own_half, sibling_half = [
+        call(
+            functools.partial(settle_kernel, hops, which),
+            half_shape,
+            [VMEM] * (hops + 1),
+            VMEM,
+        )(routes, *sources)
+        for which, sources in enumerate((own, other))
+    ]
     near_halo = lax.ppermute(sibling_half, both, to_other)
     far_halo = lax.ppermute(own_half, both, to_same)
-    far_half = lax.ppermute(sibling_half, "member", sibling)
+    (held_back,) = call(late_kernel, (half_shape,), [VMEM] * 2, (VMEM,))(sibling_half, scores[1])
+    far_half = lax.ppermute(held_back, "member", sibling)
     while bit * 2 < domains and domains & (domains - 1) == 0:
         bit *= 2
         score = scores[0] + scores[1]
@@ -505,7 +519,7 @@
         functools.partial(total_kernel, rows * domains * width),
         jax.ShapeDtypeStruct((1, 1), jnp.float32),
         [VMEM] * 3,
-        SMEM,
+        VMEM,
     )(*scores, last)
     return after[None], jnp.reshape(score, (1,))
 

time: 28.9 us -> 28.8 us (level)
  waiting for transfers between devices: 2.28 us -> 1.41 us
  starting transfers between devices: 15.5 us -> 15.9 us
    ppermute x1, starting transfers between devices: 0.1 us -> 2.63 us  [on_device(): held.append(lax.ppermute(other, 'member', other_core(k)))]
    ppermute x1, starting transfers between devices: 2.57 us -> 1.49 us  [on_device(): held.append(lax.ppermute(mine, 'member', same_core(True, k)))]
    ppermute x1, waiting for transfers between devices: 0.97 us -> 0.01 us  [on_device(): held.append(lax.ppermute(other, 'member', other_core(k)))]
    ppermute x1, starting transfers between devices: 1.11 us -> 0.36 us  [on_device(): near_halo = lax.ppermute(sibling_half, both, to_other)]
    ppermute x5, starting transfers between devices: 3.28 us -> 2.57 us  [the longest x1 1.35 us: on_device(): other.append(lax.ppermute(picked[2 * k + 1], 'member', other_core(k + 1)))]
    ppermute x1, starting transfers between devices: 2.4 us -> 2.76 us  [on_device(): scores = [score, lax.ppermute(score, 'domain', pairs)]]
    ppermute x1, starting transfers between devices: 1.64 us -> 2 us  [on_device(): lax.ppermute(score, 'domain', [(z, z ^ 1) for z in range(domains)])]
    ppermute x1, waiting for transfers between devices: 0.3 us -> 0.01 us  [on_device(): far_halo = lax.ppermute(own_half, both, to_same)]
  transfers between devices with their start and end apart: 14 -> 14, of which waited for: 3 -> 2; matrix products, arithmetic and copies ran while one was open for 0% -> 0% of each run, Pallas kernels for 30% -> 31%
where the time goes in v8:
time: 28.8 us; the launch traced here: 28.4 us
  starting transfers between devices  15.9 us (55%)
  Pallas kernels  9.3 us (32%)
  waiting for transfers between devices  1.41 us (5%)
  local copies, waits for them, and re-layouts  0.96 us (3%)
  between operations  0.75 us (3%)
    pallas_call x1, Pallas kernels, on_device(): call(functools.partial(final_kernel, sizes, domains), (jax.ShapeDtypeStru...  5.8 us
    ppermute x1, starting transfers between devices, on_device(): scores = [score, lax.ppermute(score, 'domain', pairs)]  2.76 us
    ppermute x1, starting transfers between devices, on_device(): held.append(lax.ppermute(other, 'member', other_core(k)))  2.63 us
    pallas_call x1, Pallas kernels, on_device(): call(functools.partial(score_kernel, sizes, domains), wide_shape, [VMEM]...  2 us
    ppermute x1, starting transfers between devices, on_device(): lax.ppermute(score, 'domain', [(z, z ^ 1) for z in range(domains)])  2 us
    ppermute x1, starting transfers between devices, on_device(): far_halo = lax.ppermute(own_half, both, to_same)  1.97 us
    ppermute x1, starting transfers between devices, on_device(): edge_one = lax.ppermute(edge_one, both, pair_one)  1.64 us
    ppermute x1, starting transfers between devices, on_device(): held.append(lax.ppermute(mine, 'member', same_core(True, k)))  1.49 us
  transfers between devices with their start and end apart: 14, of which 2 were waited for; matrix products, arithmetic and copies ran while one was open for 0% of the time, Pallas kernels for 31%

profile of v8, /device:TPU:0, one launch (start us, length us, event | category | flops | bytes accessed | tf_op | source)
XLA Modules:
  0.0 28.4 jit_solution(7476161681029467372)
XLA Ops:
  0.6 0.0 copy-start
  0.6 0.9 %copy-done = f32[1,4,32,512]{3,2,1,0:T(8,128)S(1)} copy-done((f32[1,4,32,512]{3,2,1,0:T(8,128)S(1)}, f32[1,4,32,512]{3,2,1,0:T(8,128)}, u32[]{:S(2)}) %copy-start) | copy-done | bytes 262168
  1.6 0.0 copy-start.2
  1.6 0.5 %collective-permute-start = (f32[72,512]{1,0:T(8,128)S(1)}, f32[72,512]{1,0:T(8,128)S(1)}, u32[]{:S(2)}, u32[]{:S(2)}) collective-permute-start(f32[72,512]{1,0:T(8,128)S(1)} %get-tuple-element.13), channel_id=1, source_target_pairs={{0,4},{4,0},{8,12},{12,8},{16,20},{20,16},{24,28},{28,24},{1,5},{5... | collective-permute-start | bytes 442376 | tf_op jit(solution)/shard_map/ppermute | solution.py:444
  2.1 2.6 %collective-permute-start.2 = (f32[72,512]{1,0:T(8,128)S(1)}, f32[72,512]{1,0:T(8,128)S(1)}, u32[]{:S(2)}, u32[]{:S(2)}) collective-permute-start(f32[72,512]{1,0:T(8,128)S(1)} %get-tuple-element.13), channel_id=1, source_target_pairs={{0,20},{4,8},{8,28},{12,0},{16,4},{20,24},{24,12},{28,16},{1,21},{... | collective-permute-start | bytes 442376 | tf_op jit(solution)/shard_map/ppermute | solution.py:447
  4.8 1.5 %collective-permute-start.1 = (f32[72,512]{1,0:T(8,128)S(1)}, f32[72,512]{1,0:T(8,128)S(1)}, u32[]{:S(2)}, u32[]{:S(2)}) collective-permute-start(f32[72,512]{1,0:T(8,128)S(1)} %get-tuple-element.12.refs_0_), channel_id=1, source_target_pairs={{0,8},{4,20},{8,0},{12,28},{16,24},{20,4},{24,16},{28,12},{1,9},{5... | collective-permute-start | bytes 442376 | tf_op jit(solution)/shard_map/ppermute | solution.py:446
  6.3 0.0 collective-permute-done.refs_1_._
  6.3 0.0 copy-done.2
  6.3 0.0 copy-start.3
  6.3 1.6 %collective-permute-start.7 = (f32[72,512]{1,0:T(8,128)S(1)}, f32[72,512]{1,0:T(8,128)S(1)}, u32[]{:S(2)}, u32[]{:S(2)}) collective-permute-start(f32[72,512]{1,0:T(8,128)S(1)} %get-tuple-element.18), channel_id=1, source_target_pairs={{0,1},{1,0},{2,3},{3,2},{4,5},{5,4},{6,7},{7,6},{8,9},{9,8},{10,11... | collective-permute-start | bytes 442376 | tf_op jit(solution)/shard_map/ppermute | solution.py:451
  8.0 0.0 collective-permute-start.8
  8.0 0.0 copy-done.3
  8.0 0.7 %shard_map.50.routes = s32[48,128]{1,0:T(8,128)S(1)} custom-call(s32[8]{0:T(128)S(1)} %copy-done.3), custom_call_target="tpu_custom_call" | custom-call | tf_op jit(solution)/shard_map/pallas_call | solution.py:453
  8.6 0.0 collective-permute-done.2.refs_3_
  8.6 1.3 %collective-permute-done.1.refs_2_ = f32[72,512]{1,0:T(8,128)S(1)} collective-permute-done((f32[72,512]{1,0:T(8,128)S(1)}, f32[72,512]{1,0:T(8,128)S(1)}, u32[]{:S(2)}, u32[]{:S(2)}) %collective-permute-start.1) | collective-permute-done | bytes 147488 | tf_op jit(solution)/shard_map/ppermute | solution.py:446
  9.9 0.1 shard_map.52
  10.0 0.0 copy-start.1
  10.0 0.1 shard_map.53
  10.1 0.1 collective-permute-start.5
  10.1 1.4 %collective-permute-start.6 = (f32[72,512]{1,0:T(8,128)S(1)}, f32[72,512]{1,0:T(8,128)S(1)}, u32[]{:S(2)}, u32[]{:S(2)}) collective-permute-start(f32[72,512]{1,0:T(8,128)S(1)} %get-tuple-element.17), channel_id=1, source_target_pairs={{0,20},{4,8},{8,28},{12,0},{16,4},{20,24},{24,12},{28,16},{1,21},{... | collective-permute-start | bytes 442376 | tf_op jit(solution)/shard_map/ppermute | solution.py:492
  11.5 0.3 %collective-permute-start.3 = (f32[72,512]{1,0:T(8,128)S(1)}, f32[72,512]{1,0:T(8,128)S(1)}, u32[]{:S(2)}, u32[]{:S(2)}) collective-permute-start(f32[72,512]{1,0:T(8,128)S(1)} %get-tuple-element.15._), channel_id=1, source_target_pairs={{0,4},{4,0},{8,12},{12,8},{16,20},{20,16},{24,28},{28,24},{1,5},{5... | collective-permute-start | bytes 442376 | tf_op jit(solution)/shard_map/ppermute | solution.py:488
  11.8 0.1 collective-permute-done.7.edge_one
  11.9 0.8 %collective-permute-start.4 = (f32[72,512]{1,0:T(8,128)S(1)}, f32[72,512]{1,0:T(8,128)S(1)}, u32[]{:S(2)}, u32[]{:S(2)}) collective-permute-start(f32[72,512]{1,0:T(8,128)S(1)} %get-tuple-element.14.refs_4_), channel_id=1, source_target_pairs={{0,20},{4,8},{8,28},{12,0},{16,4},{20,24},{24,12},{28,16},{1,21},{... | collective-permute-start | bytes 442376 | tf_op jit(solution)/shard_map/ppermute | solution.py:491
  12.7 0.0 collective-permute-done.8.edge_two
  12.7 0.0 copy-done.1
  12.7 2.0 %shard_map.57 = f32[16,512]{1,0:T(8,128)S(1)} custom-call(f32[4,32,512]{2,1,0:T(8,128)S(1)} %bitcast.6, f32[72,512]{1,0:T(8,128)S(1)} %collective-permute-done.7.edge_one, f32[72,512]{1,0:T(8,128)S(1)} %collective-permute-done.8.edge_two, f32[72,512]{1,0:T(8,128)S(1)} %get-tuple-element.15._), custom_call_target="tpu_custom_call" | custom-call | tf_op jit(solution)/shard_map/pallas_call | solution.py:473
  14.7 2.0 %collective-permute-start.9 = (f32[16,512]{1,0:T(8,128)S(1)}, f32[16,512]{1,0:T(8,128)S(1)}, u32[]{:S(2)}, u32[]{:S(2)}) collective-permute-start(f32[16,512]{1,0:T(8,128)S(1)} %shard_map.57), channel_id=1, source_target_pairs={{0,1},{1,0},{2,3},{3,2},{4,5},{5,4},{6,7},{7,6},{8,9},{9,8},{10,11... | collective-permute-start | bytes 98312 | tf_op jit(solution)/shard_map/ppermute | solution.py:485
  16.7 0.0 collective-permute-done.5.refs_0_
  16.7 0.0 collective-permute-done.6.refs_1_
  16.7 0.4 %collective-permute-start.11 = (f32[72,512]{1,0:T(8,128)S(1)}, f32[72,512]{1,0:T(8,128)S(1)}, u32[]{:S(2)}, u32[]{:S(2)}) collective-permute-start(f32[72,512]{1,0:T(8,128)S(1)} %shard_map.55.half), channel_id=1, source_target_pairs={{0,5},{1,6},{2,7},{3,11},{4,12},{5,0},{6,1},{7,2},{8,13},{9,14},{1... | collective-permute-start | bytes 442376 | tf_op jit(solution)/shard_map/ppermute | solution.py:502
  17.1 0.0 collective-permute-done.3.refs_0_
  17.1 0.0 collective-permute-done.4.refs_1_
  17.1 2.0 %collective-permute-start.12 = (f32[72,512]{1,0:T(8,128)S(1)}, f32[72,512]{1,0:T(8,128)S(1)}, u32[]{:S(2)}, u32[]{:S(2)}) collective-permute-start(f32[72,512]{1,0:T(8,128)S(1)} %shard_map.54.own_half), channel_id=1, source_target_pairs={{0,1},{1,2},{2,3},{3,7},{4,0},{5,4},{6,5},{7,6},{8,9},{9,10},{10,1... | collective-permute-start | bytes 442376 | tf_op jit(solution)/shard_map/ppermute | solution.py:503
  19.1 0.0 collective-permute-done.9
  19.1 0.1 collective-permute-start.10
  19.2 2.8 %collective-permute-start.13 = (f32[8,128]{1,0:T(8,128)S(1)}, f32[8,128]{1,0:T(8,128)S(1)}, u32[]{:S(2)}, u32[]{:S(2)}) collective-permute-start(f32[8,128]{1,0:T(8,128)S(1)} %get-tuple-element.22.score_one), channel_id=1, source_target_pairs={{0,2},{1,3},{2,0},{3,1},{4,6},{5,7},{6,4},{7,5},{8,10},{9,11},{10,... | collective-permute-start | bytes 12296 | tf_op jit(solution)/shard_map/ppermute | solution.py:510
  21.9 0.0 collective-permute-done.11.near_halo
  22.0 0.0 collective-permute-done.12.far_halo
  22.0 0.0 collective-permute-done.10.far_half
  22.0 5.8 %shard_map.59 = (f32[4,32,512]{2,1,0:T(8,128)}, f32[8,128]{1,0:T(8,128)S(1)}) custom-call(f32[72,512]{1,0:T(8,128)S(1)} %shard_map.54.own_half, f32[72,512]{1,0:T(8,128)S(1)} %collective-permute-done.10.far_half, f32[72,512]{1,0:T(8,128)S(1)} %collective-permute-done.11.near_halo, f32[72,512]{1,0:T(8,128)S(1)} %collective-permute-done.12.far_halo, ...), custom_call_target="tpu_custom_call" | custom-call | tf_op jit(solution)/shard_map/pallas_call | solution.py:511
  27.8 0.0 collective-permute-done.13.score_two
  27.8 0.6 %shard_map.60 = f32[1,1]{1,0:T(1,128)} custom-call(f32[8,128]{1,0:T(8,128)S(1)} %get-tuple-element.22.score_one, f32[8,128]{1,0:T(8,128)S(1)} %collective-permute-done.13.score_two, f32[8,128]{1,0:T(8,128)S(1)} %get-tuple-element.21._), custom_call_target="tpu_custom_call" | custom-call | tf_op jit(solution)/shard_map/pallas_call | solution.py:518
  (6 shorter events, 0.1 us)
Async XLA Ops:
  0.6 1.0 %copy-start = (f32[1,4,32,512]{3,2,1,0:T(8,128)S(1)}, f32[1,4,32,512]{3,2,1,0:T(8,128)}, u32[]{:S(2)}) copy-start(f32[1,4,32,512]{3,2,1,0:T(8,128)} %param.3) | copy-start | bytes 786436
  1.6 4.7 %copy-start.2 = (f32[1,4,32,512]{3,2,1,0:T(8,128)S(1)}, f32[1,4,32,512]{3,2,1,0:T(8,128)}, u32[]{:S(2)}) copy-start(f32[1,4,32,512]{3,2,1,0:T(8,128)} %param.4) | copy-start | bytes 786436
  1.6 4.6 %collective-permute-start = (f32[72,512]{1,0:T(8,128)S(1)}, f32[72,512]{1,0:T(8,128)S(1)}, u32[]{:S(2)}, u32[]{:S(2)}) collective-permute-start(f32[72,512]{1,0:T(8,128)S(1)} %get-tuple-element.13), channel_id=1, source_target_pairs={{0,4},{4,0},{8,12},{12,8},{16,20},{20,16},{24,28},{28,24},{1,5},{5... | collective-permute-start | bytes 442376 | tf_op jit(solution)/shard_map/ppermute | solution.py:444
  2.1 6.5 %collective-permute-start.2 = (f32[72,512]{1,0:T(8,128)S(1)}, f32[72,512]{1,0:T(8,128)S(1)}, u32[]{:S(2)}, u32[]{:S(2)}) collective-permute-start(f32[72,512]{1,0:T(8,128)S(1)} %get-tuple-element.13), channel_id=1, source_target_pairs={{0,20},{4,8},{8,28},{12,0},{16,4},{20,24},{24,12},{28,16},{1,21},{... | collective-permute-start | bytes 442376 | tf_op jit(solution)/shard_map/ppermute | solution.py:447
  4.8 5.1 %collective-permute-start.1 = (f32[72,512]{1,0:T(8,128)S(1)}, f32[72,512]{1,0:T(8,128)S(1)}, u32[]{:S(2)}, u32[]{:S(2)}) collective-permute-start(f32[72,512]{1,0:T(8,128)S(1)} %get-tuple-element.12.refs_0_), channel_id=1, source_target_pairs={{0,8},{4,20},{8,0},{12,28},{16,24},{20,4},{24,16},{28,12},{1,9},{5... | collective-permute-start | bytes 442376 | tf_op jit(solution)/shard_map/ppermute | solution.py:446
  6.3 1.7 %copy-start.3 = (s32[8]{0:T(128)S(1)}, s32[8]{0:T(128)}, u32[]{:S(2)}) copy-start(s32[8]{0:T(128)} %parents.1) | copy-start | bytes 100
  6.3 5.6 %collective-permute-start.7 = (f32[72,512]{1,0:T(8,128)S(1)}, f32[72,512]{1,0:T(8,128)S(1)}, u32[]{:S(2)}, u32[]{:S(2)}) collective-permute-start(f32[72,512]{1,0:T(8,128)S(1)} %get-tuple-element.18), channel_id=1, source_target_pairs={{0,1},{1,0},{2,3},{3,2},{4,5},{5,4},{6,7},{7,6},{8,9},{9,8},{10,11... | collective-permute-start | bytes 442376 | tf_op jit(solution)/shard_map/ppermute | solution.py:451
  8.0 4.7 %collective-permute-start.8 = (f32[72,512]{1,0:T(8,128)S(1)}, f32[72,512]{1,0:T(8,128)S(1)}, u32[]{:S(2)}, u32[]{:S(2)}) collective-permute-start(f32[72,512]{1,0:T(8,128)S(1)} %get-tuple-element.19), channel_id=1, source_target_pairs={{0,4},{1,2},{2,1},{3,7},{4,0},{5,6},{6,5},{7,3},{8,12},{9,10},{10,... | collective-permute-start | bytes 442376 | tf_op jit(solution)/shard_map/ppermute | solution.py:452
  10.0 2.7 %copy-start.1 = (f32[1,4,32,512]{3,2,1,0:T(8,128)S(1)}, f32[1,4,32,512]{3,2,1,0:T(8,128)}, u32[]{:S(2)}) copy-start(f32[1,4,32,512]{3,2,1,0:T(8,128)} %param.3) | copy-start | bytes 786436
  10.1 6.6 %collective-permute-start.5 = (f32[72,512]{1,0:T(8,128)S(1)}, f32[72,512]{1,0:T(8,128)S(1)}, u32[]{:S(2)}, u32[]{:S(2)}) collective-permute-start(f32[72,512]{1,0:T(8,128)S(1)} %get-tuple-element.16), channel_id=1, source_target_pairs={{0,4},{4,0},{8,12},{12,8},{16,20},{20,16},{24,28},{28,24},{1,5},{5... | collective-permute-start | bytes 442376 | tf_op jit(solution)/shard_map/ppermute | solution.py:489
  10.1 6.6 %collective-permute-start.6 = (f32[72,512]{1,0:T(8,128)S(1)}, f32[72,512]{1,0:T(8,128)S(1)}, u32[]{:S(2)}, u32[]{:S(2)}) collective-permute-start(f32[72,512]{1,0:T(8,128)S(1)} %get-tuple-element.17), channel_id=1, source_target_pairs={{0,20},{4,8},{8,28},{12,0},{16,4},{20,24},{24,12},{28,16},{1,21},{... | collective-permute-start | bytes 442376 | tf_op jit(solution)/shard_map/ppermute | solution.py:492
  11.5 5.6 %collective-permute-start.3 = (f32[72,512]{1,0:T(8,128)S(1)}, f32[72,512]{1,0:T(8,128)S(1)}, u32[]{:S(2)}, u32[]{:S(2)}) collective-permute-start(f32[72,512]{1,0:T(8,128)S(1)} %get-tuple-element.15._), channel_id=1, source_target_pairs={{0,4},{4,0},{8,12},{12,8},{16,20},{20,16},{24,28},{28,24},{1,5},{5... | collective-permute-start | bytes 442376 | tf_op jit(solution)/shard_map/ppermute | solution.py:488
  11.9 5.2 %collective-permute-start.4 = (f32[72,512]{1,0:T(8,128)S(1)}, f32[72,512]{1,0:T(8,128)S(1)}, u32[]{:S(2)}, u32[]{:S(2)}) collective-permute-start(f32[72,512]{1,0:T(8,128)S(1)} %get-tuple-element.14.refs_4_), channel_id=1, source_target_pairs={{0,20},{4,8},{8,28},{12,0},{16,4},{20,24},{24,12},{28,16},{1,21},{... | collective-permute-start | bytes 442376 | tf_op jit(solution)/shard_map/ppermute | solution.py:491
  14.7 4.4 %collective-permute-start.9 = (f32[16,512]{1,0:T(8,128)S(1)}, f32[16,512]{1,0:T(8,128)S(1)}, u32[]{:S(2)}, u32[]{:S(2)}) collective-permute-start(f32[16,512]{1,0:T(8,128)S(1)} %shard_map.57), channel_id=1, source_target_pairs={{0,1},{1,0},{2,3},{3,2},{4,5},{5,4},{6,7},{7,6},{8,9},{9,8},{10,11... | collective-permute-start | bytes 98312 | tf_op jit(solution)/shard_map/ppermute | solution.py:485
  16.7 5.2 %collective-permute-start.11 = (f32[72,512]{1,0:T(8,128)S(1)}, f32[72,512]{1,0:T(8,128)S(1)}, u32[]{:S(2)}, u32[]{:S(2)}) collective-permute-start(f32[72,512]{1,0:T(8,128)S(1)} %shard_map.55.half), channel_id=1, source_target_pairs={{0,5},{1,6},{2,7},{3,11},{4,12},{5,0},{6,1},{7,2},{8,13},{9,14},{1... | collective-permute-start | bytes 442376 | tf_op jit(solution)/shard_map/ppermute | solution.py:502
  17.1 4.8 %collective-permute-start.12 = (f32[72,512]{1,0:T(8,128)S(1)}, f32[72,512]{1,0:T(8,128)S(1)}, u32[]{:S(2)}, u32[]{:S(2)}) collective-permute-start(f32[72,512]{1,0:T(8,128)S(1)} %shard_map.54.own_half), channel_id=1, source_target_pairs={{0,1},{1,2},{2,3},{3,7},{4,0},{5,4},{6,5},{7,6},{8,9},{9,10},{10,1... | collective-permute-start | bytes 442376 | tf_op jit(solution)/shard_map/ppermute | solution.py:503
  19.1 2.8 %collective-permute-start.10 = (f32[72,512]{1,0:T(8,128)S(1)}, f32[72,512]{1,0:T(8,128)S(1)}, u32[]{:S(2)}, u32[]{:S(2)}) collective-permute-start(f32[72,512]{1,0:T(8,128)S(1)} %shard_map.58), channel_id=1, source_target_pairs={{0,4},{4,0},{8,12},{12,8},{16,20},{20,16},{24,28},{28,24},{1,5},{5... | collective-permute-start | bytes 442376 | tf_op jit(solution)/shard_map/ppermute | solution.py:505
  19.2 8.6 %collective-permute-start.13 = (f32[8,128]{1,0:T(8,128)S(1)}, f32[8,128]{1,0:T(8,128)S(1)}, u32[]{:S(2)}, u32[]{:S(2)}) collective-permute-start(f32[8,128]{1,0:T(8,128)S(1)} %get-tuple-element.22.score_one), channel_id=1, source_target_pairs={{0,2},{1,3},{2,0},{3,1},{4,6},{5,7},{6,4},{7,5},{8,10},{9,11},{10,... | collective-permute-start | bytes 12296 | tf_op jit(solution)/shard_map/ppermute | solution.py:510

commit v9 on v8

--- a/solution.py
+++ b/solution.py
@@ -102,6 +102,8 @@
         reach -= 1
         first, count = origin - reach, rows + 2 * reach
         fields = range(4) if number < 3 * STEPS - 1 else last_fields
+        if number == 3 * STEPS - 2 and last_fields == (3,):
+            fields = (1, 2, 3)
         stage(src, state, dst, first, count, keep, gain, scales, (turn_first, slope), walls, fields)
 
 
@@ -499,8 +501,8 @@
         )(routes, *sources)
         for which, sources in enumerate((own, other))
     ]
+    far_halo = lax.ppermute(own_half, both, to_same)
     near_halo = lax.ppermute(sibling_half, both, to_other)
-    far_halo = lax.ppermute(own_half, both, to_same)
     (held_back,) = call(late_kernel, (half_shape,), [VMEM] * 2, (VMEM,))(sibling_half, scores[1])
     far_half = lax.ppermute(held_back, "member", sibling)
     while bit * 2 < domains and domains & (domains - 1) == 0:

time: 28.8 us -> 28.8 us (level)
  no operation moved by 1% of the time
where the time goes in v9:
time: 28.8 us; the launch traced here: 28.3 us
  starting transfers between devices  15.9 us (55%)
  Pallas kernels  9.26 us (32%)
  waiting for transfers between devices  1.41 us (5%)
  local copies, waits for them, and re-layouts  0.96 us (3%)
  between operations  0.75 us (3%)
    pallas_call x1, Pallas kernels, on_device(): call(functools.partial(final_kernel, sizes, domains), (jax.ShapeDtypeStru...  5.8 us
    ppermute x1, starting transfers between devices, on_device(): scores = [score, lax.ppermute(score, 'domain', pairs)]  2.76 us
    ppermute x1, starting transfers between devices, on_device(): held.append(lax.ppermute(other, 'member', other_core(k)))  2.63 us
    ppermute x1, starting transfers between devices, on_device(): lax.ppermute(score, 'domain', [(z, z ^ 1) for z in range(domains)])  2 us
    pallas_call x1, Pallas kernels, on_device(): call(functools.partial(score_kernel, sizes, domains), wide_shape, [VMEM]...  1.96 us
    ppermute x1, starting transfers between devices, on_device(): far_halo = lax.ppermute(own_half, both, to_same)  1.93 us
    ppermute x1, starting transfers between devices, on_device(): edge_one = lax.ppermute(edge_one, both, pair_one)  1.64 us
    ppermute x1, starting transfers between devices, on_device(): held.append(lax.ppermute(mine, 'member', same_core(True, k)))  1.49 us
  transfers between devices with their start and end apart: 14, of which 2 were waited for; matrix products, arithmetic and copies ran while one was open for 0% of the time, Pallas kernels for 31%

profile of v9, /device:TPU:0, one launch (start us, length us, event | category | flops | bytes accessed | tf_op | source)
XLA Modules:
  0.0 28.3 jit_solution(16726514983152959673)
XLA Ops:
  0.6 0.0 copy-start
  0.6 0.9 %copy-done = f32[1,4,32,512]{3,2,1,0:T(8,128)S(1)} copy-done((f32[1,4,32,512]{3,2,1,0:T(8,128)S(1)}, f32[1,4,32,512]{3,2,1,0:T(8,128)}, u32[]{:S(2)}) %copy-start) | copy-done | bytes 262168
  1.6 0.0 copy-start.2
  1.6 0.5 %collective-permute-start = (f32[72,512]{1,0:T(8,128)S(1)}, f32[72,512]{1,0:T(8,128)S(1)}, u32[]{:S(2)}, u32[]{:S(2)}) collective-permute-start(f32[72,512]{1,0:T(8,128)S(1)} %get-tuple-element.13), channel_id=1, source_target_pairs={{0,4},{4,0},{8,12},{12,8},{16,20},{20,16},{24,28},{28,24},{1,5},{5... | collective-permute-start | bytes 442376 | tf_op jit(solution)/shard_map/ppermute | solution.py:446
  2.1 2.6 %collective-permute-start.2 = (f32[72,512]{1,0:T(8,128)S(1)}, f32[72,512]{1,0:T(8,128)S(1)}, u32[]{:S(2)}, u32[]{:S(2)}) collective-permute-start(f32[72,512]{1,0:T(8,128)S(1)} %get-tuple-element.13), channel_id=1, source_target_pairs={{0,20},{4,8},{8,28},{12,0},{16,4},{20,24},{24,12},{28,16},{1,21},{... | collective-permute-start | bytes 442376 | tf_op jit(solution)/shard_map/ppermute | solution.py:449
  4.8 1.5 %collective-permute-start.1 = (f32[72,512]{1,0:T(8,128)S(1)}, f32[72,512]{1,0:T(8,128)S(1)}, u32[]{:S(2)}, u32[]{:S(2)}) collective-permute-start(f32[72,512]{1,0:T(8,128)S(1)} %get-tuple-element.12.refs_0_), channel_id=1, source_target_pairs={{0,8},{4,20},{8,0},{12,28},{16,24},{20,4},{24,16},{28,12},{1,9},{5... | collective-permute-start | bytes 442376 | tf_op jit(solution)/shard_map/ppermute | solution.py:448
  6.3 0.0 collective-permute-done.refs_1_._
  6.3 0.0 copy-done.2
  6.3 0.0 copy-start.3
  6.3 1.6 %collective-permute-start.7 = (f32[72,512]{1,0:T(8,128)S(1)}, f32[72,512]{1,0:T(8,128)S(1)}, u32[]{:S(2)}, u32[]{:S(2)}) collective-permute-start(f32[72,512]{1,0:T(8,128)S(1)} %get-tuple-element.18), channel_id=1, source_target_pairs={{0,1},{1,0},{2,3},{3,2},{4,5},{5,4},{6,7},{7,6},{8,9},{9,8},{10,11... | collective-permute-start | bytes 442376 | tf_op jit(solution)/shard_map/ppermute | solution.py:453
  8.0 0.0 collective-permute-start.8
  8.0 0.0 copy-done.3
  8.0 0.7 %shard_map.50.routes = s32[48,128]{1,0:T(8,128)S(1)} custom-call(s32[8]{0:T(128)S(1)} %copy-done.3), custom_call_target="tpu_custom_call" | custom-call | tf_op jit(solution)/shard_map/pallas_call | solution.py:455
  8.6 0.0 collective-permute-done.2.refs_3_
  8.6 1.3 %collective-permute-done.1.refs_2_ = f32[72,512]{1,0:T(8,128)S(1)} collective-permute-done((f32[72,512]{1,0:T(8,128)S(1)}, f32[72,512]{1,0:T(8,128)S(1)}, u32[]{:S(2)}, u32[]{:S(2)}) %collective-permute-start.1) | collective-permute-done | bytes 147488 | tf_op jit(solution)/shard_map/ppermute | solution.py:448
  9.9 0.1 shard_map.52
  10.0 0.0 copy-start.1
  10.0 0.1 shard_map.53
  10.1 0.1 collective-permute-start.5
  10.1 1.4 %collective-permute-start.6 = (f32[72,512]{1,0:T(8,128)S(1)}, f32[72,512]{1,0:T(8,128)S(1)}, u32[]{:S(2)}, u32[]{:S(2)}) collective-permute-start(f32[72,512]{1,0:T(8,128)S(1)} %get-tuple-element.17), channel_id=1, source_target_pairs={{0,20},{4,8},{8,28},{12,0},{16,4},{20,24},{24,12},{28,16},{1,21},{... | collective-permute-start | bytes 442376 | tf_op jit(solution)/shard_map/ppermute | solution.py:494
  11.5 0.3 %collective-permute-start.3 = (f32[72,512]{1,0:T(8,128)S(1)}, f32[72,512]{1,0:T(8,128)S(1)}, u32[]{:S(2)}, u32[]{:S(2)}) collective-permute-start(f32[72,512]{1,0:T(8,128)S(1)} %get-tuple-element.15._), channel_id=1, source_target_pairs={{0,4},{4,0},{8,12},{12,8},{16,20},{20,16},{24,28},{28,24},{1,5},{5... | collective-permute-start | bytes 442376 | tf_op jit(solution)/shard_map/ppermute | solution.py:490
  11.8 0.1 collective-permute-done.7.edge_one
  11.9 0.8 %collective-permute-start.4 = (f32[72,512]{1,0:T(8,128)S(1)}, f32[72,512]{1,0:T(8,128)S(1)}, u32[]{:S(2)}, u32[]{:S(2)}) collective-permute-start(f32[72,512]{1,0:T(8,128)S(1)} %get-tuple-element.14.refs_4_), channel_id=1, source_target_pairs={{0,20},{4,8},{8,28},{12,0},{16,4},{20,24},{24,12},{28,16},{1,21},{... | collective-permute-start | bytes 442376 | tf_op jit(solution)/shard_map/ppermute | solution.py:493
  12.7 0.0 collective-permute-done.8.edge_two
  12.7 0.0 copy-done.1
  12.7 2.0 %shard_map.57 = f32[16,512]{1,0:T(8,128)S(1)} custom-call(f32[4,32,512]{2,1,0:T(8,128)S(1)} %bitcast.6, f32[72,512]{1,0:T(8,128)S(1)} %collective-permute-done.7.edge_one, f32[72,512]{1,0:T(8,128)S(1)} %collective-permute-done.8.edge_two, f32[72,512]{1,0:T(8,128)S(1)} %get-tuple-element.15._), custom_call_target="tpu_custom_call" | custom-call | tf_op jit(solution)/shard_map/pallas_call | solution.py:475
  14.7 2.0 %collective-permute-start.9 = (f32[16,512]{1,0:T(8,128)S(1)}, f32[16,512]{1,0:T(8,128)S(1)}, u32[]{:S(2)}, u32[]{:S(2)}) collective-permute-start(f32[16,512]{1,0:T(8,128)S(1)} %shard_map.57), channel_id=1, source_target_pairs={{0,1},{1,0},{2,3},{3,2},{4,5},{5,4},{6,7},{7,6},{8,9},{9,8},{10,11... | collective-permute-start | bytes 98312 | tf_op jit(solution)/shard_map/ppermute | solution.py:487
  16.7 0.0 collective-permute-done.5.refs_0_
  16.7 0.0 collective-permute-done.6.refs_1_
  16.7 0.4 %collective-permute-start.11 = (f32[72,512]{1,0:T(8,128)S(1)}, f32[72,512]{1,0:T(8,128)S(1)}, u32[]{:S(2)}, u32[]{:S(2)}) collective-permute-start(f32[72,512]{1,0:T(8,128)S(1)} %shard_map.55.half), channel_id=1, source_target_pairs={{0,5},{1,6},{2,7},{3,11},{4,12},{5,0},{6,1},{7,2},{8,13},{9,14},{1... | collective-permute-start | bytes 442376 | tf_op jit(solution)/shard_map/ppermute | solution.py:505
  17.1 0.0 collective-permute-done.3.refs_0_
  17.1 0.0 collective-permute-done.4.refs_1_
  17.1 1.9 %collective-permute-start.12 = (f32[72,512]{1,0:T(8,128)S(1)}, f32[72,512]{1,0:T(8,128)S(1)}, u32[]{:S(2)}, u32[]{:S(2)}) collective-permute-start(f32[72,512]{1,0:T(8,128)S(1)} %shard_map.54.own_half), channel_id=1, source_target_pairs={{0,1},{1,2},{2,3},{3,7},{4,0},{5,4},{6,5},{7,6},{8,9},{9,10},{10,1... | collective-permute-start | bytes 442376 | tf_op jit(solution)/shard_map/ppermute | solution.py:504
  19.1 0.0 collective-permute-done.9
  19.1 0.1 collective-permute-start.10
  19.2 2.8 %collective-permute-start.13 = (f32[8,128]{1,0:T(8,128)S(1)}, f32[8,128]{1,0:T(8,128)S(1)}, u32[]{:S(2)}, u32[]{:S(2)}) collective-permute-start(f32[8,128]{1,0:T(8,128)S(1)} %get-tuple-element.22.score_one), channel_id=1, source_target_pairs={{0,2},{1,3},{2,0},{3,1},{4,6},{5,7},{6,4},{7,5},{8,10},{9,11},{10,... | collective-permute-start | bytes 12296 | tf_op jit(solution)/shard_map/ppermute | solution.py:512
  21.9 0.0 collective-permute-done.11.near_halo
  21.9 0.0 collective-permute-done.12.far_halo
  21.9 0.0 collective-permute-done.10.far_half
  21.9 5.8 %shard_map.59 = (f32[4,32,512]{2,1,0:T(8,128)}, f32[8,128]{1,0:T(8,128)S(1)}) custom-call(f32[72,512]{1,0:T(8,128)S(1)} %shard_map.54.own_half, f32[72,512]{1,0:T(8,128)S(1)} %collective-permute-done.10.far_half, f32[72,512]{1,0:T(8,128)S(1)} %collective-permute-done.11.near_halo, f32[72,512]{1,0:T(8,128)S(1)} %collective-permute-done.12.far_halo, ...), custom_call_target="tpu_custom_call" | custom-call | tf_op jit(solution)/shard_map/pallas_call | solution.py:513
  27.7 0.0 collective-permute-done.13.score_two
  27.7 0.6 %shard_map.60 = f32[1,1]{1,0:T(1,128)} custom-call(f32[8,128]{1,0:T(8,128)S(1)} %get-tuple-element.22.score_one, f32[8,128]{1,0:T(8,128)S(1)} %collective-permute-done.13.score_two, f32[8,128]{1,0:T(8,128)S(1)} %get-tuple-element.21._), custom_call_target="tpu_custom_call" | custom-call | tf_op jit(solution)/shard_map/pallas_call | solution.py:520
  (6 shorter events, 0.1 us)
Async XLA Ops:
  0.6 1.0 %copy-start = (f32[1,4,32,512]{3,2,1,0:T(8,128)S(1)}, f32[1,4,32,512]{3,2,1,0:T(8,128)}, u32[]{:S(2)}) copy-start(f32[1,4,32,512]{3,2,1,0:T(8,128)} %param.3) | copy-start | bytes 786436
  1.6 4.7 %copy-start.2 = (f32[1,4,32,512]{3,2,1,0:T(8,128)S(1)}, f32[1,4,32,512]{3,2,1,0:T(8,128)}, u32[]{:S(2)}) copy-start(f32[1,4,32,512]{3,2,1,0:T(8,128)} %param.4) | copy-start | bytes 786436
  1.6 4.6 %collective-permute-start = (f32[72,512]{1,0:T(8,128)S(1)}, f32[72,512]{1,0:T(8,128)S(1)}, u32[]{:S(2)}, u32[]{:S(2)}) collective-permute-start(f32[72,512]{1,0:T(8,128)S(1)} %get-tuple-element.13), channel_id=1, source_target_pairs={{0,4},{4,0},{8,12},{12,8},{16,20},{20,16},{24,28},{28,24},{1,5},{5... | collective-permute-start | bytes 442376 | tf_op jit(solution)/shard_map/ppermute | solution.py:446
  2.1 6.5 %collective-permute-start.2 = (f32[72,512]{1,0:T(8,128)S(1)}, f32[72,512]{1,0:T(8,128)S(1)}, u32[]{:S(2)}, u32[]{:S(2)}) collective-permute-start(f32[72,512]{1,0:T(8,128)S(1)} %get-tuple-element.13), channel_id=1, source_target_pairs={{0,20},{4,8},{8,28},{12,0},{16,4},{20,24},{24,12},{28,16},{1,21},{... | collective-permute-start | bytes 442376 | tf_op jit(solution)/shard_map/ppermute | solution.py:449
  4.8 5.1 %collective-permute-start.1 = (f32[72,512]{1,0:T(8,128)S(1)}, f32[72,512]{1,0:T(8,128)S(1)}, u32[]{:S(2)}, u32[]{:S(2)}) collective-permute-start(f32[72,512]{1,0:T(8,128)S(1)} %get-tuple-element.12.refs_0_), channel_id=1, source_target_pairs={{0,8},{4,20},{8,0},{12,28},{16,24},{20,4},{24,16},{28,12},{1,9},{5... | collective-permute-start | bytes 442376 | tf_op jit(solution)/shard_map/ppermute | solution.py:448
  6.3 1.7 %copy-start.3 = (s32[8]{0:T(128)S(1)}, s32[8]{0:T(128)}, u32[]{:S(2)}) copy-start(s32[8]{0:T(128)} %parents.1) | copy-start | bytes 100
  6.3 5.6 %collective-permute-start.7 = (f32[72,512]{1,0:T(8,128)S(1)}, f32[72,512]{1,0:T(8,128)S(1)}, u32[]{:S(2)}, u32[]{:S(2)}) collective-permute-start(f32[72,512]{1,0:T(8,128)S(1)} %get-tuple-element.18), channel_id=1, source_target_pairs={{0,1},{1,0},{2,3},{3,2},{4,5},{5,4},{6,7},{7,6},{8,9},{9,8},{10,11... | collective-permute-start | bytes 442376 | tf_op jit(solution)/shard_map/ppermute | solution.py:453
  8.0 4.7 %collective-permute-start.8 = (f32[72,512]{1,0:T(8,128)S(1)}, f32[72,512]{1,0:T(8,128)S(1)}, u32[]{:S(2)}, u32[]{:S(2)}) collective-permute-start(f32[72,512]{1,0:T(8,128)S(1)} %get-tuple-element.19), channel_id=1, source_target_pairs={{0,4},{1,2},{2,1},{3,7},{4,0},{5,6},{6,5},{7,3},{8,12},{9,10},{10,... | collective-permute-start | bytes 442376 | tf_op jit(solution)/shard_map/ppermute | solution.py:454
  10.0 2.7 %copy-start.1 = (f32[1,4,32,512]{3,2,1,0:T(8,128)S(1)}, f32[1,4,32,512]{3,2,1,0:T(8,128)}, u32[]{:S(2)}) copy-start(f32[1,4,32,512]{3,2,1,0:T(8,128)} %param.3) | copy-start | bytes 786436
  10.1 6.6 %collective-permute-start.5 = (f32[72,512]{1,0:T(8,128)S(1)}, f32[72,512]{1,0:T(8,128)S(1)}, u32[]{:S(2)}, u32[]{:S(2)}) collective-permute-start(f32[72,512]{1,0:T(8,128)S(1)} %get-tuple-element.16), channel_id=1, source_target_pairs={{0,4},{4,0},{8,12},{12,8},{16,20},{20,16},{24,28},{28,24},{1,5},{5... | collective-permute-start | bytes 442376 | tf_op jit(solution)/shard_map/ppermute | solution.py:491
  10.1 6.5 %collective-permute-start.6 = (f32[72,512]{1,0:T(8,128)S(1)}, f32[72,512]{1,0:T(8,128)S(1)}, u32[]{:S(2)}, u32[]{:S(2)}) collective-permute-start(f32[72,512]{1,0:T(8,128)S(1)} %get-tuple-element.17), channel_id=1, source_target_pairs={{0,20},{4,8},{8,28},{12,0},{16,4},{20,24},{24,12},{28,16},{1,21},{... | collective-permute-start | bytes 442376 | tf_op jit(solution)/shard_map/ppermute | solution.py:494
  11.5 5.6 %collective-permute-start.3 = (f32[72,512]{1,0:T(8,128)S(1)}, f32[72,512]{1,0:T(8,128)S(1)}, u32[]{:S(2)}, u32[]{:S(2)}) collective-permute-start(f32[72,512]{1,0:T(8,128)S(1)} %get-tuple-element.15._), channel_id=1, source_target_pairs={{0,4},{4,0},{8,12},{12,8},{16,20},{20,16},{24,28},{28,24},{1,5},{5... | collective-permute-start | bytes 442376 | tf_op jit(solution)/shard_map/ppermute | solution.py:490
  11.9 5.2 %collective-permute-start.4 = (f32[72,512]{1,0:T(8,128)S(1)}, f32[72,512]{1,0:T(8,128)S(1)}, u32[]{:S(2)}, u32[]{:S(2)}) collective-permute-start(f32[72,512]{1,0:T(8,128)S(1)} %get-tuple-element.14.refs_4_), channel_id=1, source_target_pairs={{0,20},{4,8},{8,28},{12,0},{16,4},{20,24},{24,12},{28,16},{1,21},{... | collective-permute-start | bytes 442376 | tf_op jit(solution)/shard_map/ppermute | solution.py:493
  14.7 4.4 %collective-permute-start.9 = (f32[16,512]{1,0:T(8,128)S(1)}, f32[16,512]{1,0:T(8,128)S(1)}, u32[]{:S(2)}, u32[]{:S(2)}) collective-permute-start(f32[16,512]{1,0:T(8,128)S(1)} %shard_map.57), channel_id=1, source_target_pairs={{0,1},{1,0},{2,3},{3,2},{4,5},{5,4},{6,7},{7,6},{8,9},{9,8},{10,11... | collective-permute-start | bytes 98312 | tf_op jit(solution)/shard_map/ppermute | solution.py:487
  16.7 5.2 %collective-permute-start.11 = (f32[72,512]{1,0:T(8,128)S(1)}, f32[72,512]{1,0:T(8,128)S(1)}, u32[]{:S(2)}, u32[]{:S(2)}) collective-permute-start(f32[72,512]{1,0:T(8,128)S(1)} %shard_map.55.half), channel_id=1, source_target_pairs={{0,5},{1,6},{2,7},{3,11},{4,12},{5,0},{6,1},{7,2},{8,13},{9,14},{1... | collective-permute-start | bytes 442376 | tf_op jit(solution)/shard_map/ppermute | solution.py:505
  17.1 4.8 %collective-permute-start.12 = (f32[72,512]{1,0:T(8,128)S(1)}, f32[72,512]{1,0:T(8,128)S(1)}, u32[]{:S(2)}, u32[]{:S(2)}) collective-permute-start(f32[72,512]{1,0:T(8,128)S(1)} %shard_map.54.own_half), channel_id=1, source_target_pairs={{0,1},{1,2},{2,3},{3,7},{4,0},{5,4},{6,5},{7,6},{8,9},{9,10},{10,1... | collective-permute-start | bytes 442376 | tf_op jit(solution)/shard_map/ppermute | solution.py:504
  19.1 2.8 %collective-permute-start.10 = (f32[72,512]{1,0:T(8,128)S(1)}, f32[72,512]{1,0:T(8,128)S(1)}, u32[]{:S(2)}, u32[]{:S(2)}) collective-permute-start(f32[72,512]{1,0:T(8,128)S(1)} %shard_map.58), channel_id=1, source_target_pairs={{0,4},{4,0},{8,12},{12,8},{16,20},{20,16},{24,28},{28,24},{1,5},{5... | collective-permute-start | bytes 442376 | tf_op jit(solution)/shard_map/ppermute | solution.py:507
  19.2 8.6 %collective-permute-start.13 = (f32[8,128]{1,0:T(8,128)S(1)}, f32[8,128]{1,0:T(8,128)S(1)}, u32[]{:S(2)}, u32[]{:S(2)}) collective-permute-start(f32[8,128]{1,0:T(8,128)S(1)} %get-tuple-element.22.score_one), channel_id=1, source_target_pairs={{0,2},{1,3},{2,0},{3,1},{4,6},{5,7},{6,4},{7,5},{8,10},{9,11},{10,... | collective-permute-start | bytes 12296 | tf_op jit(solution)/shard_map/ppermute | solution.py:512
